TPU v7x, 32 devices: a whole 2x2x4 slice. The times are simulated.
32 devices in a mesh: members: 2 (over x), space: 16 (over z, y, core).
Axes of the slice: x: 2, y: 2, z: 4, core: 2. Of those that a mesh axis runs over, the one named last changes fastest.
Arguments:
- spectra: float32 [16384, 1296], P(('members', 'space')), parts along dimension 0, may hold values from 0.05 to 5
- wind_files: float32 [32, 2, 1024], P(('members', 'space')), parts along dimension 0, may hold values from -25 to 25
- current_files: float32 [32, 2, 1024], P(('members', 'space')), parts along dimension 0, may hold values from -1 to 1
- reader_turn: int32 [2], replicated, may hold values from 0 to 15
- cell_point: int32 [8192], P('space'), may hold values from 0 to 1023, as said below
- coupling: bfloat16 [1296, 1296], replicated, may hold values from -0.078125 to 0.078125
- send_list: int32 [16, 16, 64], P('space'), may hold values from 0 to 511, as said below
- send_count: int32 [16, 16], P('space'), may hold values from 0 to 64, as said below
- recv_list: int32 [16, 16, 64], P('space'), may hold values from 0 to 1023, as said below
- wet_mask: int32 [128, 128], P('space'), may hold values from 0 to 1, as said below
Outputs:
- new_spectra: float32 [16384, 1296], P(('members', 'space')), parts along dimension 0
There are 2 independent parts, one for each index of `members`. A program takes and returns all parts, laid end to end along the dimension named above; an argument that names none is the same for every part. Nothing has to cross between parts.
Inputs may be any that keep to these rules, and one draw needn't show every extreme that they name: `send_count`: every entry is at most 64, and 64 is reached in every draw; each row sums to 512; column b sums to the number of wet cells of strip b. `send_list`: the live entries of row s name every local row of share s exactly once; entries past the count are 0. `recv_list`: the live entries for strip b name every wet cell of strip b exactly once (row-major within the strip's 8 x 128 cells), matched slot by slot to send_list; entries past the count are 0. `wet_mask`: equals 1 exactly on the cells that recv_list names. `cell_point`: the forcing point of the grid cell to which the row is sent.
All inputs are finite; a program needn't handle non-finite values.
Results may differ from a plain program's by a relative error of at most 0.0016.
Values sent between devices are 32-bit elements; how exact they have to be, the bound alone decides.
No kernel may reach another device: no remote copies, remote signals or barrier semaphores. Data moves between devices by JAX's collectives and lax.ppermute only.
A program may use at most 64 MiB of HBM per device.

v0:
```python
import math

import jax
import jax.numpy as jnp
from jax import lax
from jax.sharding import PartitionSpec as P

DIRS = 36
FREQS = 36
COARSE = 4


gravity = 9.81
base_freq = 0.0418
freq_ratio = 1.1
freq_span = 35.0
input_coef = 0.0001
wind_gain = 1.12
dissip_coef = 0.0005
half_length = 300.0
courant_scale = 0.05


def from_root(array, axis, root):
    mine = lax.axis_index(axis) == root
    return lax.psum(jnp.where(mine, array, jnp.zeros_like(array)), axis)


def extended(array, sides, width):
    for axis, dim in sides:
        size, length = (lax.axis_size(axis), array.shape[dim])
        up = [(i, (i + 1) % size) for i in range(size - 1)]
        down = [(j, i) for i, j in up]
        last = lax.slice_in_dim(array, length - width, length, axis=dim)
        first = lax.slice_in_dim(array, 0, width, axis=dim)
        before = lax.ppermute(last, axis, up)
        after = lax.ppermute(first, axis, down)
        array = jnp.concatenate([before, array, after], axis=dim)
    return array


def spectral_tables():
    direction = 2.0 * math.pi / DIRS * jnp.arange(DIRS, dtype=jnp.float32)
    exponent = jnp.arange(FREQS, dtype=jnp.float32) * (freq_span / (FREQS - 1))
    frequency = base_freq * freq_ratio**exponent
    angular = 2.0 * math.pi * frequency
    phase_speed = gravity / angular
    return (jnp.cos(direction), jnp.sin(direction), angular, phase_speed, 0.5 * phase_speed)


def source_half(energy, wind_east, wind_north, coupling):
    cos_dir, sine_dir, angular, phase_speed, group_speed = spectral_tables()
    along_wind = wind_east[:, None] * cos_dir[None, :] + wind_north[:, None] * sine_dir[None, :]
    growth = (
        input_coef
        * angular[None, None, :]
        * jnp.maximum(wind_gain * along_wind[:, :, None] / phase_speed[None, None, :] - 1.0, 0.0)
    )
    growth = growth.reshape(energy.shape[0], -1)
    mean_square = jnp.mean(energy * energy, axis=1, keepdims=True)
    decay_rate = dissip_coef * jnp.tile(angular, DIRS)[None, :] * mean_square
    local_part = energy * (1.0 + half_length * growth) / (1.0 + half_length * decay_rate)
    return local_part + jnp.dot(
        local_part.astype(jnp.bfloat16), coupling, preferred_element_type=jnp.float32
    )


def advect(center, upwind_lo, upwind_hi, courant):
    ahead_part = jnp.maximum(courant, 0.0)
    behind = jnp.minimum(courant, 0.0)
    return center - ahead_part * (center - upwind_lo) - behind * (upwind_hi - center)


def sweep_cols(energy_grid, drift_east, wet_field):
    cos_dir, sine_dir, angular, phase_speed, group_speed = spectral_tables()
    wave_speed = (cos_dir[:, None] * group_speed[None, :]).reshape(-1)
    courant = (wave_speed[None, None, :] + drift_east[:, :, None]) * courant_scale
    zero_edge = jnp.zeros_like(energy_grid[:, :1])
    upwind_lo = jnp.concatenate([zero_edge, energy_grid[:, :-1]], axis=1)
    upwind_hi = jnp.concatenate([energy_grid[:, 1:], zero_edge], axis=1)
    return advect(energy_grid, upwind_lo, upwind_hi, courant) * wet_field[:, :, None]


def sweep_rows(energy_grid, row_above, row_below, drift_north, wet_field):
    cos_dir, sine_dir, angular, phase_speed, group_speed = spectral_tables()
    wave_speed = (sine_dir[:, None] * group_speed[None, :]).reshape(-1)
    courant = (wave_speed[None, None, :] + drift_north[:, :, None]) * courant_scale
    return advect(energy_grid, row_above, row_below, courant) * wet_field[:, :, None]


def forcing_points(row_start, row_count, col_count):
    rows_idx = row_start + jnp.arange(row_count, dtype=jnp.int32)
    cols_idx = jnp.arange(col_count, dtype=jnp.int32)
    return rows_idx[:, None] // COARSE * (col_count // COARSE) + cols_idx[None, :] // COARSE


def on_device(
    spectra,
    wind_files,
    current_files,
    reader_turn,
    cell_point,
    coupling,
    send_list,
    send_count,
    recv_list,
    wet_mask,
):
    levels = []
    for time_level in range(2):
        levels.append(
            (
                from_root(wind_files[0], "space", reader_turn[time_level]),
                from_root(current_files[0], "space", reader_turn[time_level]),
            )
        )
    wind_mean = 0.5 * (levels[0][0] + levels[1][0])
    current_mean = 0.5 * (levels[0][1] + levels[1][1])
    cell_wind = jnp.take(wind_mean, cell_point, axis=1)
    first_half = source_half(spectra, cell_wind[0], cell_wind[1], coupling)
    send_rows = send_list[0]
    counts = send_count[0]
    places = recv_list[0]
    slot_count = send_rows.shape[1]
    spec_width = spectra.shape[1]
    live_slots = (jnp.arange(slot_count, dtype=jnp.int32)[None, :] < counts[:, None]).astype(
        jnp.float32
    )
    packed = first_half[send_rows] * live_slots[:, :, None]
    arrived = lax.all_to_all(packed, "space", split_axis=0, concat_axis=0, tiled=True)
    row_count = wet_mask.shape[0]
    col_count = wet_mask.shape[1]
    energy_grid = (
        jnp.zeros((row_count * col_count, spec_width), jnp.float32)
        .at[places.reshape(-1)]
        .add(arrived.reshape(-1, spec_width))
    )
    energy_grid = energy_grid.reshape(row_count, col_count, spec_width)
    points = forcing_points(lax.axis_index("space") * row_count, row_count, col_count)
    drift = jnp.take(current_mean, points, axis=1)
    wet_field = wet_mask.astype(jnp.float32)
    swept_cols = sweep_cols(energy_grid, drift[0], wet_field)
    padded = extended(swept_cols, (("space", 0),), 1)
    swept = sweep_rows(swept_cols, padded[:-2], padded[2:], drift[1], wet_field).reshape(
        -1, spec_width
    )
    outgoing = swept[places]
    flat_rows = send_rows.reshape(-1)
    empty_rows = jnp.zeros((spectra.shape[0], spec_width), jnp.float32)
    returned = lax.all_to_all(outgoing, "space", split_axis=0, concat_axis=0, tiled=True)
    back_rows = empty_rows.at[flat_rows].add(
        (returned * live_slots[:, :, None]).reshape(-1, spec_width)
    )
    result = source_half(back_rows, cell_wind[0], cell_wind[1], coupling)
    return result


def solution(mesh):
    placed = (
        P(("members", "space"), None),
        P(("members", "space"), None, None),
        P(("members", "space"), None, None),
        P(),
        P("space"),
        P(),
        P("space", None, None),
        P("space", None),
        P("space", None, None),
        P("space", None),
    )
    return jax.shard_map(
        on_device,
        mesh=mesh,
        in_specs=placed,
        out_specs=P(("members", "space"), None),
        check_vma=False,
    )
```

profile of v0, /device:TPU:15, one launch (start us, length us, event | category | flops | bytes accessed | tf_op | source)
XLA Modules:
  0.0 471.9 jit_solution(9839202872670301571)
XLA Ops:
  0.1 0.7 compare_and_fusion
  0.8 0.7 compare_select_fusion.6
  1.5 1.4 fusion.38
  4.2 2.0 multiply_reduce_fusion.1
  6.2 0.7 fusion.21
  7.0 0.7 compare_select_fusion.3
  7.7 0.1 reshape.481
  7.7 0.7 add_bitcast_fusion
  8.5 44.6 %all-reduce.2 = (f32[2,1024]{1,0:T(2,128)S(1)}, f32[2,1024]{1,0:T(2,128)S(1)}) all-reduce(f32[2,1024]{1,0:T(2,128)S(1)} %get-tuple-element.20, f32[2,1024]{1,0:T(2,128)S(1)} %get-tuple-element.19), channel_id=1, replica_groups=mesh['members'=2,'space'=16] {'space'}, use_global_device_ids=true, to_apply=%region_0.1 | all-reduce | flops 4096 | bytes 32768 | tf_op jit(solution)/shard_map/psum | solution.py:26
  53.1 0.1 div.83
  53.2 0.1 mul.346
  53.4 0.1 mul.326
  53.5 0.2 copy.64
  53.7 1.0 gather_fusion
  54.7 0.1 select_bitcast_fusion
  54.9 0.3 slice_reduce_fusion.1
  55.2 0.1 add_multiply_fusion
  55.3 0.4 div.79
  55.6 1.8 div.80
  57.4 10.7 %convolution_add_fusion.1 = f32[512,1296]{0,1:T(8,128)} fusion(bf16[1296,1296]{1,0:T(8,128)(2,1)} %param.15, f32[512,1296]{0,1:T(8,128)} %param.10, f32[512]{0:T(512)S(1)} %broadcast_multiply_fusion.7, f32[1296]{0:T(1024)S(1)} %mul.346, f32[512,1296]{0,1:T(8,128)} %div.80, f32[1296]{0:T(1024)S(1)} %div.83, f32[1296]{0:T(1024)S(1)} %mul.326), kind=kOutput, calls=%fused_computation.17 | convolution fusion | flops 1735852032 | bytes 11339456 | tf_op jit(solution)/shard_map/dot_general | solution.py:63
  68.1 2.2 copy.65
  70.3 5.9 %gather_fusion.1 = f32[1024,1296]{1,0:T(8,128)} fusion(f32[512,1296]{1,0:T(8,128)S(1)} %copy.65, s32[1024]{0:T(1024)S(1)} %broadcast_clamp_fusion), kind=kCustom, calls=%fused_computation.1 | custom fusion | bytes 10620928 | tf_op jit(solution)/shard_map/gather | solution.py:129
  76.2 5.6 %broadcast_multiply_fusion.1 = f32[16,64,1296]{2,1,0:T(8,128)} fusion(f32[16,64,1296]{2,1,0:T(8,128)} %bitcast.43, f32[16,64]{1,0:T(8,128)S(1)} %fusion.21), kind=kLoop, calls=%fused_computation.20 | loop fusion | flops 1327104 | bytes 10620928 | tf_op jit(solution)/shard_map/mul | solution.py:129
  81.8 0.0 copy-start.4
  81.8 0.0 copy-start.2
  81.8 22.1 %all-to-all-start = ((f32[16,64,1296]{2,1,0:T(8,128)}), f32[16,64,1296]{2,1,0:T(8,128)}, u32[]{:S(2)}, u32[]{:S(2)}) async-start(f32[16,64,1296]{2,1,0:T(8,128)} %broadcast_multiply_fusion.1), calls=%async_computation | async-start | bytes 11534336 | tf_op jit(solution)/shard_map/all_to_all | solution.py:130
  103.9 0.0 copy-done.4
  103.9 0.0 copy-done.2
  103.9 0.1 reshape_squeeze.7
  104.0 0.1 broadcast_multiply_fusion.2
  104.1 0.1 mul.358
  104.2 0.2 copy.66
  104.5 0.1 fusion.23
  104.6 2.8 gather_fusion.2
  107.4 0.2 copy.67
  107.6 0.1 fusion.26
  107.7 122.4 %all-to-all-done = f32[16,64,1296]{2,1,0:T(8,128)} async-done(((f32[16,64,1296]{2,1,0:T(8,128)}), f32[16,64,1296]{2,1,0:T(8,128)}, u32[]{:S(2)}, u32[]{:S(2)}) %all-to-all-start) | async-done | bytes 5308448 | tf_op jit(solution)/shard_map/all_to_all | solution.py:130
  230.1 14.5 %scatter_custom_fusion = f32[1024,1296]{1,0:T(8,128)} fusion(s32[1024]{0:T(1024)S(1)} %bitcast.46, f32[1024,1296]{1,0:T(8,128)} %bitcast.9, f32[]{:T(128)} %constant.36.clone.1), kind=kCustom, calls=%fused_computation.21 | custom fusion | flops 1327104 | bytes 5308928 | tf_op jit(solution)/shard_map/scatter-add | solution.py:136
  244.6 6.1 %copy.70 = f32[8,128,1296]{1,2,0:T(8,128)} copy(f32[8,128,1296]{2,1,0:T(8,128)} %bitcast.41) | data formatting | bytes 10616832 | tf_op jit(solution)/shard_map/reshape | solution.py:138
  250.7 8.2 %fusion.37 = (f32[8,127,1296]{1,2,0:T(8,128)S(1)}, f32[8,127,1296]{1,2,0:T(8,128)}) fusion(f32[8,128,1296]{1,2,0:T(8,128)} %copy.70), kind=kLoop, calls=%fused_computation.94 | loop fusion | bytes 21067776 | tf_op jit(solution)/shard_map/slice | solution.py:79
  258.8 0.0 copy-done
  258.8 4.4 subtract_multiply_fusion
  263.2 0.0 copy-start.1
  263.2 2.3 copy-done.1
  265.5 0.1 fusion.36
  265.6 3.6 collective-permute-start
  269.2 1.9 collective-permute-start.1
  271.1 0.1 reshape.497
  271.2 0.1 mul.369
  271.3 5.5 %collective-permute-done = f32[1,128,1296]{1,2,0:T(8,128)S(1)} collective-permute-done((f32[1,128,1296]{1,2,0:T(8,128)S(1)}, f32[1,128,1296]{1,2,0:T(8,128)S(1)}, u32[]{:S(2)}, u32[]{:S(2)}) %collective-permute-start) | collective-permute-done | bytes 663584 | tf_op jit(solution)/shard_map/ppermute | solution.py:36
  276.8 5.4 %collective-permute-done.1 = f32[1,128,1296]{1,2,0:T(8,128)S(1)} collective-permute-done((f32[1,128,1296]{1,2,0:T(8,128)S(1)}, f32[1,128,1296]{1,2,0:T(8,128)S(1)}, u32[]{:S(2)}, u32[]{:S(2)}) %collective-permute-start.1) | collective-permute-done | bytes 663584 | tf_op jit(solution)/shard_map/ppermute | solution.py:37
  282.2 8.0 %fusion.3 = f32[8,128,1296]{1,2,0:T(8,128)} fusion(f32[8,128,1296]{1,2,0:T(8,128)} %copy-done.1, f32[1,128,1296]{1,2,0:T(8,128)S(1)} %collective-permute-done.1, f32[1,128,1296]{1,2,0:T(8,128)S(1)} %collective-permute-done, f32[8,128]{1,0:T(8,128)S(1)} %get-tuple-element.13, f32[1296]{0:T(1024)S(1)} %mul.369, f32[8,128]{1,0:T(8,128)S(1)} %convert_element_type.18), kind=kLoop, calls=%fused_computation.10 | loop fusion | flops 17252352 | bytes 11957312 | tf_op jit(solution)/shard_map/mul | solution.py:88
  290.1 6.1 %copy.73 = f32[8,128,1296]{2,1,0:T(8,128)} copy(f32[8,128,1296]{1,2,0:T(8,128)} %fusion.3) | data formatting | bytes 10616832 | tf_op jit(solution)/shard_map/mul | solution.py:88
  296.3 10.0 %gather_fusion.3 = f32[1024,1296]{1,0:T(8,128)} fusion(f32[1024,1296]{1,0:T(8,128)} %bitcast.40, s32[1024]{0:T(1024)S(1)} %broadcast_clamp_fusion.1), kind=kCustom, calls=%fused_computation.3 | custom fusion | bytes 10620928 | tf_op jit(solution)/shard_map/gather | solution.py:147
  306.2 0.0 copy-start.3
  306.2 7.4 %all-to-all-start.1 = ((f32[16,64,1296]{2,1,0:T(8,128)}), f32[16,64,1296]{2,1,0:T(8,128)}, u32[]{:S(2)}, u32[]{:S(2)}) async-start(f32[16,64,1296]{2,1,0:T(8,128)} %bitcast.42), calls=%async_computation.1 | async-start | bytes 11534336 | tf_op jit(solution)/shard_map/all_to_all | solution.py:150
  313.7 0.0 copy-done.3
  313.7 0.1 reshape_squeeze.6
  313.8 126.8 %all-to-all-done.1 = f32[16,64,1296]{2,1,0:T(8,128)} async-done(((f32[16,64,1296]{2,1,0:T(8,128)}), f32[16,64,1296]{2,1,0:T(8,128)}, u32[]{:S(2)}, u32[]{:S(2)}) %all-to-all-start.1) | async-done | bytes 5308448 | tf_op jit(solution)/shard_map/all_to_all | solution.py:150
  440.6 5.6 %broadcast_multiply_fusion = f32[16,64,1296]{2,1,0:T(8,128)} fusion(f32[16,64,1296]{2,1,0:T(8,128)} %all-to-all-done.1, f32[16,64]{1,0:T(8,128)S(1)} %fusion.21), kind=kLoop, calls=%fused_computation.19 | loop fusion | flops 1327104 | bytes 10620928 | tf_op jit(solution)/shard_map/mul | solution.py:152
  446.2 12.3 %scatter_custom_fusion.1 = f32[512,1296]{1,0:T(8,128)S(1)} fusion(s32[1024]{0:T(1024)S(1)} %bitcast.47, f32[1024,1296]{1,0:T(8,128)} %bitcast.44, f32[]{:T(128)} %constant.36.clone.1), kind=kCustom, calls=%fused_computation.27 | custom fusion | flops 1327104 | bytes 2654720 | tf_op jit(solution)/shard_map/scatter-add | solution.py:151
  458.5 0.3 multiply_reduce_fusion
  458.8 2.2 copy.75
  461.0 10.8 %convolution_add_fusion = f32[512,1296]{0,1:T(8,128)} fusion(bf16[1296,1296]{1,0:T(8,128)(2,1)} %param.15, f32[512,1296]{0,1:T(8,128)} %copy.75, f32[512]{0:T(512)S(1)} %broadcast_multiply_fusion.6, f32[1296]{0:T(1024)S(1)} %mul.346, f32[512,1296]{0,1:T(8,128)} %div.80, f32[1296]{0:T(1024)S(1)} %div.83, f32[1296]{0:T(1024)S(1)} %mul.326), kind=kOutput, calls=%fused_computation.16 | convolution fusion | flops 1735852032 | bytes 11339456 | tf_op jit(solution)/shard_map/dot_general | solution.py:63
  (24 shorter events, 0.2 us)
Async XLA Ops:
  81.8 22.1 %copy-start.4 = (s32[8,128]{1,0:T(8,128)S(1)}, s32[8,128]{1,0:T(8,128)}, u32[]{:S(2)}) copy-start(s32[8,128]{1,0:T(8,128)} %param.19) | copy-start | bytes 12292
  81.8 22.1 %copy-start.2 = (s32[1,16,64]{2,1,0:T(8,128)S(1)}, s32[1,16,64]{2,1,0:T(8,128)}, u32[]{:S(2)}) copy-start(s32[1,16,64]{2,1,0:T(8,128)} %param.18) | copy-start | bytes 12292
  81.8 148.2 %all-to-all-start = ((f32[16,64,1296]{2,1,0:T(8,128)}), f32[16,64,1296]{2,1,0:T(8,128)}, u32[]{:S(2)}, u32[]{:S(2)}) async-start(f32[16,64,1296]{2,1,0:T(8,128)} %broadcast_multiply_fusion.1), calls=%async_computation | async-start | bytes 11534336 | tf_op jit(solution)/shard_map/all_to_all | solution.py:130
  250.7 8.2 %copy-start = (f32[8,128,1296]{1,2,0:T(8,128)S(1)}, f32[8,128,1296]{1,2,0:T(8,128)}, u32[]{:S(2)}) copy-start(f32[8,128,1296]{1,2,0:T(8,128)} %copy.70) | copy-start | bytes 15925252
  263.2 2.3 copy-start.1
  265.6 11.2 %collective-permute-start = (f32[1,128,1296]{1,2,0:T(8,128)S(1)}, f32[1,128,1296]{1,2,0:T(8,128)S(1)}, u32[]{:S(2)}, u32[]{:S(2)}) collective-permute-start(f32[1,128,1296]{1,2,0:T(8,128)S(1)} %get-tuple-element.9), channel_id=1, source_target_pairs={{0,1},{1,2},{2,3},{3,4},{4,5},{5,6},{6,7},{7,8},{8,9},{9,10},{10,1... | collective-permute-start | bytes 1990664 | tf_op jit(solution)/shard_map/ppermute | solution.py:36
  269.2 13.0 %collective-permute-start.1 = (f32[1,128,1296]{1,2,0:T(8,128)S(1)}, f32[1,128,1296]{1,2,0:T(8,128)S(1)}, u32[]{:S(2)}, u32[]{:S(2)}) collective-permute-start(f32[1,128,1296]{1,2,0:T(8,128)S(1)} %get-tuple-element.10), channel_id=1, source_target_pairs={{1,0},{2,1},{3,2},{4,3},{5,4},{6,5},{7,6},{8,7},{9,8},{10,9},{11,1... | collective-permute-start | bytes 1990664 | tf_op jit(solution)/shard_map/ppermute | solution.py:37
  306.2 7.4 %copy-start.3 = (s32[1,16,64]{2,1,0:T(8,128)S(1)}, s32[1,16,64]{2,1,0:T(8,128)}, u32[]{:S(2)}) copy-start(s32[1,16,64]{2,1,0:T(8,128)} %param.16) | copy-start | bytes 12292
  306.2 134.3 %all-to-all-start.1 = ((f32[16,64,1296]{2,1,0:T(8,128)}), f32[16,64,1296]{2,1,0:T(8,128)}, u32[]{:S(2)}, u32[]{:S(2)}) async-start(f32[16,64,1296]{2,1,0:T(8,128)} %bitcast.42), calls=%async_computation.1 | async-start | bytes 11534336 | tf_op jit(solution)/shard_map/all_to_all | solution.py:150
where the time goes:
time: 473 us; the launch traced here: 472 us
  waiting for transfers between devices  260 us (55%)
  other arithmetic  56.8 us (12%)
  local copies, waits for them, and re-layouts  52.2 us (11%)
  blocking collectives  44.6 us (9%)
  starting transfers between devices  35 us (7%)
  matrix products  21.6 us (5%)
    all_to_all x1, waiting for transfers between devices, on_device(): lax.all_to_all(outgoing, 'space', split_axis=0, concat_axis=0, tiled=True)  127 us
    all_to_all x1, waiting for transfers between devices, on_device(): lax.all_to_all(packed, 'space', split_axis=0, concat_axis=0, tiled=True)  122 us
    psum x1, blocking collectives, from_root(): return lax.psum(jnp.where(mine, array, jnp.zeros_like(array)), axis)  44.6 us
    all_to_all x1, starting transfers between devices, on_device(): lax.all_to_all(packed, 'space', split_axis=0, concat_axis=0, tiled=True)  22.1 us
    dot_general x2, matrix products, source_half(): jnp.dot(local_part.astype(jnp.bfloat16), coupling, preferred_element_type...  21.6 us
    scatter-add x1, other arithmetic, on_device(): energy_grid = jnp.zeros((row_count * col_count, spec_width), jnp.float32)...  14.5 us
    scatter-add x1, other arithmetic, on_device(): empty_rows.at[flat_rows]  12.3 us
    gather x1, local copies, waits for them, and re-layouts, on_device(): outgoing = swept[places]  9.96 us
  transfers between devices with their start and end apart: 4, of which 4 were waited for; matrix products, arithmetic and copies ran while one was open for 1% of the time, Pallas kernels for 0%

commit v1 on v0

--- a/solution.py
+++ b/solution.py
@@ -1,8 +1,12 @@
+import functools
 import math
 
 import jax
 import jax.numpy as jnp
+import numpy as np
 from jax import lax
+from jax.experimental import pallas as pl
+from jax.experimental.pallas import tpu as pltpu
 from jax.sharding import PartitionSpec as P
 
 DIRS = 36
@@ -94,7 +98,7 @@
     return rows_idx[:, None] // COARSE * (col_count // COARSE) + cols_idx[None, :] // COARSE
 
 
-def on_device(
+def on_strips(
     spectra,
     wind_files,
     current_files,
@@ -155,6 +159,365 @@
     return result
 
 
+LANES = 128
+F32 = jnp.float32
+VMEM_LIMIT = 56 * 1024 * 1024
+
+
+def wave_tables():
+    direction = 2.0 * np.pi / DIRS * np.arange(DIRS)
+    frequency = base_freq * freq_ratio ** (np.arange(FREQS) * (freq_span / (FREQS - 1)))
+    angular = 2.0 * np.pi * frequency
+    phase = gravity / angular
+    group = 0.5 * phase
+    cos_dir, sin_dir = np.cos(direction)[:, None], np.sin(direction)[:, None]
+    flat = lambda t: np.broadcast_to(t, (DIRS, FREQS)).reshape(-1)
+    source = np.zeros((8, DIRS * FREQS), np.float32)
+    source[0] = flat(wind_gain * cos_dir / phase)
+    source[1] = flat(wind_gain * sin_dir / phase)
+    source[2] = flat(half_length * input_coef * angular)
+    source[3] = flat(half_length * dissip_coef * angular)
+    east = flat(courant_scale * cos_dir * group).astype(np.float32)
+    north = flat(courant_scale * sin_dir * group).astype(np.float32)
+    return source, east, north
+
+
+def pad_lanes(array, rows):
+    flat = array.reshape(-1)
+    return jnp.pad(flat, (0, rows * LANES - flat.shape[0])).reshape(rows, LANES)
+
+
+def ceil_to(value, step):
+    return -(-value // step) * step
+
+
+def local_rows(energy, cp, winds, table_ref, spec):
+    half = len(winds) // 2
+    rows = energy.shape[0]
+    lane = lax.broadcasted_iota(jnp.int32, (rows, LANES), 1)
+    east = jnp.zeros((rows, LANES), F32)
+    north = jnp.zeros((rows, LANES), F32)
+    for q in range(half):
+        hit = cp == lane + q * LANES
+        east += jnp.where(hit, winds[q], 0.0)
+        north += jnp.where(hit, winds[half + q], 0.0)
+    east = jnp.sum(east, axis=1, keepdims=True)
+    north = jnp.sum(north, axis=1, keepdims=True)
+    mean_square = jnp.sum(energy * energy, axis=1, keepdims=True) * (1.0 / spec)
+    along = east * table_ref[0:1, :] + north * table_ref[1:2, :]
+    gain = 1.0 + table_ref[2:3, :] * jnp.maximum(along - 1.0, 0.0)
+    loss = 1.0 + table_ref[3:4, :] * mean_square
+    return energy * gain / loss
+
+
+def local_all(energy_ref, cp_ref, wind_ref, table_ref, loc_ref, locb_ref, block=32):
+    rows, spec = energy_ref.shape
+    wind = jnp.sum(wind_ref[...], axis=0)
+    winds = [wind[q : q + 1, :] for q in range(wind.shape[0])]
+
+    @pl.loop(0, rows // block)
+    def _(i):
+        at = pl.ds(pl.multiple_of(i * block, block), block)
+        local = local_rows(energy_ref[at, :], cp_ref[at, :], winds, table_ref, spec)
+        loc_ref[at, :] = local
+        locb_ref[at, :] = local.astype(jnp.bfloat16)
+
+
+def first_kernel(energy_ref, cp_ref, wind_ref, table_ref, coup_ref, out_ref, loc_ref, locb_ref):
+    rows, spec = energy_ref.shape
+    tiles = rows // LANES
+    local_all(energy_ref, cp_ref, wind_ref, table_ref, loc_ref, locb_ref)
+    wide = 2 * LANES
+    whole = spec // wide
+
+    @pl.loop(0, whole)
+    def _(q):
+        cols = pl.ds(pl.multiple_of(q * wide, wide), wide)
+        full = loc_ref[:, cols] + jnp.dot(
+            locb_ref[...], coup_ref[:, cols], preferred_element_type=F32
+        )
+        turned = full.T
+        start = pl.multiple_of(q * (wide * tiles), 8)
+        for j in range(tiles):
+            out_ref[pl.ds(start + j, wide, stride=tiles), :] = turned[:, j * LANES : (j + 1) * LANES]
+
+    left = spec - whole * wide
+    if left:
+        cols = pl.ds(whole * wide, left)
+        full = loc_ref[:, cols] + jnp.dot(
+            locb_ref[...], coup_ref[:, cols], preferred_element_type=F32
+        )
+        turned = full.T
+        for j in range(tiles):
+            out_ref[pl.ds(whole * wide * tiles + j, left, stride=tiles), :] = turned[
+                :, j * LANES : (j + 1) * LANES
+            ]
+
+
+def last_kernel(
+    turned_ref, cp_ref, wind_ref, table_ref, coup_ref, out_ref, energy_ref, loc_ref, locb_ref
+):
+    rows, spec = energy_ref.shape
+    tiles = rows // LANES
+    whole = spec // LANES
+
+    @pl.loop(0, whole)
+    def _(q):
+        start = pl.multiple_of(q * (LANES * tiles), 8)
+        cols = pl.ds(pl.multiple_of(q * LANES, LANES), LANES)
+        for j in range(tiles):
+            piece = turned_ref[pl.ds(start + j, LANES, stride=tiles), :]
+            energy_ref[j * LANES : (j + 1) * LANES, cols] = piece.T
+
+    left = spec - whole * LANES
+    if left:
+        for j in range(tiles):
+            piece = turned_ref[pl.ds(whole * LANES * tiles + j, left, stride=tiles), :]
+            energy_ref[j * LANES : (j + 1) * LANES, whole * LANES :] = piece.T
+
+    local_all(energy_ref, cp_ref, wind_ref, table_ref, loc_ref, locb_ref)
+    wide = 2 * LANES
+    whole = spec // wide
+
+    @pl.loop(0, whole)
+    def _(q):
+        cols = pl.ds(pl.multiple_of(q * wide, wide), wide)
+        out_ref[:, cols] = loc_ref[:, cols] + jnp.dot(
+            locb_ref[...], coup_ref[:, cols], preferred_element_type=F32
+        )
+
+    left = spec - whole * wide
+    if left:
+        cols = pl.ds(whole * wide, left)
+        out_ref[:, cols] = loc_ref[:, cols] + jnp.dot(
+            locb_ref[...], coup_ref[:, cols], preferred_element_type=F32
+        )
+
+
+def upwind(center, before, after, courant):
+    return center + jnp.abs(courant) * (jnp.where(courant > 0.0, before, after) - center)
+
+
+def sweep_kernel(
+    grid_rows, cols, depth, tiles,
+    place_ref, came_ref, east_ref, north_ref, speed_ref, out_ref, cell_ref, one_ref, two_ref, piece_ref,
+):
+    pitch = cols + 8
+    blocks = came_ref.shape[0] // (depth * tiles) * tiles
+    flag = depth
+    spare = lax.broadcasted_iota(jnp.int32, (LANES, LANES), 0) == flag
+    piece_ref[...] = jnp.where(spare, 1.0, 0.0)
+
+    @pl.loop(0, one_ref.shape[0] // LANES)
+    def _(i):
+        at = pl.ds(pl.multiple_of(i * LANES, LANES), LANES)
+        one_ref[at, :] = jnp.zeros((LANES, LANES), F32)
+
+    for edge in (0, grid_rows + 1):
+        two_ref[edge * pitch : (edge + 1) * pitch, :] = jnp.zeros((pitch, LANES), F32)
+
+    @pl.loop(0, blocks // tiles)
+    def _(s):
+        for j in range(tiles):
+            start = s * (depth * tiles) + j
+            piece_ref[0:depth, :] = came_ref[pl.ds(start, depth, stride=tiles), :]
+            at = pl.ds(pl.multiple_of((s * tiles + j) * LANES, LANES), LANES)
+            cell_ref[at, :] = piece_ref[...].T
+
+    unroll = 32
+
+    @pl.loop(0, blocks * LANES // unroll)
+    def _(i):
+        for t in range(unroll):
+            row = i * unroll + t
+            one_ref[pl.ds(place_ref[row], 1), :] = cell_ref[pl.ds(row, 1), :]
+
+    @pl.loop(0, grid_rows // COARSE)
+    def _(r4):
+        point = pl.ds(pl.multiple_of(r4 * cols, cols), cols)
+        courant = speed_ref[0:1, :] + east_ref[point, :]
+        for dr in range(COARSE):
+            base = pl.multiple_of((r4 * COARSE + dr + 1) * pitch + 8, 8)
+            center = one_ref[pl.ds(base, cols), :]
+            before = one_ref[pl.ds(base - 1, cols), :]
+            after = one_ref[pl.ds(base + 1, cols), :]
+            wet = jnp.broadcast_to(center[:, flag : flag + 1], center.shape)
+            two_ref[pl.ds(base, cols), :] = upwind(center, before, after, courant) * wet
+
+    @pl.loop(0, grid_rows // COARSE)
+    def _(r4):
+        point = pl.ds(pl.multiple_of(r4 * cols, cols), cols)
+        courant = speed_ref[1:2, :] + north_ref[point, :]
+        for dr in range(COARSE):
+            base = pl.multiple_of((r4 * COARSE + dr + 1) * pitch + 8, 8)
+            above = pl.multiple_of(base - pitch, 8)
+            below = pl.multiple_of(base + pitch, 8)
+            one_ref[pl.ds(base, cols), :] = upwind(
+                two_ref[pl.ds(base, cols), :],
+                two_ref[pl.ds(above, cols), :],
+                two_ref[pl.ds(below, cols), :],
+                courant,
+            )
+
+    @pl.loop(0, blocks * LANES // unroll)
+    def _(i):
+        for t in range(unroll):
+            row = i * unroll + t
+            cell_ref[pl.ds(row, 1), :] = one_ref[pl.ds(place_ref[row], 1), :]
+
+    @pl.loop(0, blocks // tiles)
+    def _(s):
+        for j in range(tiles):
+            start = s * (depth * tiles) + j
+            at = pl.ds(pl.multiple_of((s * tiles + j) * LANES, LANES), LANES)
+            turned = cell_ref[at, :].T
+            out_ref[pl.ds(start, depth, stride=tiles), :] = turned[0:depth, :]
+
+
+def in_vmem(count):
+    return [pl.BlockSpec(memory_space=pltpu.VMEM)] * count
+
+
+def on_spectrum(
+    spectra,
+    wind_files,
+    current_files,
+    reader_turn,
+    cell_point,
+    coupling,
+    send_list,
+    send_count,
+    recv_list,
+    wet_mask,
+):
+    shares = lax.axis_size("space")
+    me = lax.axis_index("space")
+    rows, spec = spectra.shape
+    depth = spec // shares
+    tiles = rows // LANES
+    cap = send_list.shape[2]
+    strip_rows, cols = wet_mask.shape
+    grid_rows = strip_rows * shares
+    points = wind_files.shape[2]
+    pitch = cols + 8
+    source, east_speed, north_speed = wave_tables()
+    table = jnp.asarray(source)
+
+    mine = 0.5 * (
+        (reader_turn[0] == me).astype(F32) + (reader_turn[1] == me).astype(F32)
+    )
+    force_rows = 2 * points // LANES
+    list_rows = -(-shares * cap // LANES)
+    pack = jnp.concatenate(
+        [
+            mine * wind_files[0].reshape(force_rows, LANES),
+            mine * current_files[0].reshape(force_rows, LANES),
+            pad_lanes(send_list[0].astype(F32), list_rows),
+            pad_lanes(recv_list[0].astype(F32), list_rows),
+            pad_lanes(send_count[0].astype(F32), -(-shares // LANES)),
+        ],
+        axis=0,
+    )
+    pack = jnp.pad(pack, ((0, ceil_to(pack.shape[0], 8) - pack.shape[0]), (0, 0)))
+    every = lax.all_gather(pack, "space")
+    wind = every[:, :force_rows]
+    current = jnp.sum(every[:, force_rows : 2 * force_rows], axis=0).reshape(2, points)
+    at = 2 * force_rows
+    sends = every[:, at : at + list_rows].reshape(shares, -1)[:, : shares * cap]
+    at += list_rows
+    lands = every[:, at : at + list_rows].reshape(shares, -1)[:, : shares * cap]
+    at += list_rows
+    counts = every[:, at:].reshape(shares, -1)[:, :shares]
+    sends = sends.reshape(shares, shares, cap)
+    lands = lands.reshape(shares, shares, cap).transpose(1, 0, 2)
+    strip = jnp.arange(shares, dtype=F32)[None, :, None] * (strip_rows * cols)
+    cell = (lands + strip).astype(jnp.int32)
+    position = (cell // cols + 1) * pitch + 8 + cell % cols
+    live = jnp.arange(cap, dtype=F32)[None, None, :] < counts[:, :, None]
+    position = jnp.where(live, position, 0).reshape(shares, 1, shares * cap)
+    names = jnp.where(live, sends, -1.0).reshape(shares, 1, shares * cap)
+    own = jnp.arange(rows, dtype=F32)[None, :, None]
+    place = jnp.sum(jnp.where(names == own, position, 0), axis=2).reshape(-1)
+
+    drift = (courant_scale * current).reshape(2, grid_rows // COARSE, cols // COARSE)
+    drift = jnp.repeat(drift, COARSE, axis=2).reshape(2, grid_rows // COARSE * cols, 1)
+    drift = jnp.broadcast_to(drift, (2, grid_rows // COARSE * cols, LANES))
+    speed = jnp.stack([jnp.asarray(east_speed), jnp.asarray(north_speed)])
+    speed = jnp.pad(speed, ((0, 6), (0, LANES)))
+    speed = lax.dynamic_slice(speed, (0, me * depth), (8, LANES))
+
+    cp = cell_point.reshape(rows, 1)
+    params = pltpu.CompilerParams(vmem_limit_bytes=VMEM_LIMIT)
+    flops = 2 * rows * spec * spec
+    turned = pl.pallas_call(
+        first_kernel,
+        out_shape=jax.ShapeDtypeStruct((spec * tiles, LANES), F32),
+        in_specs=in_vmem(5),
+        out_specs=pl.BlockSpec(memory_space=pltpu.VMEM),
+        scratch_shapes=[pltpu.VMEM((rows, spec), F32), pltpu.VMEM((rows, spec), jnp.bfloat16)],
+        compiler_params=params,
+        cost_estimate=pl.CostEstimate(
+            flops=flops, bytes_accessed=12 * rows * spec, transcendentals=0
+        ),
+        name="first_half",
+    )(spectra, cp, wind, table, coupling)
+    came = lax.all_to_all(
+        turned.reshape(shares, depth, tiles, LANES), "space", 0, 0, tiled=True
+    ).reshape(spec * tiles, LANES)
+    grid_size = ceil_to((grid_rows + 2) * pitch + 8, LANES)
+    swept = pl.pallas_call(
+        functools.partial(sweep_kernel, grid_rows, cols, depth, tiles),
+        out_shape=jax.ShapeDtypeStruct((spec * tiles, LANES), F32),
+        in_specs=[pl.BlockSpec(memory_space=pltpu.SMEM)] + in_vmem(4),
+        out_specs=pl.BlockSpec(memory_space=pltpu.VMEM),
+        scratch_shapes=[
+            pltpu.VMEM((shares * rows, LANES), F32),
+            pltpu.VMEM((grid_size, LANES), F32),
+            pltpu.VMEM((grid_size, LANES), F32),
+            pltpu.VMEM((LANES, LANES), F32),
+        ],
+        compiler_params=params,
+        cost_estimate=pl.CostEstimate(
+            flops=20 * grid_size * LANES, bytes_accessed=8 * rows * spec, transcendentals=0
+        ),
+        name="sweeps",
+    )(place, came, drift[0], drift[1], speed)
+    back = lax.all_to_all(
+        swept.reshape(shares, depth, tiles, LANES), "space", 0, 0, tiled=True
+    ).reshape(spec * tiles, LANES)
+    return pl.pallas_call(
+        last_kernel,
+        out_shape=jax.ShapeDtypeStruct((rows, spec), F32),
+        in_specs=in_vmem(5),
+        out_specs=pl.BlockSpec(memory_space=pltpu.VMEM),
+        scratch_shapes=[
+            pltpu.VMEM((rows, spec), F32),
+            pltpu.VMEM((rows, spec), F32),
+            pltpu.VMEM((rows, spec), jnp.bfloat16),
+        ],
+        compiler_params=params,
+        cost_estimate=pl.CostEstimate(
+            flops=flops, bytes_accessed=12 * rows * spec, transcendentals=0
+        ),
+        name="last_half",
+    )(back, cp, wind, table, coupling)
+
+
+def fits(shares, rows, spec, strip_rows, cols):
+    if spec % shares or spec // shares >= LANES or rows % LANES or cols % LANES:
+        return False
+    cells = shares * strip_rows * cols
+    held = LANES * 4 * (2 * (cells + cells // 8) + shares * rows + cells // 2)
+    return held + 8 * rows * spec < VMEM_LIMIT
+
+
+def on_device(*args):
+    spectra, wet_mask = args[0], args[9]
+    if fits(lax.axis_size("space"), *spectra.shape, *wet_mask.shape):
+        return on_spectrum(*args)
+    return on_strips(*args)
+
+
 def solution(mesh):
     placed = (
         P(("members", "space"), None),

time: 473 us -> 230 us (0.49)
  waiting for transfers between devices: 260 us -> 52 us
  Pallas kernels: 0 us -> 56.9 us
  other arithmetic: 56.8 us -> 7.15 us
  blocking collectives: 44.6 us -> 81.3 us
  local copies, waits for them, and re-layouts: 52.2 us -> 17.4 us
  starting transfers between devices: 35 us -> 10.3 us
  matrix products: 21.6 us -> 0 us
    all_to_all x2 -> x1, waiting for transfers between devices: 249 us -> 52 us  [on_spectrum(): lax.all_to_all(turned.reshape(shares, depth, tiles, LANES), 'space', 0, 0...]
    all_to_all x0 -> x1, blocking collectives: none -> 64.4 us  [on_spectrum(): lax.all_to_all(swept.reshape(shares, depth, tiles, LANES), 'space', 0, 0,...]
    pallas_call x0 -> x3, Pallas kernels: none -> 56.9 us  [the longest x1 32 us: on_spectrum(): pl.pallas_call(functools.partial(sweep_kernel, grid_rows, cols, depth, ti...]
    psum x1 -> x0, blocking collectives: 44.6 us -> none  [from_root(): return lax.psum(jnp.where(mine, array, jnp.zeros_like(array)), axis)]
    scatter-add x2 -> x0, other arithmetic: 26.8 us -> none  [the longest x1 14.5 us: on_device(): energy_grid = jnp.zeros((row_count * col_count, spec_width), jnp.float32)...]
    mul x12 -> x3, other arithmetic: 23.8 us -> 0.73 us  [the longest x1 0.72 us: on_spectrum(): mine * current_files[0].reshape(force_rows, LANES)]
    dot_general x2 -> x0, matrix products: 21.6 us -> none  [source_half(): jnp.dot(local_part.astype(jnp.bfloat16), coupling, preferred_element_type...]
    gather x5 -> x0, local copies, waits for them, and re-layouts: 19.8 us -> none  [the longest x1 9.96 us: on_device(): outgoing = swept[places]]
  transfers between devices with their start and end apart: 4 -> 1, of which waited for: 4 -> 1; matrix products, arithmetic and copies ran while one was open for 1% -> 3% of each run, Pallas kernels for 0% -> 0%
where the time goes in v1:
time: 230 us; the launch traced here: 226 us
  blocking collectives  81.3 us (35%)
  Pallas kernels  56.9 us (25%)
  waiting for transfers between devices  52 us (23%)
  local copies, waits for them, and re-layouts  17.4 us (8%)
  starting transfers between devices  10.3 us (4%)
  other arithmetic  7.15 us (3%)
    all_to_all x1, blocking collectives, on_spectrum(): lax.all_to_all(swept.reshape(shares, depth, tiles, LANES), 'space', 0, 0,...  64.4 us
    all_to_all x1, waiting for transfers between devices, on_spectrum(): lax.all_to_all(turned.reshape(shares, depth, tiles, LANES), 'space', 0, 0...  52 us
    pallas_call x1, Pallas kernels, on_spectrum(): pl.pallas_call(functools.partial(sweep_kernel, grid_rows, cols, depth, ti...  32 us
    all_gather x1, blocking collectives, on_spectrum(): every = lax.all_gather(pack, 'space')  16.9 us
    pallas_call x1, Pallas kernels, on_spectrum(): pl.pallas_call(last_kernel, out_shape=jax.ShapeDtypeStruct((rows, spec),...  12.9 us
    pallas_call x1, Pallas kernels, on_spectrum(): pl.pallas_call(first_kernel, out_shape=jax.ShapeDtypeStruct((spec * tiles...  11.9 us
    all_to_all x1, starting transfers between devices, on_spectrum(): lax.all_to_all(turned.reshape(shares, depth, tiles, LANES), 'space', 0, 0...  10.3 us
  transfers between devices with their start and end apart: 1, of which 1 were waited for; matrix products, arithmetic and copies ran while one was open for 3% of the time, Pallas kernels for 0%

profile of v1, /device:TPU:15, one launch (start us, length us, event | category | flops | bytes accessed | tf_op | source)
XLA Modules:
  0.0 226.5 jit_solution(13191810024320737061)
XLA Ops:
  0.0 1.3 fusion.13
  2.6 0.7 broadcast_multiply_fusion.1
  3.4 0.7 convert_element_type.40
  4.1 0.1 convert_element_type.41
  4.1 0.7 convert_element_type.42
  4.8 0.1 convert_element_type.43
  4.9 0.7 convert_bitcast_fusion
  5.6 16.9 %all-gather = f32[896,128]{1,0:T(8,128)S(1)} all-gather(f32[56,128]{1,0:T(8,128)S(1)} %pad.13), channel_id=2, replica_groups=mesh['members'=2,'space'=16] {'space'}, dimensions={0}, use_global_device_ids=true | all-gather | bytes 487424 | tf_op jit(solution)/shard_map/all_gather | solution.py:422
  22.5 0.7 slice_reduce_fusion
  23.2 1.5 copy.23.cp_ref
  24.7 3.3 %copy.22.energy_ref = f32[512,1296]{1,0:T(8,128)} copy(f32[512,1296]{0,1:T(8,128)} %param.13) | data formatting | bytes 5308416 | tf_op args[0]
  28.1 11.9 %first_half.1 = f32[5184,128]{1,0:T(8,128)} custom-call(f32[512,1296]{1,0:T(8,128)} %copy.22.energy_ref, s32[512,1]{1,0:T(8,128)} %copy.23.cp_ref, f32[16,16,128]{2,1,0:T(8,128)} %get-tuple-element.6.wind_ref, f32[8,1296]{1,0:T(8,128)} %constant.59.clone.table_ref, bf16[1296,1296]{1,0:T(8,128)(2,1)} %coup_ref.3), custom_call_target="tpu_custom_call" | custom-call | flops 1719926784 | bytes 7962624 | tf_op jit(solution)/shard_map/first_half/pallas_call | solution.py:452
  40.0 10.3 %all-to-all-start = ((f32[16,81,4,128]{3,2,1,0:T(4,128)}), f32[16,81,4,128]{3,2,1,0:T(4,128)S(1)}, u32[]{:S(2)}, u32[]{:S(2)}) async-start(f32[16,81,4,128]{3,2,1,0:T(4,128)} %bitcast.42), calls=%async_computation | async-start | bytes 5308416 | tf_op jit(solution)/shard_map/all_to_all | solution.py:464
  50.3 0.1 lt.39
  50.4 0.1 lt.40
  50.5 0.1 lt.37
  50.6 0.1 reshape_reshape.8
  50.7 0.2 fusion.4
  50.9 0.1 broadcast_in_dim.41
  51.1 3.4 %select_reduce_fusion = s32[16,512]{1,0:T(8,128)S(1)} fusion(s32[16,1024]{1,0:T(8,128)S(1)} %broadcast_in_dim.41, f32[16,1024]{1,0:T(8,128)S(1)} %bitcast_select_fusion), kind=kLoop, calls=%fused_computation | loop fusion | flops 25157632 | bytes 163840 | tf_op jit(solution)/shard_map/reduce_sum | solution.py:440
  54.5 0.6 copy.28
  55.1 0.1 slice.51
  55.2 0.2 broadcast_in_dim.44
  55.4 0.3 broadcast_in_dim.45
  55.7 0.1 slice.53
  55.8 0.2 broadcast_in_dim.47
  56.0 0.3 broadcast_in_dim.48
  56.2 1.4 constant_dynamic-slice_fusion.speed_ref
  57.6 52.0 %all-to-all-done = f32[16,81,4,128]{3,2,1,0:T(4,128)S(1)} async-done(((f32[16,81,4,128]{3,2,1,0:T(4,128)}), f32[16,81,4,128]{3,2,1,0:T(4,128)S(1)}, u32[]{:S(2)}, u32[]{:S(2)}) %all-to-all-start) | async-done | bytes 2654240 | tf_op jit(solution)/shard_map/all_to_all | solution.py:464
  109.6 0.0 copy-start
  109.7 2.2 broadcast_in_dim.46.east_ref
  111.8 2.0 broadcast_in_dim.49.north_ref
  113.8 0.0 copy-done
  113.8 32.0 %sweeps.1 = f32[5184,128]{1,0:T(8,128)} custom-call(s32[8192]{0:T(1024)} %bitcast.49, f32[5184,128]{1,0:T(8,128)} %bitcast.41, f32[4096,128]{1,0:T(8,128)} %broadcast_in_dim.46.east_ref, f32[4096,128]{1,0:T(8,128)} %broadcast_in_dim.49.north_ref, f32[8,128]{1,0:T(8,128)} %constant_dynamic-slice_fusion.speed_ref), custom_call_target="tpu_custom_call" | custom-call | flops 45547520 | bytes 5308416 | tf_op jit(solution)/shard_map/sweeps/pallas_call | solution.py:468
  145.8 64.4 %all_to_all.10 = f32[16,81,4,128]{3,2,1,0:T(4,128)} all-to-all(f32[16,81,4,128]{3,2,1,0:T(4,128)} %bitcast.43), channel_id=1, replica_groups=mesh['members'=2,'space'=16] {'space'}, dimensions={0} | all-to-all | bytes 5308416 | tf_op jit(solution)/shard_map/all_to_all | solution.py:485
  210.3 12.9 %last_half.1 = f32[512,1296]{1,0:T(8,128)} custom-call(f32[5184,128]{1,0:T(8,128)} %bitcast.44, s32[512,1]{1,0:T(8,128)} %copy.23.cp_ref, f32[16,16,128]{2,1,0:T(8,128)} %get-tuple-element.6.wind_ref, f32[8,1296]{1,0:T(8,128)} %constant.59.clone.table_ref, bf16[1296,1296]{1,0:T(8,128)(2,1)} %coup_ref.3), custom_call_target="tpu_custom_call" | custom-call | flops 1719926784 | bytes 7962624 | tf_op jit(solution)/shard_map/last_half/pallas_call | solution.py:488
  223.2 3.3 %copy.25 = f32[512,1296]{0,1:T(8,128)} copy(f32[512,1296]{1,0:T(8,128)} %last_half.1) | data formatting | bytes 5308416 | tf_op jit(solution)/shard_map/last_half/pallas_call | solution.py:488
  (17 shorter events, 0.2 us)
Async XLA Ops:
  40.0 69.6 %all-to-all-start = ((f32[16,81,4,128]{3,2,1,0:T(4,128)}), f32[16,81,4,128]{3,2,1,0:T(4,128)S(1)}, u32[]{:S(2)}, u32[]{:S(2)}) async-start(f32[16,81,4,128]{3,2,1,0:T(4,128)} %bitcast.42), calls=%async_computation | async-start | bytes 5308416 | tf_op jit(solution)/shard_map/all_to_all | solution.py:464
  109.6 4.2 %copy-start = (f32[16,81,4,128]{3,2,1,0:T(4,128)}, f32[16,81,4,128]{3,2,1,0:T(4,128)S(1)}, u32[]{:S(2)}) copy-start(f32[16,81,4,128]{3,2,1,0:T(4,128)S(1)} %all-to-all-done) | copy-start | bytes 7962628

commit v2 on v0

--- a/solution.py
+++ b/solution.py
@@ -1,8 +1,12 @@
+import functools
 import math
 
 import jax
 import jax.numpy as jnp
+import numpy as np
 from jax import lax
+from jax.experimental import pallas as pl
+from jax.experimental.pallas import tpu as pltpu
 from jax.sharding import PartitionSpec as P
 
 DIRS = 36
@@ -94,7 +98,7 @@
     return rows_idx[:, None] // COARSE * (col_count // COARSE) + cols_idx[None, :] // COARSE
 
 
-def on_device(
+def on_strips(
     spectra,
     wind_files,
     current_files,
@@ -155,6 +159,394 @@
     return result
 
 
+LANES = 128
+F32 = jnp.float32
+BF16 = jnp.bfloat16
+MIB = 1024 * 1024
+GRID_VMEM = 56 * MIB
+CHUNKS = 1
+
+
+def wave_tables():
+    direction = 2.0 * np.pi / DIRS * np.arange(DIRS)
+    frequency = base_freq * freq_ratio ** (np.arange(FREQS) * (freq_span / (FREQS - 1)))
+    angular = 2.0 * np.pi * frequency
+    phase = gravity / angular
+    group = 0.5 * phase
+    cos_dir, sin_dir = np.cos(direction)[:, None], np.sin(direction)[:, None]
+    flat = lambda t: np.broadcast_to(t, (DIRS, FREQS)).reshape(-1)
+    source = np.zeros((DIRS * FREQS, 8), np.float32)
+    source[:, 0] = flat(wind_gain * cos_dir / phase)
+    source[:, 1] = flat(wind_gain * sin_dir / phase)
+    source[:, 2] = flat(half_length * input_coef * angular)
+    source[:, 3] = flat(half_length * dissip_coef * angular)
+    east = flat(courant_scale * cos_dir * group).astype(np.float32)
+    north = flat(courant_scale * sin_dir * group).astype(np.float32)
+    return source, east, north
+
+
+def pad_lanes(array, rows):
+    flat = array.reshape(-1)
+    return jnp.pad(flat, (0, rows * LANES - flat.shape[0])).reshape(rows, LANES)
+
+
+def ceil_to(value, step):
+    return -(-value // step) * step
+
+
+def largest_step(size, step, most):
+    return max(s for s in range(step, most + 1, step) if size % s == 0)
+
+
+def cell_winds(wind_ref, cp_ref):
+    wind = jnp.sum(wind_ref[...], axis=0)
+    points, rows = wind.shape[1], cp_ref.shape[1]
+    high = wind.astype(BF16).astype(F32)
+    middle = (wind - high).astype(BF16).astype(F32)
+    low = wind - high - middle
+    parts = jnp.concatenate([high, middle, low, jnp.zeros((10, points), F32)], axis=0)
+    point = lax.broadcasted_iota(jnp.int32, (points, rows), 0)
+    hit = jnp.where(point == cp_ref[...], 1.0, 0.0).astype(BF16)
+    picked = jnp.dot(parts.astype(BF16), hit, preferred_element_type=F32)
+    both = picked[0:2] + picked[2:4] + picked[4:6]
+    return both[0:1], both[1:2]
+
+
+def half_step(load, spec, rows, wind_ref, cp_ref, table_ref, coup_ref, loc_ref, locb_ref, store):
+    east, north = cell_winds(wind_ref, cp_ref)
+    step = largest_step(spec, 16, 64)
+
+    def squares(i, total):
+        piece = load(pl.multiple_of(i * step, step), step)
+        return total + jnp.sum((piece * piece).reshape(step // 8, 8, rows), axis=0)
+
+    total = lax.fori_loop(0, spec // step, squares, jnp.zeros((8, rows), F32))
+    mean_square = jnp.sum(total, axis=0, keepdims=True) * (1.0 / spec)
+
+    @pl.loop(0, spec // step)
+    def _(i):
+        first = pl.multiple_of(i * step, step)
+        at = pl.ds(first, step)
+        table = table_ref[at, :]
+        along = east * table[:, 0:1] + north * table[:, 1:2]
+        gain = 1.0 + table[:, 2:3] * jnp.maximum(along - 1.0, 0.0)
+        loss = 1.0 + table[:, 3:4] * mean_square
+        local = load(first, step) * gain / loss
+        loc_ref[at, :] = local
+        locb_ref[at, :] = local.astype(BF16)
+
+    tall = largest_step(spec, 16, 512)
+
+    @pl.loop(0, spec // tall)
+    def _(q):
+        first = pl.multiple_of(q * tall, tall)
+        at = pl.ds(first, tall)
+        store(
+            first,
+            loc_ref[at, :]
+            + jnp.dot(coup_ref[at, :], locb_ref[...], preferred_element_type=F32),
+        )
+
+
+def strided_load(ref, tiles):
+    def load(first, count):
+        start = pl.multiple_of(first * tiles, 8)
+        return jnp.concatenate(
+            [ref[pl.ds(start + j, count, stride=tiles), :] for j in range(tiles)], axis=1
+        )
+
+    return load
+
+
+def strided_store(ref, tiles):
+    def store(first, values):
+        start = pl.multiple_of(first * tiles, 8)
+        for j in range(tiles):
+            ref[pl.ds(start + j, values.shape[0], stride=tiles), :] = values[
+                :, j * LANES : (j + 1) * LANES
+            ]
+
+    return store
+
+
+def first_kernel(energy_ref, cp_ref, wind_ref, table_ref, coup_ref, out_ref, loc_ref, locb_ref):
+    spec, rows = energy_ref.shape
+    half_step(
+        lambda first, count: energy_ref[pl.ds(first, count), :],
+        spec, rows, wind_ref, cp_ref, table_ref, coup_ref, loc_ref, locb_ref,
+        strided_store(out_ref, rows // LANES),
+    )
+
+
+def last_kernel(came_ref, cp_ref, wind_ref, table_ref, coup_ref, out_ref, loc_ref, locb_ref):
+    spec, rows = out_ref.shape
+
+    def store(first, values):
+        out_ref[pl.ds(first, values.shape[0]), :] = values
+
+    half_step(
+        strided_load(came_ref, rows // LANES),
+        spec, rows, wind_ref, cp_ref, table_ref, coup_ref, loc_ref, locb_ref, store,
+    )
+
+
+def upwind(center, before, after, courant):
+    return center + jnp.abs(courant) * (jnp.where(courant > 0.0, before, after) - center)
+
+
+class Sweeps:
+    def __init__(self, grid_rows, cols, depth, shares, rows, chunks):
+        self.grid_rows, self.cols, self.depth, self.shares = grid_rows, cols, depth, shares
+        self.rows = rows
+        self.part = rows // chunks
+        self.tiles = self.part // LANES
+        self.pitch = cols + 8
+        self.size = ceil_to((grid_rows + 2) * self.pitch + 8, LANES)
+
+    def clear(self, grid_ref):
+        @pl.loop(0, self.size // LANES)
+        def _(i):
+            at = pl.ds(pl.multiple_of(i * LANES, LANES), LANES)
+            grid_ref[at, :] = jnp.zeros((LANES, LANES), F32)
+
+    def turn_in(self, came_ref, cell_ref, piece_ref):
+        depth, tiles = self.depth, self.tiles
+        spare = lax.broadcasted_iota(jnp.int32, (LANES, LANES), 0) == depth
+        piece_ref[...] = jnp.where(spare, 1.0, 0.0)
+
+        @pl.loop(0, self.shares)
+        def _(s):
+            for j in range(tiles):
+                start = s * (depth * tiles) + j
+                piece_ref[0:depth, :] = came_ref[pl.ds(start, depth, stride=tiles), :]
+                at = pl.ds(pl.multiple_of((s * tiles + j) * LANES, LANES), LANES)
+                cell_ref[at, :] = piece_ref[...].T
+
+    def turn_out(self, cell_ref, out_ref):
+        depth, tiles = self.depth, self.tiles
+
+        @pl.loop(0, self.shares)
+        def _(s):
+            for j in range(tiles):
+                start = s * (depth * tiles) + j
+                at = pl.ds(pl.multiple_of((s * tiles + j) * LANES, LANES), LANES)
+                turned = cell_ref[at, :].T
+                out_ref[pl.ds(start, depth, stride=tiles), :] = turned[0:depth, :]
+
+    def each_row(self, chunk, place_ref, body, unroll=32):
+        per = self.part // unroll
+
+        @pl.loop(0, self.shares * per)
+        def _(i):
+            share, block = i // per, i % per
+            first = share * self.rows + chunk * self.part + block * unroll
+            for t in range(unroll):
+                body(i * unroll + t, place_ref[first + t])
+
+    def scatter(self, chunk, place_ref, cell_ref, grid_ref):
+        def body(row, place):
+            grid_ref[pl.ds(place, 1), :] = cell_ref[pl.ds(row, 1), :]
+
+        self.each_row(chunk, place_ref, body)
+
+    def gather(self, chunk, place_ref, cell_ref, grid_ref):
+        def body(row, place):
+            cell_ref[pl.ds(row, 1), :] = grid_ref[pl.ds(place, 1), :]
+
+        self.each_row(chunk, place_ref, body)
+
+    def sweep(self, drift_ref, speed_ref, one_ref, two_ref):
+        grid_rows, cols, pitch, flag = self.grid_rows, self.cols, self.pitch, self.depth
+        coarse_rows = grid_rows // COARSE
+        for edge in (0, grid_rows + 1):
+            two_ref[edge * pitch : (edge + 1) * pitch, :] = jnp.zeros((pitch, LANES), F32)
+        lane = lax.broadcasted_iota(jnp.int32, (cols, drift_ref.shape[1]), 1)
+
+        def courants(which, r4):
+            hit = lane == which * coarse_rows + r4
+            drift = jnp.sum(jnp.where(hit, drift_ref[...], 0.0), axis=1, keepdims=True)
+            return speed_ref[which : which + 1, :] + drift
+
+        @pl.loop(0, coarse_rows)
+        def _(r4):
+            courant = courants(0, r4)
+            for dr in range(COARSE):
+                base = pl.multiple_of((r4 * COARSE + dr + 1) * pitch + 8, 8)
+                center = one_ref[pl.ds(base, cols), :]
+                before = one_ref[pl.ds(base - 1, cols), :]
+                after = one_ref[pl.ds(base + 1, cols), :]
+                wet = jnp.broadcast_to(center[:, flag : flag + 1], center.shape)
+                two_ref[pl.ds(base, cols), :] = upwind(center, before, after, courant) * wet
+
+        @pl.loop(0, coarse_rows)
+        def _(r4):
+            courant = courants(1, r4)
+            for dr in range(COARSE):
+                base = pl.multiple_of((r4 * COARSE + dr + 1) * pitch + 8, 8)
+                above = pl.multiple_of(base - pitch, 8)
+                below = pl.multiple_of(base + pitch, 8)
+                one_ref[pl.ds(base, cols), :] = upwind(
+                    two_ref[pl.ds(base, cols), :],
+                    two_ref[pl.ds(above, cols), :],
+                    two_ref[pl.ds(below, cols), :],
+                    courant,
+                )
+
+
+def sweep_kernel(
+    sweeps, place_ref, came_ref, drift_ref, speed_ref, out_ref, cell_ref, one_ref, two_ref, piece_ref
+):
+    sweeps.clear(one_ref)
+    sweeps.turn_in(came_ref, cell_ref, piece_ref)
+    sweeps.scatter(0, place_ref, cell_ref, one_ref)
+    sweeps.sweep(drift_ref, speed_ref, one_ref, two_ref)
+    sweeps.gather(0, place_ref, cell_ref, one_ref)
+    sweeps.turn_out(cell_ref, out_ref)
+
+
+def in_vmem(count):
+    return [pl.BlockSpec(memory_space=pltpu.VMEM)] * count
+
+
+def on_spectrum(
+    spectra,
+    wind_files,
+    current_files,
+    reader_turn,
+    cell_point,
+    coupling,
+    send_list,
+    send_count,
+    recv_list,
+    wet_mask,
+):
+    shares = lax.axis_size("space")
+    me = lax.axis_index("space")
+    rows, spec = spectra.shape
+    depth = spec // shares
+    cap = send_list.shape[2]
+    strip_rows, cols = wet_mask.shape
+    grid_rows = strip_rows * shares
+    points = wind_files.shape[2]
+    sweeps = Sweeps(grid_rows, cols, depth, shares, rows, CHUNKS)
+    part, tiles, pitch = sweeps.part, sweeps.tiles, sweeps.pitch
+    source, east_speed, north_speed = wave_tables()
+    table = jnp.asarray(source)
+
+    mine = 0.5 * (
+        (reader_turn[0] == me).astype(F32) + (reader_turn[1] == me).astype(F32)
+    )
+    wind = lax.all_to_all(
+        jnp.broadcast_to(mine * wind_files, (shares, 2, points)), "space", 0, 0, tiled=True
+    )
+
+    force_rows = 2 * points // LANES
+    list_rows = -(-shares * cap // LANES)
+    pack = jnp.concatenate(
+        [
+            (mine * current_files[0]).reshape(force_rows, LANES),
+            pad_lanes(send_list[0].astype(F32), list_rows),
+            pad_lanes(recv_list[0].astype(F32), list_rows),
+            pad_lanes(send_count[0].astype(F32), -(-shares // LANES)),
+        ],
+        axis=0,
+    )
+    pack = jnp.pad(pack, ((0, ceil_to(pack.shape[0], 8) - pack.shape[0]), (0, 0)))
+    every = lax.all_gather(pack, "space")
+    current = jnp.sum(every[:, :force_rows], axis=0).reshape(2, points)
+    at = force_rows
+    sends = every[:, at : at + list_rows].reshape(shares, -1)[:, : shares * cap]
+    at += list_rows
+    lands = every[:, at : at + list_rows].reshape(shares, -1)[:, : shares * cap]
+    at += list_rows
+    counts = every[:, at:].reshape(shares, -1)[:, :shares]
+    sends = sends.reshape(shares, shares, cap)
+    lands = lands.reshape(shares, shares, cap).transpose(1, 0, 2)
+    strip = jnp.arange(shares, dtype=F32)[None, :, None] * (strip_rows * cols)
+    cell = (lands + strip).astype(jnp.int32)
+    position = (cell // cols + 1) * pitch + 8 + cell % cols
+    live = jnp.arange(cap, dtype=F32)[None, None, :] < counts[:, :, None]
+    position = jnp.where(live, position, 0).reshape(shares, 1, shares * cap)
+    names = jnp.where(live, sends, -1.0).reshape(shares, 1, shares * cap)
+    own = jnp.arange(rows, dtype=F32)[None, :, None]
+    place = jnp.sum(jnp.where(names == own, position, 0), axis=2).reshape(-1)
+
+    coarse_rows = grid_rows // COARSE
+    drift = (courant_scale * current).reshape(2 * coarse_rows, cols // COARSE)
+    drift = jnp.repeat(drift.T, COARSE, axis=0)
+    speed = jnp.stack([jnp.asarray(east_speed), jnp.asarray(north_speed)])
+    speed = jnp.pad(speed, ((0, 6), (0, LANES)))
+    speed = lax.dynamic_slice(speed, (0, me * depth), (8, LANES))
+
+    energy = spectra.T
+    cp = cell_point.reshape(1, rows)
+    coup = coupling.T
+    h_params = pltpu.CompilerParams(vmem_limit_bytes=28 * MIB)
+    h_cost = pl.CostEstimate(
+        flops=2 * part * spec * spec, bytes_accessed=12 * part * spec, transcendentals=0
+    )
+    h_scratch = [pltpu.VMEM((spec, part), F32), pltpu.VMEM((spec, part), BF16)]
+    turned = pl.pallas_call(
+        first_kernel,
+        out_shape=jax.ShapeDtypeStruct((spec * tiles, LANES), F32),
+        in_specs=in_vmem(5),
+        out_specs=pl.BlockSpec(memory_space=pltpu.VMEM),
+        scratch_shapes=h_scratch,
+        compiler_params=h_params,
+        cost_estimate=h_cost,
+        name="first_half",
+    )(energy, cp, wind, table, coup)
+    came = lax.all_to_all(
+        turned.reshape(shares, depth, tiles, LANES), "space", 0, 0, tiled=True
+    ).reshape(spec * tiles, LANES)
+    swept = pl.pallas_call(
+        functools.partial(sweep_kernel, sweeps),
+        out_shape=jax.ShapeDtypeStruct((spec * tiles, LANES), F32),
+        in_specs=[pl.BlockSpec(memory_space=pltpu.SMEM)] + in_vmem(3),
+        out_specs=pl.BlockSpec(memory_space=pltpu.VMEM),
+        scratch_shapes=[
+            pltpu.VMEM((shares * part, LANES), F32),
+            pltpu.VMEM((sweeps.size, LANES), F32),
+            pltpu.VMEM((sweeps.size, LANES), F32),
+            pltpu.VMEM((LANES, LANES), F32),
+        ],
+        compiler_params=pltpu.CompilerParams(vmem_limit_bytes=GRID_VMEM),
+        cost_estimate=pl.CostEstimate(
+            flops=20 * sweeps.size * LANES, bytes_accessed=8 * rows * spec, transcendentals=0
+        ),
+        name="sweeps",
+    )(place, came, drift, speed)
+    back = lax.all_to_all(
+        swept.reshape(shares, depth, tiles, LANES), "space", 0, 0, tiled=True
+    ).reshape(spec * tiles, LANES)
+    result = pl.pallas_call(
+        last_kernel,
+        out_shape=jax.ShapeDtypeStruct((spec, rows), F32),
+        in_specs=in_vmem(5),
+        out_specs=pl.BlockSpec(memory_space=pltpu.VMEM),
+        scratch_shapes=h_scratch,
+        compiler_params=h_params,
+        cost_estimate=h_cost,
+        name="last_half",
+    )(back, cp, wind, table, coup)
+    return result.T
+
+
+def fits(shares, rows, spec, strip_rows, cols):
+    if spec % shares or spec // shares >= LANES or rows % (CHUNKS * LANES) or cols % LANES:
+        return False
+    cells = shares * strip_rows * cols
+    held = LANES * 4 * (2 * (cells + cells // 8) + shares * rows)
+    return held + 8 * rows * spec < GRID_VMEM
+
+
+def on_device(*args):
+    spectra, wet_mask = args[0], args[9]
+    if fits(lax.axis_size("space"), *spectra.shape, *wet_mask.shape):
+        return on_spectrum(*args)
+    return on_strips(*args)
+
+
 def solution(mesh):
     placed = (
         P(("members", "space"), None),

time: 473 us -> 236 us (0.50)
  waiting for transfers between devices: 260 us -> 0.01 us
  blocking collectives: 44.6 us -> 134 us
  Pallas kernels: 0 us -> 53 us
  other arithmetic: 56.8 us -> 7.09 us
  local copies, waits for them, and re-layouts: 52.2 us -> 23.8 us
  starting transfers between devices: 35 us -> 12.7 us
  matrix products: 21.6 us -> 0 us
    all_to_all x2, waiting for transfers between devices: 249 us -> 0.01 us  [the longest x1 0.01 us: on_spectrum(): lax.all_to_all(turned.reshape(shares, depth, tiles, LANES), 'space', 0, 0...]
    all_gather x0 -> x1, blocking collectives: none -> 69.6 us  [on_spectrum(): every = lax.all_gather(pack, 'space')]
    all_to_all x0 -> x1, blocking collectives: none -> 64.7 us  [on_spectrum(): lax.all_to_all(swept.reshape(shares, depth, tiles, LANES), 'space', 0, 0,...]
    pallas_call x0 -> x3, Pallas kernels: none -> 53 us  [the longest x1 37.1 us: on_spectrum(): pl.pallas_call(functools.partial(sweep_kernel, sweeps), out_shape=jax.Sha...]
    psum x1 -> x0, blocking collectives: 44.6 us -> none  [from_root(): return lax.psum(jnp.where(mine, array, jnp.zeros_like(array)), axis)]
    scatter-add x2 -> x0, other arithmetic: 26.8 us -> none  [the longest x1 14.5 us: on_device(): energy_grid = jnp.zeros((row_count * col_count, spec_width), jnp.float32)...]
    mul x12 -> x3, other arithmetic: 23.8 us -> 0.02 us  [the longest x1 0.01 us: on_spectrum(): strip = jnp.arange(shares, dtype=F32)[None, :, None] * (strip_rows * cols)]
    dot_general x2 -> x0, matrix products: 21.6 us -> none  [source_half(): jnp.dot(local_part.astype(jnp.bfloat16), coupling, preferred_element_type...]
  transfers between devices with their start and end apart: 4 -> 2, of which waited for: 4 -> 0; matrix products, arithmetic and copies ran while one was open for 1% -> 10% of each run, Pallas kernels for 0% -> 0%
where the time goes in v2:
time: 236 us; the launch traced here: 232 us
  blocking collectives  134 us (57%)
  Pallas kernels  53 us (22%)
  local copies, waits for them, and re-layouts  23.8 us (10%)
  starting transfers between devices  12.7 us (5%)
  other arithmetic  7.09 us (3%)
    all_gather x1, blocking collectives, on_spectrum(): every = lax.all_gather(pack, 'space')  69.6 us
    all_to_all x1, blocking collectives, on_spectrum(): lax.all_to_all(swept.reshape(shares, depth, tiles, LANES), 'space', 0, 0,...  64.7 us
    pallas_call x1, Pallas kernels, on_spectrum(): pl.pallas_call(functools.partial(sweep_kernel, sweeps), out_shape=jax.Sha...  37.1 us
    unnamed x25, local copies, waits for them, and re-layouts  10.5 us
    pallas_call x1, Pallas kernels, on_spectrum(): pl.pallas_call(first_kernel, out_shape=jax.ShapeDtypeStruct((spec * tiles...  7.98 us
    pallas_call x1, Pallas kernels, on_spectrum(): pl.pallas_call(last_kernel, out_shape=jax.ShapeDtypeStruct((spec, rows),...  7.95 us
    all_to_all x1, starting transfers between devices, on_spectrum(): lax.all_to_all(jnp.broadcast_to(mine * wind_files, (shares, 2, points)),...  6.55 us
    all_to_all x1, starting transfers between devices, on_spectrum(): lax.all_to_all(turned.reshape(shares, depth, tiles, LANES), 'space', 0, 0...  6.16 us
  transfers between devices with their start and end apart: 2, of which 0 were waited for; matrix products, arithmetic and copies ran while one was open for 10% of the time, Pallas kernels for 0%

profile of v2, /device:TPU:15, one launch (start us, length us, event | category | flops | bytes accessed | tf_op | source)
XLA Modules:
  0.0 232.3 jit_solution(7502237641630301461)
XLA Ops:
  0.0 1.3 fusion.11
  2.6 0.7 multiply_bitcast_fusion
  3.3 0.7 broadcast_in_dim.39
  4.0 6.6 %all-to-all-start = ((f32[16,2,1024]{2,1,0:T(2,128)}), f32[16,2,1024]{2,1,0:T(2,128)S(1)}, u32[]{:S(2)}, u32[]{:S(2)}) async-start(f32[16,2,1024]{2,1,0:T(2,128)} %broadcast_in_dim.39), calls=%async_computation | async-start | bytes 262144 | tf_op jit(solution)/shard_map/all_to_all | solution.py:439
  10.5 0.0 copy-start.2
  10.6 0.0 copy-start.3
  10.6 0.0 copy-start.4
  10.6 6.2 %copy.25 = bf16[1296,1296]{0,1:T(8,128)(2,1)} copy(bf16[1296,1296]{1,0:T(8,128)(2,1)} %param.18) | data formatting | bytes 6718464 | tf_op args[5]
  16.8 0.0 all-to-all-done.wind_ref
  16.8 0.0 copy-done.2
  16.8 0.0 copy-done.3
  16.8 0.0 copy-done.4
  16.8 0.0 copy-start
  16.8 2.0 copy-done
  18.8 8.0 %first_half.1 = f32[5184,128]{1,0:T(8,128)} custom-call(f32[1296,512]{1,0:T(8,128)S(1)} %bitcast.48, s32[1,512]{1,0:T(1,128)S(1)} %bitcast.49, f32[16,2,1024]{2,1,0:T(2,128)S(1)} %all-to-all-done.wind_ref, f32[1296,8]{1,0:T(8,128)S(1)} %copy-done.2, bf16[1296,1296]{1,0:T(8,128)(2,1)S(1)} %bitcast.45), custom_call_target="tpu_custom_call" | custom-call | flops 1719926784 | bytes 7962624 | tf_op jit(solution)/shard_map/first_half/pallas_call | solution.py:489
  26.8 0.0 copy-start.7
  26.8 0.0 copy-start.8
  26.8 0.0 copy-start.9
  26.8 0.0 copy-start.10
  26.8 6.2 %all-to-all-start.1 = ((f32[16,81,4,128]{3,2,1,0:T(4,128)}), f32[16,81,4,128]{3,2,1,0:T(4,128)S(1)}, u32[]{:S(2)}, u32[]{:S(2)}) async-start(f32[16,81,4,128]{3,2,1,0:T(4,128)} %bitcast.11), calls=%async_computation.1 | async-start | bytes 5308416 | tf_op jit(solution)/shard_map/all_to_all | solution.py:499
  33.0 0.0 copy-done.7
  33.0 0.0 copy-done.8
  33.0 0.1 convert_element_type.41
  33.1 0.0 copy-done.9
  33.1 0.1 convert_element_type.43
  33.2 0.1 lt.37
  33.2 0.0 copy-done.10
  33.3 69.6 %all-gather = f32[640,128]{1,0:T(8,128)S(1)} all-gather(f32[40,128]{1,0:T(8,128)S(1)} %select_maximum_fusion), channel_id=2, replica_groups=mesh['members'=2,'space'=16] {'space'}, dimensions={0}, use_global_device_ids=true | all-gather | bytes 348160 | tf_op jit(solution)/shard_map/all_gather | solution.py:455
  102.8 0.0 copy-start.6
  102.8 0.7 copy-done.6
  103.6 0.1 mul.50
  103.7 0.1 copy.26
  103.8 1.6 fusion.10
  105.3 1.6 reshape_reshape.7
  106.9 1.0 copy.27
  107.9 0.7 slice.29
  108.6 0.1 copy.28
  108.7 1.1 fusion.4
  109.8 0.7 copy.24
  110.5 1.6 broadcast_in_dim.35
  112.1 0.8 lt.39.clone
  112.9 1.0 lt.40
  113.9 0.9 bitcast_select_fusion
  114.7 4.3 %select_reduce_fusion = s32[16,512]{1,0:T(8,128)S(1)} fusion(s32[16,1024]{1,0:T(8,128)} %broadcast_in_dim.35, f32[16,1024]{1,0:T(8,128)S(1)} %bitcast_select_fusion), kind=kLoop, calls=%fused_computation | loop fusion | flops 25157632 | bytes 163840 | tf_op jit(solution)/shard_map/reduce_sum | solution.py:472
  119.1 0.6 copy.30
  119.7 1.3 constant_dynamic-slice_fusion.speed_ref
  121.0 0.0 all-to-all-done.1
  121.0 0.0 copy-start.5
  121.0 0.7 broadcast_in_dim.40
  121.7 0.8 copy-done.5
  122.6 37.1 %sweeps.1 = f32[5184,128]{1,0:T(8,128)} custom-call(s32[8192]{0:T(1024)} %bitcast.58, f32[5184,128]{1,0:T(8,128)} %bitcast.51, f32[128,64]{1,0:T(8,128)} %bitcast.56, f32[8,128]{1,0:T(8,128)} %constant_dynamic-slice_fusion.speed_ref), custom_call_target="tpu_custom_call" | custom-call | flops 45547520 | bytes 5308416 | tf_op jit(solution)/shard_map/sweeps/pallas_call | solution.py:502
  159.6 0.0 copy-start.1
  159.7 64.7 %all_to_all.15 = f32[16,81,4,128]{3,2,1,0:T(4,128)S(1)} all-to-all(f32[16,81,4,128]{3,2,1,0:T(4,128)} %bitcast.52), channel_id=1, replica_groups=mesh['members'=2,'space'=16] {'space'}, dimensions={0} | all-to-all | bytes 5308416 | tf_op jit(solution)/shard_map/all_to_all | solution.py:519
  224.4 0.0 copy-done.1
  224.4 7.9 %last_half.1 = f32[1296,512]{1,0:T(8,128)} custom-call(f32[5184,128]{1,0:T(8,128)S(1)} %bitcast.47, s32[1,512]{1,0:T(1,128)S(1)} %bitcast.50, f32[16,2,1024]{2,1,0:T(2,128)S(1)} %all-to-all-done.wind_ref, f32[1296,8]{1,0:T(8,128)S(1)} %copy-done.2, bf16[1296,1296]{1,0:T(8,128)(2,1)S(1)} %bitcast.46), custom_call_target="tpu_custom_call" | custom-call | flops 1719926784 | bytes 7962624 | tf_op jit(solution)/shard_map/last_half/pallas_call | solution.py:522
  (11 shorter events, 0.1 us)
Async XLA Ops:
  4.0 12.8 %all-to-all-start = ((f32[16,2,1024]{2,1,0:T(2,128)}), f32[16,2,1024]{2,1,0:T(2,128)S(1)}, u32[]{:S(2)}, u32[]{:S(2)}) async-start(f32[16,2,1024]{2,1,0:T(2,128)} %broadcast_in_dim.39), calls=%async_computation | async-start | bytes 262144 | tf_op jit(solution)/shard_map/all_to_all | solution.py:439
  10.5 6.2 %copy-start.2 = (f32[1296,8]{1,0:T(8,128)S(1)}, f32[1296,8]{1,0:T(8,128)}, u32[]{:S(2)}) copy-start(f32[1296,8]{1,0:T(8,128)} %constant.59.clone.table_ref) | copy-start | bytes 124420
  10.6 6.2 %copy-start.3 = (f32[512,1296]{0,1:T(8,128)S(1)}, f32[512,1296]{0,1:T(8,128)}, u32[]{:S(2)}) copy-start(f32[512,1296]{0,1:T(8,128)} %param.13) | copy-start | bytes 7962628
  10.6 6.2 %copy-start.4 = (s32[512]{0:T(512)S(1)}, s32[512]{0:T(512)}, u32[]{:S(2)}) copy-start(s32[512]{0:T(512)} %param.17) | copy-start | bytes 6148
  16.8 2.0 copy-start
  26.8 6.2 %copy-start.7 = (f32[1,2,1024]{2,1,0:T(2,128)S(1)}, f32[1,2,1024]{2,1,0:T(2,128)}, u32[]{:S(2)}) copy-start(f32[1,2,1024]{2,1,0:T(2,128)} %param.15) | copy-start | bytes 24580
  26.8 6.2 %copy-start.8 = (s32[1,16,64]{2,1,0:T(8,128)S(1)}, s32[1,16,64]{2,1,0:T(8,128)}, u32[]{:S(2)}) copy-start(s32[1,16,64]{2,1,0:T(8,128)} %param.19) | copy-start | bytes 12292
  26.8 6.3 %copy-start.9 = (s32[1,16,64]{2,1,0:T(8,128)S(1)}, s32[1,16,64]{2,1,0:T(8,128)}, u32[]{:S(2)}) copy-start(s32[1,16,64]{2,1,0:T(8,128)} %param.21) | copy-start | bytes 12292
  26.8 6.5 %copy-start.10 = (s32[1,16]{1,0:T(1,128)S(1)}, s32[1,16]{1,0:T(1,128)}, u32[]{:S(2)}) copy-start(s32[1,16]{1,0:T(1,128)} %param.20) | copy-start | bytes 196
  26.8 94.2 %all-to-all-start.1 = ((f32[16,81,4,128]{3,2,1,0:T(4,128)}), f32[16,81,4,128]{3,2,1,0:T(4,128)S(1)}, u32[]{:S(2)}, u32[]{:S(2)}) async-start(f32[16,81,4,128]{3,2,1,0:T(4,128)} %bitcast.11), calls=%async_computation.1 | async-start | bytes 5308416 | tf_op jit(solution)/shard_map/all_to_all | solution.py:499
  102.8 0.8 copy-start.6
  121.0 1.5 copy-start.5
  159.6 64.7 %copy-start.1 = (bf16[1296,1296]{0,1:T(8,128)(2,1)S(1)}, bf16[1296,1296]{0,1:T(8,128)(2,1)}, u32[]{:S(2)}) copy-start(bf16[1296,1296]{0,1:T(8,128)(2,1)} %copy.25) | copy-start | bytes 10077700

commit v3 on v0

--- a/solution.py
+++ b/solution.py
@@ -1,8 +1,12 @@
+import functools
 import math
 
 import jax
 import jax.numpy as jnp
+import numpy as np
 from jax import lax
+from jax.experimental import pallas as pl
+from jax.experimental.pallas import tpu as pltpu
 from jax.sharding import PartitionSpec as P
 
 DIRS = 36
@@ -94,7 +98,7 @@
     return rows_idx[:, None] // COARSE * (col_count // COARSE) + cols_idx[None, :] // COARSE
 
 
-def on_device(
+def on_strips(
     spectra,
     wind_files,
     current_files,
@@ -155,6 +159,507 @@
     return result
 
 
+LANES = 128
+F32 = jnp.float32
+BF16 = jnp.bfloat16
+MIB = 1024 * 1024
+GRID_VMEM = 44 * MIB
+CHUNKS = 2
+
+
+def wave_tables():
+    direction = 2.0 * np.pi / DIRS * np.arange(DIRS)
+    frequency = base_freq * freq_ratio ** (np.arange(FREQS) * (freq_span / (FREQS - 1)))
+    angular = 2.0 * np.pi * frequency
+    phase = gravity / angular
+    group = 0.5 * phase
+    cos_dir, sin_dir = np.cos(direction)[:, None], np.sin(direction)[:, None]
+    flat = lambda t: np.broadcast_to(t, (DIRS, FREQS)).reshape(-1)
+    source = np.zeros((DIRS * FREQS, 8), np.float32)
+    source[:, 0] = flat(wind_gain * cos_dir / phase)
+    source[:, 1] = flat(wind_gain * sin_dir / phase)
+    source[:, 2] = flat(half_length * input_coef * angular)
+    source[:, 3] = flat(half_length * dissip_coef * angular)
+    east = flat(courant_scale * cos_dir * group).astype(np.float32)
+    north = flat(courant_scale * sin_dir * group).astype(np.float32)
+    return source, east, north
+
+
+def ceil_to(value, step):
+    return -(-value // step) * step
+
+
+def largest_step(size, step, most):
+    return max(s for s in range(step, most + 1, step) if size % s == 0)
+
+
+class Plan:
+    def __init__(self, shares, rows, spec, cap, strip_rows, cols, points):
+        self.shares, self.rows, self.spec, self.cap = shares, rows, spec, cap
+        self.cols, self.points = cols, points
+        self.depth = spec // shares
+        self.part = rows // CHUNKS
+        self.tiles = self.part // LANES
+        self.data = self.depth * self.tiles
+        self.force = 2 * points // (LANES * shares)
+        self.block = ceil_to(self.data + self.tiles + self.force, 8)
+        self.strip = strip_rows * cols
+        self.grid_rows = strip_rows * shares
+        self.coarse_rows = self.grid_rows // COARSE
+        self.pitch = cols + 8
+        self.size = ceil_to((self.grid_rows + 2) * self.pitch + 8, LANES)
+
+    def fits(self):
+        if self.spec % self.shares or self.depth >= LANES or self.rows % (CHUNKS * LANES):
+            return False
+        if 2 * self.points % (LANES * self.shares) or self.cap > LANES or self.cols != LANES:
+            return False
+        if 2 * self.points // LANES > LANES:
+            return False
+        cells = 2 * self.size + 2 * self.coarse_rows * self.cols + self.shares * self.part
+        held = LANES * 4 * (cells + self.shares * (self.block + self.data))
+        return held + 4 * MIB < GRID_VMEM
+
+
+def pack_kernel(plan, turn_ref, wind_ref, current_ref, recv_ref, out_ref):
+    me = lax.axis_index("space")
+    half = lambda at: jnp.where(turn_ref[at] == me, 0.5, 0.0)
+    mine = half(0) + half(1)
+    wind = mine * wind_ref[0]
+    points, width, cap = plan.points, plan.force * LANES, plan.cap
+    for s in range(plan.shares):
+        out_ref[s, :, 0:points] = wind
+        out_ref[s, :, points:] = jnp.zeros((2, out_ref.shape[2] - points), F32)
+        out_ref[s, 0:1, points : points + cap] = recv_ref[0, s : s + 1, :].astype(F32)
+        which, first = divmod(s * width, points)
+        out_ref[s, 1:2, points : points + width] = (
+            mine * current_ref[0, which : which + 1, first : first + width]
+        )
+
+
+def cell_winds(wind, cp):
+    points, rows = wind.shape[1], cp.shape[1]
+    high = wind.astype(BF16).astype(F32)
+    middle = (wind - high).astype(BF16).astype(F32)
+    low = wind - high - middle
+    parts = jnp.concatenate([high, middle, low, jnp.zeros((10, points), F32)], axis=0)
+    point = lax.broadcasted_iota(jnp.int32, (points, rows), 0)
+    hit = jnp.where(point == cp, 1.0, 0.0).astype(BF16)
+    picked = jnp.dot(parts.astype(BF16), hit, preferred_element_type=F32)
+    both = picked[0:2] + picked[2:4] + picked[4:6]
+    return both[0:1], both[1:2]
+
+
+def half_step(plan, load, wind, cp, table_ref, coup_ref, loc_ref, locb_ref, store):
+    spec, rows = plan.spec, plan.part
+    east, north = cell_winds(wind, cp)
+    step = largest_step(spec, 16, 64)
+
+    def squares(i, total):
+        piece = load(pl.multiple_of(i * step, step), step)
+        return total + jnp.sum((piece * piece).reshape(step // 8, 8, rows), axis=0)
+
+    total = lax.fori_loop(0, spec // step, squares, jnp.zeros((8, rows), F32))
+    mean_square = jnp.sum(total, axis=0, keepdims=True) * (1.0 / spec)
+
+    @pl.loop(0, spec // step)
+    def _(i):
+        first = pl.multiple_of(i * step, step)
+        at = pl.ds(first, step)
+        table = table_ref[at, :]
+        along = east * table[:, 0:1] + north * table[:, 1:2]
+        gain = 1.0 + table[:, 2:3] * jnp.maximum(along - 1.0, 0.0)
+        loss = 1.0 + table[:, 3:4] * mean_square
+        local = load(first, step) * gain / loss
+        loc_ref[at, :] = local
+        locb_ref[at, :] = local.astype(BF16)
+
+    tall = largest_step(spec, 16, 512)
+    for q in range(spec // tall):
+        at = slice(q * tall, (q + 1) * tall)
+        store(
+            q * tall,
+            loc_ref[at, :]
+            + jnp.dot(coup_ref[at, :], locb_ref[...], preferred_element_type=F32),
+        )
+
+
+def first_kernel(
+    plan, chunk,
+    energy_ref, cp_ref, parcel_ref, names_ref, table_ref, coup_ref, out_ref, buf_ref, loc_ref, locb_ref,
+):
+    part, tiles, shares, points = plan.part, plan.tiles, plan.shares, plan.points
+    lanes = slice(chunk * part, (chunk + 1) * part)
+
+    def store(first, values):
+        for j in range(tiles):
+            buf_ref[pl.ds(first * tiles + j, values.shape[0], stride=tiles), :] = values[
+                :, j * LANES : (j + 1) * LANES
+            ]
+
+    wind = jnp.sum(parcel_ref[:, :, 0:points], axis=0)
+    half_step(
+        plan, lambda first, count: energy_ref[pl.ds(first, count), lanes],
+        wind, cp_ref[:, lanes], table_ref, coup_ref, loc_ref, locb_ref, store,
+    )
+
+    landing = jnp.concatenate(
+        [parcel_ref[b, 0:1, points : points + LANES] for b in range(shares)], axis=0
+    ).astype(jnp.int32)
+    cell = landing + plan.strip * lax.broadcasted_iota(jnp.int32, (shares, LANES), 0)
+    place = (cell + lax.div(cell, plan.cols) * (plan.pitch - plan.cols) + plan.pitch + 8).astype(F32)
+    own = lax.broadcasted_iota(jnp.int32, (part, LANES), 0) + chunk * part
+    found = jnp.zeros((part, LANES), F32)
+    for b in range(shares):
+        found += jnp.where(names_ref[b : b + 1, :] == own, place[b : b + 1, :], 0.0)
+    found = jnp.broadcast_to(jnp.sum(found, axis=1, keepdims=True), (part, LANES))
+    spare = [found[j * LANES : (j + 1) * LANES, :].T[0:1, :] for j in range(tiles)]
+    if chunk == 0:
+        width = plan.force * LANES
+        current = jnp.sum(parcel_ref[:, :, points : points + width], axis=0)
+        spare += [current[1:2, f * LANES : (f + 1) * LANES] for f in range(plan.force)]
+    spare.append(jnp.zeros((plan.block - plan.data - len(spare), LANES), F32))
+    spare = jnp.concatenate(spare, axis=0)
+    for d in range(shares):
+        out_ref[d * plan.block : (d + 1) * plan.block, :] = buf_ref[
+            d * plan.data : d * plan.data + plan.block, :
+        ]
+        out_ref[d * plan.block + plan.data : (d + 1) * plan.block, :] = spare
+
+
+def last_kernel(
+    plan, chunk,
+    came_ref, cp_ref, parcel_ref, table_ref, coup_ref, held_ref, out_ref, res_ref, loc_ref, locb_ref, sems,
+):
+    part, tiles = plan.part, plan.tiles
+    lanes = slice(chunk * part, (chunk + 1) * part)
+    copies = []
+
+    def load(first, count):
+        start = pl.multiple_of(first * tiles, 8)
+        return jnp.concatenate(
+            [came_ref[pl.ds(start + j, count, stride=tiles), :] for j in range(tiles)], axis=1
+        )
+
+    def store(first, values):
+        at = slice(first, first + values.shape[0])
+        res_ref[at, :] = values
+        copies.append(
+            pltpu.make_async_copy(res_ref.at[at, :], out_ref.at[at, lanes], sems.at[len(copies)])
+        )
+        copies[-1].start()
+
+    wind = jnp.sum(parcel_ref[:, :, 0 : plan.points], axis=0)
+    half_step(plan, load, wind, cp_ref[:, lanes], table_ref, coup_ref, loc_ref, locb_ref, store)
+    for copy in copies:
+        copy.wait()
+
+
+def upwind(center, before, after, courant):
+    return center + jnp.abs(courant) * (jnp.where(courant > 0.0, before, after) - center)
+
+
+def clear(plan, grid_ref):
+    @pl.loop(0, plan.size // LANES)
+    def _(i):
+        at = pl.ds(pl.multiple_of(i * LANES, LANES), LANES)
+        grid_ref[at, :] = jnp.zeros((LANES, LANES), F32)
+
+
+def turn_in(plan, came_ref, cell_ref, piece_ref):
+    depth, tiles = plan.depth, plan.tiles
+    flag = lax.broadcasted_iota(jnp.int32, (LANES, LANES), 0) == depth
+    piece_ref[...] = jnp.where(flag, 1.0, 0.0)
+
+    @pl.loop(0, plan.shares)
+    def _(s):
+        for j in range(tiles):
+            piece_ref[0:depth, :] = came_ref[pl.ds(s * plan.block + j, depth, stride=tiles), :]
+            at = pl.ds(pl.multiple_of((s * tiles + j) * LANES, LANES), LANES)
+            cell_ref[at, :] = piece_ref[...].T
+
+
+def turn_out(plan, cell_ref, out_ref):
+    depth, tiles = plan.depth, plan.tiles
+
+    @pl.loop(0, plan.shares)
+    def _(s):
+        for j in range(tiles):
+            at = pl.ds(pl.multiple_of((s * tiles + j) * LANES, LANES), LANES)
+            turned = cell_ref[at, :].T
+            out_ref[pl.ds(s * plan.data + j, depth, stride=tiles), :] = turned[0:depth, :]
+
+
+def places(plan, came_ref, spot_ref):
+    for s in range(plan.shares):
+        first = s * plan.block + plan.data
+        spot_ref[s * plan.tiles : (s + 1) * plan.tiles, :] = came_ref[
+            first : first + plan.tiles, :
+        ].astype(jnp.int32)
+
+
+def each_row(plan, spot_ref, body, unroll=32):
+    per = LANES // unroll
+
+    @pl.loop(0, plan.shares * plan.tiles * per)
+    def _(i):
+        block, first = i // per, (i % per) * unroll
+        for t in range(unroll):
+            body(i * unroll + t, spot_ref[block, first + t])
+
+
+def scatter(plan, spot_ref, cell_ref, grid_ref):
+    def body(row, place):
+        grid_ref[pl.ds(place, 1), :] = cell_ref[pl.ds(row, 1), :]
+
+    each_row(plan, spot_ref, body)
+
+
+def gather(plan, spot_ref, cell_ref, grid_ref):
+    def body(row, place):
+        cell_ref[pl.ds(row, 1), :] = grid_ref[pl.ds(place, 1), :]
+
+    each_row(plan, spot_ref, body)
+
+
+def spread_drift(plan, came_ref, piece_ref, drift_ref):
+    piece_ref[...] = jnp.zeros((LANES, LANES), F32)
+    for s in range(plan.shares):
+        first = s * plan.block + plan.data + plan.tiles
+        piece_ref[s * plan.force : (s + 1) * plan.force, :] = came_ref[
+            first : first + plan.force, :
+        ]
+    turned = (courant_scale * piece_ref[...]).T
+    for q in range(plan.shares * plan.force):
+        wide = jnp.broadcast_to(turned[:, q : q + 1], (LANES, LANES))
+        for t in range(COARSE):
+            drift_ref[pl.ds(q * LANES * COARSE + t, LANES, stride=COARSE), :] = wide
+
+
+def sweep_columns(plan, drift_ref, speed_ref, one_ref, two_ref):
+    cols, pitch, flag = plan.cols, plan.pitch, plan.depth
+
+    @pl.loop(0, plan.coarse_rows)
+    def _(r4):
+        courant = speed_ref[0:1, :] + drift_ref[pl.ds(pl.multiple_of(r4 * cols, cols), cols), :]
+        for dr in range(COARSE):
+            base = pl.multiple_of((r4 * COARSE + dr + 1) * pitch + 8, 8)
+            center = one_ref[pl.ds(base, cols), :]
+            before = one_ref[pl.ds(base - 1, cols), :]
+            after = one_ref[pl.ds(base + 1, cols), :]
+            wet = jnp.broadcast_to(center[:, flag : flag + 1], center.shape)
+            two_ref[pl.ds(base, cols), :] = upwind(center, before, after, courant) * wet
+
+
+def sweep_rows_in_vmem(plan, drift_ref, speed_ref, one_ref, two_ref):
+    cols, pitch = plan.cols, plan.pitch
+
+    @pl.loop(0, plan.coarse_rows)
+    def _(r4):
+        point = pl.multiple_of((plan.coarse_rows + r4) * cols, cols)
+        courant = speed_ref[1:2, :] + drift_ref[pl.ds(point, cols), :]
+        for dr in range(COARSE):
+            base = pl.multiple_of((r4 * COARSE + dr + 1) * pitch + 8, 8)
+            above = pl.multiple_of(base - pitch, 8)
+            below = pl.multiple_of(base + pitch, 8)
+            one_ref[pl.ds(base, cols), :] = upwind(
+                two_ref[pl.ds(base, cols), :],
+                two_ref[pl.ds(above, cols), :],
+                two_ref[pl.ds(below, cols), :],
+                courant,
+            )
+
+
+def land_kernel(plan, came_ref, grid_ref, drift_ref, spot_ref, cell_ref, piece_ref, smem_ref, sem):
+    places(plan, came_ref, spot_ref)
+    copy = pltpu.make_async_copy(spot_ref, smem_ref, sem)
+    copy.start()
+    clear(plan, grid_ref)
+    spread_drift(plan, came_ref, piece_ref, drift_ref)
+    turn_in(plan, came_ref, cell_ref, piece_ref)
+    copy.wait()
+    scatter(plan, smem_ref, cell_ref, grid_ref)
+
+
+def sweep_kernel(
+    plan,
+    came_ref, spot0_ref, speed_ref, grid_ref, drift_ref,
+    out_ref, swept_ref, spot_ref,
+    cell_ref, one_ref, two_ref, wide_ref, piece_ref, smem_ref, sems,
+):
+    get_grid = pltpu.make_async_copy(grid_ref, one_ref, sems.at[0])
+    get_drift = pltpu.make_async_copy(drift_ref, wide_ref, sems.at[1])
+    get_grid.start()
+    get_drift.start()
+    places(plan, came_ref, spot_ref)
+    get_spot = pltpu.make_async_copy(spot_ref, smem_ref, sems.at[2])
+    get_spot.start()
+    for edge in (0, plan.grid_rows + 1):
+        two_ref[edge * plan.pitch : (edge + 1) * plan.pitch, :] = jnp.zeros((plan.pitch, LANES), F32)
+    turn_in(plan, came_ref, cell_ref, piece_ref)
+    get_spot.wait()
+    get_grid.wait()
+    scatter(plan, smem_ref, cell_ref, one_ref)
+    get_drift.wait()
+    sweep_columns(plan, wide_ref, speed_ref, one_ref, two_ref)
+    sweep_rows_in_vmem(plan, wide_ref, speed_ref, one_ref, two_ref)
+    put_grid = pltpu.make_async_copy(one_ref, swept_ref, sems.at[0])
+    put_grid.start()
+    gather(plan, spot0_ref, cell_ref, one_ref)
+    turn_out(plan, cell_ref, out_ref)
+    put_grid.wait()
+
+
+def take_kernel(plan, spot_ref, grid_ref, out_ref, cell_ref):
+    gather(plan, spot_ref, cell_ref, grid_ref)
+    turn_out(plan, cell_ref, out_ref)
+
+
+VMEM = pl.BlockSpec(memory_space=pltpu.VMEM)
+SMEM = pl.BlockSpec(memory_space=pltpu.SMEM)
+ANY = pl.BlockSpec(memory_space=pl.ANY)
+
+
+def on_spectrum(
+    plan,
+    spectra,
+    wind_files,
+    current_files,
+    reader_turn,
+    cell_point,
+    coupling,
+    send_list,
+    send_count,
+    recv_list,
+):
+    me = lax.axis_index("space")
+    shares, rows, spec, points = plan.shares, plan.rows, plan.spec, plan.points
+    part, tiles, size = plan.part, plan.tiles, plan.size
+    source, east_speed, north_speed = wave_tables()
+    table = jnp.asarray(source)
+    block_rows, data_rows = shares * plan.block, shares * plan.data
+    drift_rows = 2 * plan.coarse_rows * plan.cols
+
+    def kernel(body, *, vmem, flops, traffic, **options):
+        return pl.pallas_call(
+            body,
+            compiler_params=pltpu.CompilerParams(vmem_limit_bytes=vmem),
+            cost_estimate=pl.CostEstimate(flops=flops, bytes_accessed=traffic, transcendentals=0),
+            **options,
+        )
+
+    width = points + max(LANES, plan.force * LANES)
+    parcel = kernel(
+        functools.partial(pack_kernel, plan),
+        vmem=8 * MIB, flops=0, traffic=4 * shares * 2 * width,
+        out_shape=jax.ShapeDtypeStruct((shares, 2, width), F32),
+        in_specs=[SMEM, VMEM, VMEM, VMEM],
+        out_specs=VMEM,
+        name="pack",
+    )(reader_turn, wind_files, current_files, recv_list)
+    parcel = lax.all_to_all(parcel, "space", 0, 0, tiled=True)
+
+    slot = jnp.arange(plan.cap, dtype=jnp.int32)[None, :]
+    names = jnp.where(slot < send_count[0][:, None], send_list[0], -1)
+    names = jnp.pad(names, ((0, 0), (0, LANES - plan.cap)), constant_values=-1)
+    speed = jnp.stack([jnp.asarray(east_speed), jnp.asarray(north_speed)])
+    speed = jnp.pad(speed, ((0, 6), (0, LANES)))
+    speed = lax.dynamic_slice(speed, (0, me * plan.depth), (8, LANES))
+
+    energy = spectra.T
+    cp = cell_point.reshape(1, rows)
+    coup = coupling.T
+    h_flops, h_traffic = 2 * part * spec * spec, 8 * part * spec
+    h_scratch = [pltpu.VMEM((spec, part), F32), pltpu.VMEM((spec, part), BF16)]
+
+    def first(chunk):
+        block = kernel(
+            functools.partial(first_kernel, plan, chunk),
+            vmem=28 * MIB, flops=h_flops, traffic=h_traffic,
+            out_shape=jax.ShapeDtypeStruct((block_rows, LANES), F32),
+            in_specs=[VMEM] * 6,
+            out_specs=VMEM,
+            scratch_shapes=[pltpu.VMEM((data_rows + plan.block, LANES), F32)] + h_scratch,
+            name=f"first_half_{chunk}",
+        )(energy, cp, parcel, names, table, coup)
+        block = block.reshape(shares, plan.block, LANES)
+        return lax.all_to_all(block, "space", 0, 0, tiled=True).reshape(block_rows, LANES)
+
+    def home(block):
+        block = block.reshape(shares, plan.depth, tiles, LANES)
+        return lax.all_to_all(block, "space", 0, 0, tiled=True).reshape(data_rows, LANES)
+
+    cells = pltpu.VMEM((shares * part, LANES), F32)
+    piece = pltpu.VMEM((LANES, LANES), F32)
+    grid_shape = jax.ShapeDtypeStruct((size, LANES), F32)
+    spot_shape = jax.ShapeDtypeStruct((shares * tiles, LANES), jnp.int32)
+    smem = pltpu.SMEM((shares * tiles, LANES), jnp.int32)
+    block_shape = jax.ShapeDtypeStruct((data_rows, LANES), F32)
+
+    came = [first(chunk) for chunk in range(CHUNKS)]
+    grid, drift, spot0 = kernel(
+        functools.partial(land_kernel, plan),
+        vmem=GRID_VMEM, flops=0, traffic=8 * size * LANES,
+        out_shape=[grid_shape, jax.ShapeDtypeStruct((drift_rows, LANES), F32), spot_shape],
+        in_specs=[VMEM],
+        out_specs=[VMEM, VMEM, VMEM],
+        scratch_shapes=[cells, piece, smem, pltpu.SemaphoreType.DMA],
+        name="land",
+    )(came[0])
+    out0, swept, spot1 = kernel(
+        functools.partial(sweep_kernel, plan),
+        vmem=GRID_VMEM, flops=20 * size * LANES, traffic=16 * size * LANES,
+        out_shape=[block_shape, grid_shape, spot_shape],
+        in_specs=[VMEM, SMEM, VMEM, ANY, ANY],
+        out_specs=[VMEM, ANY, VMEM],
+        scratch_shapes=[
+            cells,
+            pltpu.VMEM((size, LANES), F32),
+            pltpu.VMEM((size, LANES), F32),
+            pltpu.VMEM((drift_rows, LANES), F32),
+            piece,
+            smem,
+            pltpu.SemaphoreType.DMA((3,)),
+        ],
+        name="sweeps",
+    )(came[1], spot0, speed, grid, drift)
+    back0 = home(out0)
+    out1 = kernel(
+        functools.partial(take_kernel, plan),
+        vmem=GRID_VMEM, flops=0, traffic=8 * size * LANES,
+        out_shape=block_shape,
+        in_specs=[SMEM, VMEM],
+        out_specs=VMEM,
+        scratch_shapes=[cells],
+        name="take",
+    )(spot1, swept)
+    back1 = home(out1)
+
+    result = jnp.zeros((8, LANES), F32)
+    for chunk, back in enumerate((back0, back1)):
+        result = kernel(
+            functools.partial(last_kernel, plan, chunk),
+            vmem=28 * MIB, flops=h_flops, traffic=h_traffic,
+            out_shape=jax.ShapeDtypeStruct((spec, rows), F32),
+            in_specs=[VMEM] * 5 + [ANY],
+            out_specs=ANY,
+            scratch_shapes=[pltpu.VMEM((spec, part), F32)] + h_scratch + [pltpu.SemaphoreType.DMA((8,))],
+            input_output_aliases={5: 0} if chunk else {},
+            name=f"last_half_{chunk}",
+        )(back, cp, parcel, table, coup, result)
+    return result.T
+
+
+def on_device(*args):
+    spectra, wind_files, send_list, wet_mask = args[0], args[1], args[6], args[9]
+    plan = Plan(
+        lax.axis_size("space"), *spectra.shape, send_list.shape[2], *wet_mask.shape, wind_files.shape[2]
+    )
+    if plan.fits():
+        return on_spectrum(plan, *args[:9])
+    return on_strips(*args)
+
+
 def solution(mesh):
     placed = (
         P(("members", "space"), None),

time: 473 us -> 216 us (0.46)
  waiting for transfers between devices: 260 us -> 73.7 us
  Pallas kernels: 0 us -> 89.9 us
  other arithmetic: 56.8 us -> 0.07 us
  blocking collectives: 44.6 us -> 0 us
  local copies, waits for them, and re-layouts: 52.2 us -> 24.3 us
  matrix products: 21.6 us -> 0 us
  starting transfers between devices: 35 us -> 27.2 us
    all_to_all x2 -> x5, waiting for transfers between devices: 249 us -> 73.7 us  [the longest x2 38.2 us: home(): lax.all_to_all(block, 'space', 0, 0, tiled=True).reshape(data_rows, LANES)]
    pallas_call x0 -> x8, Pallas kernels: none -> 89.9 us  [the longest x1 34 us: on_spectrum(): kernel(functools.partial(sweep_kernel, plan), vmem=GRID_VMEM, flops=20 *...]
    psum x1 -> x0, blocking collectives: 44.6 us -> none  [from_root(): return lax.psum(jnp.where(mine, array, jnp.zeros_like(array)), axis)]
    scatter-add x2 -> x0, other arithmetic: 26.8 us -> none  [the longest x1 14.5 us: on_device(): energy_grid = jnp.zeros((row_count * col_count, spec_width), jnp.float32)...]
    mul x12 -> x0, other arithmetic: 23.8 us -> none  [the longest x1 7.97 us: sweep_rows(): advect(energy_grid, row_above, row_below, courant) * wet_field[:, :, None]]
    dot_general x2 -> x0, matrix products: 21.6 us -> none  [source_half(): jnp.dot(local_part.astype(jnp.bfloat16), coupling, preferred_element_type...]
    unnamed x10 -> x35, local copies, waits for them, and re-layouts: 2.32 us -> 23.5 us
    gather x5 -> x0, local copies, waits for them, and re-layouts: 19.8 us -> none  [the longest x1 9.96 us: on_device(): outgoing = swept[places]]
  transfers between devices with their start and end apart: 4 -> 5, of which waited for: 4 -> 4; matrix products, arithmetic and copies ran while one was open for 1% -> 3% of each run, Pallas kernels for 0% -> 21%
where the time goes in v3:
time: 216 us; the launch traced here: 215 us
  Pallas kernels  89.9 us (42%)
  waiting for transfers between devices  73.7 us (34%)
  starting transfers between devices  27.2 us (13%)
  local copies, waits for them, and re-layouts  24.3 us (11%)
    all_to_all x2, waiting for transfers between devices, home(): lax.all_to_all(block, 'space', 0, 0, tiled=True).reshape(data_rows, LANES)  38.2 us
    all_to_all x2, waiting for transfers between devices, first(): lax.all_to_all(block, 'space', 0, 0, tiled=True).reshape(block_rows, LANES)  35.5 us
    pallas_call x1, Pallas kernels, on_spectrum(): kernel(functools.partial(sweep_kernel, plan), vmem=GRID_VMEM, flops=20 *...  34 us
    unnamed x35, local copies, waits for them, and re-layouts  23.5 us
    pallas_call x1, Pallas kernels, on_spectrum(): kernel(functools.partial(land_kernel, plan), vmem=GRID_VMEM, flops=0, tra...  17.7 us
    pallas_call x1, Pallas kernels, on_spectrum(): kernel(functools.partial(take_kernel, plan), vmem=GRID_VMEM, flops=0, tra...  16.1 us
    pallas_call x2, Pallas kernels, on_spectrum(): kernel(functools.partial(last_kernel, plan, chunk), vmem=28 * MIB, flops=...  11 us
    all_to_all x2, starting transfers between devices, first(): lax.all_to_all(block, 'space', 0, 0, tiled=True).reshape(block_rows, LANES)  10.9 us
  transfers between devices with their start and end apart: 5, of which 4 were waited for; matrix products, arithmetic and copies ran while one was open for 3% of the time, Pallas kernels for 21%

profile of v3, /device:TPU:15, one launch (start us, length us, event | category | flops | bytes accessed | tf_op | source)
XLA Modules:
  0.0 215.3 jit_solution(7984114982475856153)
XLA Ops:
  0.0 0.0 copy-start.11
  0.0 0.7 copy-done.11
  0.7 0.0 copy-start.12
  0.7 0.7 copy-done.12
  1.4 0.0 copy-start.13
  1.4 0.7 copy-done.13
  2.1 0.0 copy-start.14
  2.1 0.7 copy-done.14
  2.7 1.2 pack.1
  4.0 6.6 %all-to-all-start = ((f32[16,2,1152]{2,1,0:T(2,128)}), f32[16,2,1152]{2,1,0:T(2,128)S(1)}, u32[]{:S(2)}, u32[]{:S(2)}) async-start(f32[16,2,1152]{2,1,0:T(2,128)} %pack.1), calls=%async_computation | async-start | bytes 294912 | tf_op jit(solution)/shard_map/all_to_all | solution.py:560
  10.5 0.0 copy-start.15
  10.5 0.0 copy-start.16
  10.6 0.0 copy-start.4
  10.6 0.0 copy-start.5
  10.6 0.0 copy-start.10
  10.6 6.2 %copy.14 = bf16[1296,1296]{0,1:T(8,128)(2,1)} copy(bf16[1296,1296]{1,0:T(8,128)(2,1)} %param.18) | data formatting | bytes 6718464 | tf_op args[5]
  16.8 0.0 copy-done.15
  16.8 0.0 copy-done.16
  16.8 0.1 bitcast_select_fusion
  16.9 0.0 all-to-all-done.parcel_ref
  16.9 0.0 copy-done.4
  16.9 0.0 copy-done.5
  16.9 0.0 copy-done.10
  16.9 0.0 copy-start
  16.9 2.0 copy-done
  18.9 5.0 %first_half_0.1 = f32[2688,128]{1,0:T(8,128)S(1)} custom-call(f32[1296,512]{1,0:T(8,128)S(1)} %bitcast.19, s32[1,512]{1,0:T(1,128)S(1)} %bitcast.26, f32[16,2,1152]{2,1,0:T(2,128)S(1)} %all-to-all-done.parcel_ref, s32[16,128]{1,0:T(8,128)S(1)} %pad.8.names_ref, f32[1296,8]{1,0:T(8,128)S(1)} %copy-done.4, bf16[1296,1296]{1,0:T(8,128)(2,1)S(1)} %bitcast.15), custom_call_target="tpu_custom_call" | custom-call | flops 859963392 | bytes 2654208 | tf_op jit(solution)/shard_map/first_half_0/pallas_call | solution.py:576
  23.9 0.0 copy-start.7
  23.9 1.1 copy-done.7
  25.0 6.1 %all-to-all-start.2 = ((f32[16,168,128]{2,1,0:T(8,128)}), f32[16,168,128]{2,1,0:T(8,128)}, u32[]{:S(2)}, u32[]{:S(2)}) async-start(f32[16,168,128]{2,1,0:T(8,128)} %bitcast.23), calls=%async_computation.2 | async-start | bytes 2752512 | tf_op jit(solution)/shard_map/all_to_all | solution.py:586
  31.1 0.0 copy-start.1
  31.1 2.0 copy-done.1
  33.1 4.9 %first_half_1.1 = f32[2688,128]{1,0:T(8,128)S(1)} custom-call(f32[1296,512]{1,0:T(8,128)S(1)} %bitcast.20, s32[1,512]{1,0:T(1,128)S(1)} %bitcast.27, f32[16,2,1152]{2,1,0:T(2,128)S(1)} %all-to-all-done.parcel_ref, s32[16,128]{1,0:T(8,128)S(1)} %pad.8.names_ref, f32[1296,8]{1,0:T(8,128)S(1)} %copy-done.4, bf16[1296,1296]{1,0:T(8,128)(2,1)S(1)} %bitcast.16), custom_call_target="tpu_custom_call" | custom-call | flops 859963392 | bytes 2654208 | tf_op jit(solution)/shard_map/first_half_1/pallas_call | solution.py:576
  38.0 0.0 copy-start.6
  38.0 1.1 copy-done.6
  39.1 24.1 %all-to-all-done.2 = f32[16,168,128]{2,1,0:T(8,128)} async-done(((f32[16,168,128]{2,1,0:T(8,128)}), f32[16,168,128]{2,1,0:T(8,128)}, u32[]{:S(2)}, u32[]{:S(2)}) %all-to-all-start.2) | async-done | bytes 1376288 | tf_op jit(solution)/shard_map/all_to_all | solution.py:586
  63.2 4.8 %all-to-all-start.1 = ((f32[16,168,128]{2,1,0:T(8,128)}), f32[16,168,128]{2,1,0:T(8,128)S(1)}, u32[]{:S(2)}, u32[]{:S(2)}) async-start(f32[16,168,128]{2,1,0:T(8,128)} %bitcast.22), calls=%async_computation.1 | async-start | bytes 2752512 | tf_op jit(solution)/shard_map/all_to_all | solution.py:586
  68.0 0.8 constant_dynamic-slice_fusion.speed_ref
  68.8 17.7 %land.1 = (f32[17792,128]{1,0:T(8,128)}, f32[8192,128]{1,0:T(8,128)S(1)}, s32[32,128]{1,0:T(8,128)S(1)}) custom-call(f32[2688,128]{1,0:T(8,128)} %bitcast.8.came_ref), custom_call_target="tpu_custom_call" | custom-call | bytes 18219008 | tf_op jit(solution)/shard_map/land/pallas_call | solution.py:600
  86.5 0.0 copy-start.8
  86.5 2.1 copy-done.8
  88.5 11.4 %all-to-all-done.1 = f32[16,168,128]{2,1,0:T(8,128)S(1)} async-done(((f32[16,168,128]{2,1,0:T(8,128)}), f32[16,168,128]{2,1,0:T(8,128)S(1)}, u32[]{:S(2)}, u32[]{:S(2)}) %all-to-all-start.1) | async-done | bytes 1376288 | tf_op jit(solution)/shard_map/all_to_all | solution.py:586
  100.0 0.0 copy-start.9
  100.0 2.2 %copy-done.9 = f32[8192,128]{1,0:T(8,128)S(1)} copy-done((f32[8192,128]{1,0:T(8,128)S(1)}, f32[8192,128]{1,0:T(8,128)}, u32[]{:S(2)}) %copy-start.9) | copy-done | bytes 4194328
  102.2 34.0 %sweeps.1 = (f32[2592,128]{1,0:T(8,128)}, f32[17792,128]{1,0:T(8,128)}, s32[32,128]{1,0:T(8,128)S(1)}) custom-call(f32[2688,128]{1,0:T(8,128)S(1)} %bitcast.21, s32[32,128]{1,0:T(8,128)S(1)} %get-tuple-element.11.spot0_ref, f32[8,128]{1,0:T(8,128)S(1)} %constant_dynamic-slice_fusion.speed_ref, f32[17792,128]{1,0:T(8,128)} %get-tuple-element.12.grid_ref, ...), custom_call_target="tpu_custom_call" | custom-call | flops 45547520 | bytes 36438016 | tf_op jit(solution)/shard_map/sweeps/pallas_call | solution.py:609
  136.2 4.9 %all-to-all-start.4 = ((f32[16,81,2,128]{3,2,1,0:T(2,128)}), f32[16,81,2,128]{3,2,1,0:T(2,128)S(1)}, u32[]{:S(2)}, u32[]{:S(2)}) async-start(f32[16,81,2,128]{3,2,1,0:T(2,128)} %bitcast.11), calls=%async_computation.4 | async-start | bytes 2654208 | tf_op jit(solution)/shard_map/all_to_all | solution.py:590
  141.1 16.1 %take.1 = f32[2592,128]{1,0:T(8,128)} custom-call(s32[32,128]{1,0:T(8,128)S(1)} %get-tuple-element.14.spot_ref, f32[17792,128]{1,0:T(8,128)} %get-tuple-element.15.grid_ref), custom_call_target="tpu_custom_call" | custom-call | bytes 18219008 | tf_op jit(solution)/shard_map/take/pallas_call | solution.py:627
  157.2 14.8 %all-to-all-done.4 = f32[16,81,2,128]{3,2,1,0:T(2,128)S(1)} async-done(((f32[16,81,2,128]{3,2,1,0:T(2,128)}), f32[16,81,2,128]{3,2,1,0:T(2,128)S(1)}, u32[]{:S(2)}, u32[]{:S(2)}) %all-to-all-start.4) | async-done | bytes 1327136 | tf_op jit(solution)/shard_map/all_to_all | solution.py:590
  172.0 4.9 %all-to-all-start.3 = ((f32[16,81,2,128]{3,2,1,0:T(2,128)}), f32[16,81,2,128]{3,2,1,0:T(2,128)S(1)}, u32[]{:S(2)}, u32[]{:S(2)}) async-start(f32[16,81,2,128]{3,2,1,0:T(2,128)} %bitcast.9), calls=%async_computation.3 | async-start | bytes 2654208 | tf_op jit(solution)/shard_map/all_to_all | solution.py:590
  176.9 0.0 copy-start.2
  176.9 2.0 copy-done.2
  178.9 5.5 %last_half_0.1.held_ref = f32[1296,512]{1,0:T(8,128)} custom-call(f32[2592,128]{1,0:T(8,128)S(1)} %bitcast.24, s32[1,512]{1,0:T(1,128)S(1)} %bitcast.28, f32[16,2,1152]{2,1,0:T(2,128)S(1)} %all-to-all-done.parcel_ref, f32[1296,8]{1,0:T(8,128)S(1)} %copy-done.4, bf16[1296,1296]{1,0:T(8,128)(2,1)S(1)} %bitcast.17, f32[8,128]{1,0:T(8,128)S(1)} %broadcast_in_dim.9.held_ref), custom_call_target="tpu_custom_call" | custom-call | flops 859963392 | bytes 2654208 | tf_op jit(solution)/shard_map/last_half_0/pallas_call | solution.py:640
  184.4 23.4 %all-to-all-done.3 = f32[16,81,2,128]{3,2,1,0:T(2,128)S(1)} async-done(((f32[16,81,2,128]{3,2,1,0:T(2,128)}), f32[16,81,2,128]{3,2,1,0:T(2,128)S(1)}, u32[]{:S(2)}, u32[]{:S(2)}) %all-to-all-start.3) | async-done | bytes 1327136 | tf_op jit(solution)/shard_map/all_to_all | solution.py:590
  207.8 0.0 copy-start.3
  207.8 2.0 copy-done.3
  209.8 5.5 %last_half_1.1 = f32[1296,512]{1,0:T(8,128)} custom-call(f32[2592,128]{1,0:T(8,128)S(1)} %bitcast.25, s32[1,512]{1,0:T(1,128)S(1)} %bitcast.29, f32[16,2,1152]{2,1,0:T(2,128)S(1)} %all-to-all-done.parcel_ref, f32[1296,8]{1,0:T(8,128)S(1)} %copy-done.4, bf16[1296,1296]{1,0:T(8,128)(2,1)S(1)} %bitcast.18, ...), custom_call_target="tpu_custom_call", output_to_operand_aliasing={{}: (5, {})} | custom-call | flops 859963392 | bytes 2654208 | tf_op jit(solution)/shard_map/last_half_1/pallas_call | solution.py:640
  (2 shorter events, 0.0 us)
Async XLA Ops:
  0.0 0.7 copy-start.11
  0.7 0.7 copy-start.12
  1.4 0.7 copy-start.13
  2.1 0.7 copy-start.14
  4.0 12.9 %all-to-all-start = ((f32[16,2,1152]{2,1,0:T(2,128)}), f32[16,2,1152]{2,1,0:T(2,128)S(1)}, u32[]{:S(2)}, u32[]{:S(2)}) async-start(f32[16,2,1152]{2,1,0:T(2,128)} %pack.1), calls=%async_computation | async-start | bytes 294912 | tf_op jit(solution)/shard_map/all_to_all | solution.py:560
  10.5 6.2 %copy-start.15 = (s32[1,16,64]{2,1,0:T(8,128)S(1)}, s32[1,16,64]{2,1,0:T(8,128)}, u32[]{:S(2)}) copy-start(s32[1,16,64]{2,1,0:T(8,128)} %param.19) | copy-start | bytes 12292
  10.5 6.2 %copy-start.16 = (s32[1,16]{1,0:T(1,128)S(1)}, s32[1,16]{1,0:T(1,128)}, u32[]{:S(2)}) copy-start(s32[1,16]{1,0:T(1,128)} %param.20) | copy-start | bytes 196
  10.6 6.3 %copy-start.4 = (f32[1296,8]{1,0:T(8,128)S(1)}, f32[1296,8]{1,0:T(8,128)}, u32[]{:S(2)}) copy-start(f32[1296,8]{1,0:T(8,128)} %constant.21.clone.table_ref) | copy-start | bytes 124420
  10.6 6.3 %copy-start.5 = (f32[512,1296]{0,1:T(8,128)S(1)}, f32[512,1296]{0,1:T(8,128)}, u32[]{:S(2)}) copy-start(f32[512,1296]{0,1:T(8,128)} %param.13) | copy-start | bytes 7962628
  10.6 6.3 %copy-start.10 = (s32[512]{0:T(512)S(1)}, s32[512]{0:T(512)}, u32[]{:S(2)}) copy-start(s32[512]{0:T(512)} %param.17) | copy-start | bytes 6148
  16.9 2.0 copy-start
  23.9 1.1 copy-start.7
  25.0 38.2 %all-to-all-start.2 = ((f32[16,168,128]{2,1,0:T(8,128)}), f32[16,168,128]{2,1,0:T(8,128)}, u32[]{:S(2)}, u32[]{:S(2)}) async-start(f32[16,168,128]{2,1,0:T(8,128)} %bitcast.23), calls=%async_computation.2 | async-start | bytes 2752512 | tf_op jit(solution)/shard_map/all_to_all | solution.py:586
  31.1 2.0 copy-start.1
  38.0 1.1 copy-start.6
  63.2 36.8 %all-to-all-start.1 = ((f32[16,168,128]{2,1,0:T(8,128)}), f32[16,168,128]{2,1,0:T(8,128)S(1)}, u32[]{:S(2)}, u32[]{:S(2)}) async-start(f32[16,168,128]{2,1,0:T(8,128)} %bitcast.22), calls=%async_computation.1 | async-start | bytes 2752512 | tf_op jit(solution)/shard_map/all_to_all | solution.py:586
  86.5 2.1 copy-start.8
  100.0 2.2 %copy-start.9 = (f32[8192,128]{1,0:T(8,128)S(1)}, f32[8192,128]{1,0:T(8,128)}, u32[]{:S(2)}) copy-start(f32[8192,128]{1,0:T(8,128)} %copy-done.8) | copy-start | bytes 12582916
  136.2 35.8 %all-to-all-start.4 = ((f32[16,81,2,128]{3,2,1,0:T(2,128)}), f32[16,81,2,128]{3,2,1,0:T(2,128)S(1)}, u32[]{:S(2)}, u32[]{:S(2)}) async-start(f32[16,81,2,128]{3,2,1,0:T(2,128)} %bitcast.11), calls=%async_computation.4 | async-start | bytes 2654208 | tf_op jit(solution)/shard_map/all_to_all | solution.py:590
  172.0 35.8 %all-to-all-start.3 = ((f32[16,81,2,128]{3,2,1,0:T(2,128)}), f32[16,81,2,128]{3,2,1,0:T(2,128)S(1)}, u32[]{:S(2)}, u32[]{:S(2)}) async-start(f32[16,81,2,128]{3,2,1,0:T(2,128)} %bitcast.9), calls=%async_computation.3 | async-start | bytes 2654208 | tf_op jit(solution)/shard_map/all_to_all | solution.py:590
  176.9 2.0 copy-start.2
  207.8 2.0 copy-start.3

commit v4 on v3

--- a/solution.py
+++ b/solution.py
@@ -164,6 +164,7 @@
 BF16 = jnp.bfloat16
 MIB = 1024 * 1024
 GRID_VMEM = 44 * MIB
+WHOLE_VMEM = 60 * MIB
 CHUNKS = 2
 
 
@@ -202,7 +203,11 @@
         self.tiles = self.part // LANES
         self.data = self.depth * self.tiles
         self.force = 2 * points // (LANES * shares)
-        self.block = ceil_to(self.data + self.tiles + self.force, 8)
+        self.all_tiles = rows // LANES
+        self.blocks = (
+            ceil_to(self.data + self.all_tiles + self.force, 8), ceil_to(self.data, 8)
+        )
+        self.tall = ceil_to(self.depth + 1, 8)
         self.strip = strip_rows * cols
         self.grid_rows = strip_rows * shares
         self.coarse_rows = self.grid_rows // COARSE
@@ -217,7 +222,7 @@
         if 2 * self.points // LANES > LANES:
             return False
         cells = 2 * self.size + 2 * self.coarse_rows * self.cols + self.shares * self.part
-        held = LANES * 4 * (cells + self.shares * (self.block + self.data))
+        held = LANES * 4 * (cells + self.shares * (self.blocks[0] + self.data))
         return held + 4 * MIB < GRID_VMEM
 
 
@@ -250,8 +255,10 @@
     return both[0:1], both[1:2]
 
 
-def half_step(plan, load, wind, cp, table_ref, coup_ref, loc_ref, locb_ref, store):
+def half_step(plan, load, wind, cp, table_ref, coup_hbm, coup_ref, loc_ref, locb_ref, sem, store):
     spec, rows = plan.spec, plan.part
+    fetch = pltpu.make_async_copy(coup_hbm, coup_ref, sem)
+    fetch.start()
     east, north = cell_winds(wind, cp)
     step = largest_step(spec, 16, 64)
 
@@ -274,6 +281,7 @@
         loc_ref[at, :] = local
         locb_ref[at, :] = local.astype(BF16)
 
+    fetch.wait()
     tall = largest_step(spec, 16, 512)
     for q in range(spec // tall):
         at = slice(q * tall, (q + 1) * tall)
@@ -286,7 +294,8 @@
 
 def first_kernel(
     plan, chunk,
-    energy_ref, cp_ref, parcel_ref, names_ref, table_ref, coup_ref, out_ref, buf_ref, loc_ref, locb_ref,
+    energy_ref, cp_ref, parcel_ref, names_ref, table_ref, coup_hbm, out_ref,
+    buf_ref, coup_ref, loc_ref, locb_ref, sem,
 ):
     part, tiles, shares, points = plan.part, plan.tiles, plan.shares, plan.points
     lanes = slice(chunk * part, (chunk + 1) * part)
@@ -300,36 +309,42 @@
     wind = jnp.sum(parcel_ref[:, :, 0:points], axis=0)
     half_step(
         plan, lambda first, count: energy_ref[pl.ds(first, count), lanes],
-        wind, cp_ref[:, lanes], table_ref, coup_ref, loc_ref, locb_ref, store,
-    )
-
-    landing = jnp.concatenate(
-        [parcel_ref[b, 0:1, points : points + LANES] for b in range(shares)], axis=0
-    ).astype(jnp.int32)
-    cell = landing + plan.strip * lax.broadcasted_iota(jnp.int32, (shares, LANES), 0)
-    place = (cell + lax.div(cell, plan.cols) * (plan.pitch - plan.cols) + plan.pitch + 8).astype(F32)
-    own = lax.broadcasted_iota(jnp.int32, (part, LANES), 0) + chunk * part
-    found = jnp.zeros((part, LANES), F32)
-    for b in range(shares):
-        found += jnp.where(names_ref[b : b + 1, :] == own, place[b : b + 1, :], 0.0)
-    found = jnp.broadcast_to(jnp.sum(found, axis=1, keepdims=True), (part, LANES))
-    spare = [found[j * LANES : (j + 1) * LANES, :].T[0:1, :] for j in range(tiles)]
+        wind, cp_ref[:, lanes], table_ref, coup_hbm, coup_ref, loc_ref, locb_ref, sem, store,
+    )
+
+    block = plan.blocks[min(chunk, 1)]
+    spare = []
     if chunk == 0:
+        landing = jnp.concatenate(
+            [parcel_ref[b, 0:1, points : points + LANES] for b in range(shares)], axis=0
+        ).astype(jnp.int32)
+        cell = landing + plan.strip * lax.broadcasted_iota(jnp.int32, (shares, LANES), 0)
+        place = cell + lax.div(cell, plan.cols) * (plan.pitch - plan.cols) + plan.pitch + 8
+        place = place.astype(F32)
+        for j in range(plan.all_tiles):
+            own = lax.broadcasted_iota(jnp.int32, (LANES, LANES), 0) + j * LANES
+            found = jnp.zeros((LANES, LANES), F32)
+            for b in range(shares):
+                found += jnp.where(names_ref[b : b + 1, :] == own, place[b : b + 1, :], 0.0)
+            found = jnp.broadcast_to(jnp.sum(found, axis=1, keepdims=True), (LANES, LANES))
+            spare.append(found.T[0:1, :])
         width = plan.force * LANES
         current = jnp.sum(parcel_ref[:, :, points : points + width], axis=0)
         spare += [current[1:2, f * LANES : (f + 1) * LANES] for f in range(plan.force)]
-    spare.append(jnp.zeros((plan.block - plan.data - len(spare), LANES), F32))
-    spare = jnp.concatenate(spare, axis=0)
+    if block > plan.data + len(spare):
+        spare.append(jnp.zeros((block - plan.data - len(spare), LANES), F32))
     for d in range(shares):
-        out_ref[d * plan.block : (d + 1) * plan.block, :] = buf_ref[
-            d * plan.data : d * plan.data + plan.block, :
+        out_ref[d * block : d * block + plan.data, :] = buf_ref[
+            d * plan.data : (d + 1) * plan.data, :
         ]
-        out_ref[d * plan.block + plan.data : (d + 1) * plan.block, :] = spare
+        if spare:
+            out_ref[d * block + plan.data : (d + 1) * block, :] = jnp.concatenate(spare, axis=0)
 
 
 def last_kernel(
     plan, chunk,
-    came_ref, cp_ref, parcel_ref, table_ref, coup_ref, held_ref, out_ref, res_ref, loc_ref, locb_ref, sems,
+    came_ref, cp_ref, parcel_ref, table_ref, coup_hbm, held_ref, out_ref,
+    res_ref, sems, coup_ref, loc_ref, locb_ref, sem,
 ):
     part, tiles = plan.part, plan.tiles
     lanes = slice(chunk * part, (chunk + 1) * part)
@@ -350,7 +365,9 @@
         copies[-1].start()
 
     wind = jnp.sum(parcel_ref[:, :, 0 : plan.points], axis=0)
-    half_step(plan, load, wind, cp_ref[:, lanes], table_ref, coup_ref, loc_ref, locb_ref, store)
+    half_step(
+        plan, load, wind, cp_ref[:, lanes], table_ref, coup_hbm, coup_ref, loc_ref, locb_ref, sem, store
+    )
     for copy in copies:
         copy.wait()
 
@@ -366,66 +383,69 @@
         grid_ref[at, :] = jnp.zeros((LANES, LANES), F32)
 
 
-def turn_in(plan, came_ref, cell_ref, piece_ref):
-    depth, tiles = plan.depth, plan.tiles
+def turn_in(plan, block, came_ref, cell_ref, piece_ref):
+    depth, tiles, tall = plan.depth, plan.tiles, plan.tall
     flag = lax.broadcasted_iota(jnp.int32, (LANES, LANES), 0) == depth
     piece_ref[...] = jnp.where(flag, 1.0, 0.0)
 
     @pl.loop(0, plan.shares)
     def _(s):
         for j in range(tiles):
-            piece_ref[0:depth, :] = came_ref[pl.ds(s * plan.block + j, depth, stride=tiles), :]
+            piece_ref[0:depth, :] = came_ref[pl.ds(s * block + j, depth, stride=tiles), :]
             at = pl.ds(pl.multiple_of((s * tiles + j) * LANES, LANES), LANES)
-            cell_ref[at, :] = piece_ref[...].T
+            cell_ref[at, 0:tall] = piece_ref[0:tall, :].T
 
 
 def turn_out(plan, cell_ref, out_ref):
-    depth, tiles = plan.depth, plan.tiles
+    depth, tiles, tall = plan.depth, plan.tiles, plan.tall
 
     @pl.loop(0, plan.shares)
     def _(s):
         for j in range(tiles):
             at = pl.ds(pl.multiple_of((s * tiles + j) * LANES, LANES), LANES)
-            turned = cell_ref[at, :].T
+            turned = cell_ref[at, 0:tall].T
             out_ref[pl.ds(s * plan.data + j, depth, stride=tiles), :] = turned[0:depth, :]
 
 
-def places(plan, came_ref, spot_ref):
-    for s in range(plan.shares):
-        first = s * plan.block + plan.data
-        spot_ref[s * plan.tiles : (s + 1) * plan.tiles, :] = came_ref[
-            first : first + plan.tiles, :
-        ].astype(jnp.int32)
-
-
-def each_row(plan, spot_ref, body, unroll=32):
-    per = LANES // unroll
-
-    @pl.loop(0, plan.shares * plan.tiles * per)
+def row_groups(plan, chunk, place_ref, body, groups=4):
+    per = plan.part // (8 * groups)
+
+    @pl.loop(0, plan.shares * per)
     def _(i):
-        block, first = i // per, (i % per) * unroll
-        for t in range(unroll):
-            body(i * unroll + t, spot_ref[block, first + t])
-
-
-def scatter(plan, spot_ref, cell_ref, grid_ref):
-    def body(row, place):
-        grid_ref[pl.ds(place, 1), :] = cell_ref[pl.ds(row, 1), :]
-
-    each_row(plan, spot_ref, body)
-
-
-def gather(plan, spot_ref, cell_ref, grid_ref):
-    def body(row, place):
-        cell_ref[pl.ds(row, 1), :] = grid_ref[pl.ds(place, 1), :]
-
-    each_row(plan, spot_ref, body)
+        first = (i // per) * plan.rows + chunk * plan.part + (i % per) * (8 * groups)
+        for g in range(groups):
+            at = pl.ds(pl.multiple_of((i * groups + g) * 8, 8), 8)
+            body(at, [place_ref[first + g * 8 + t] for t in range(8)])
+
+
+def scatter(plan, chunk, place_ref, cell_ref, grid_ref):
+    sub = lax.broadcasted_iota(jnp.int32, (8, LANES), 0)
+
+    def body(at, spots):
+        values = cell_ref[at, :]
+        for t, spot in enumerate(spots):
+            pltpu.store(grid_ref.at[pl.ds(spot - t, 8), :], values, mask=sub == t)
+
+    row_groups(plan, chunk, place_ref, body)
+
+
+def gather(plan, chunk, place_ref, cell_ref, grid_ref):
+    sub = lax.broadcasted_iota(jnp.int32, (8, LANES), 0)
+
+    def body(at, spots):
+        values = grid_ref[pl.ds(spots[0], 8), :]
+        for t, spot in enumerate(spots):
+            if t:
+                values = jnp.where(sub == t, grid_ref[pl.ds(spot - t, 8), :], values)
+        cell_ref[at, :] = values
+
+    row_groups(plan, chunk, place_ref, body)
 
 
 def spread_drift(plan, came_ref, piece_ref, drift_ref):
     piece_ref[...] = jnp.zeros((LANES, LANES), F32)
     for s in range(plan.shares):
-        first = s * plan.block + plan.data + plan.tiles
+        first = s * plan.blocks[0] + plan.data + plan.all_tiles
         piece_ref[s * plan.force : (s + 1) * plan.force, :] = came_ref[
             first : first + plan.force, :
         ]
@@ -436,82 +456,72 @@
             drift_ref[pl.ds(q * LANES * COARSE + t, LANES, stride=COARSE), :] = wide
 
 
-def sweep_columns(plan, drift_ref, speed_ref, one_ref, two_ref):
-    cols, pitch, flag = plan.cols, plan.pitch, plan.depth
-
-    @pl.loop(0, plan.coarse_rows)
-    def _(r4):
-        courant = speed_ref[0:1, :] + drift_ref[pl.ds(pl.multiple_of(r4 * cols, cols), cols), :]
-        for dr in range(COARSE):
-            base = pl.multiple_of((r4 * COARSE + dr + 1) * pitch + 8, 8)
-            center = one_ref[pl.ds(base, cols), :]
-            before = one_ref[pl.ds(base - 1, cols), :]
-            after = one_ref[pl.ds(base + 1, cols), :]
+def sweep(plan, drift_ref, speed_ref, one_ref, two_ref, wide=32):
+    cols, pitch, flag, last = plan.cols, plan.pitch, plan.depth, plan.coarse_rows - 1
+
+    for start in range(0, cols, wide):
+
+        def courant(which, r4):
+            point = pl.multiple_of((which * plan.coarse_rows + r4) * cols + start, 8)
+            return speed_ref[which : which + 1, :] + drift_ref[pl.ds(point, wide), :]
+
+        def at(row):
+            return pl.multiple_of((row + 1) * pitch + 8 + start, 8)
+
+        def along(row, speed):
+            base = at(row)
+            center = one_ref[pl.ds(base, wide), :]
+            before = one_ref[pl.ds(base - 1, wide), :]
+            after = one_ref[pl.ds(base + 1, wide), :]
             wet = jnp.broadcast_to(center[:, flag : flag + 1], center.shape)
-            two_ref[pl.ds(base, cols), :] = upwind(center, before, after, courant) * wet
-
-
-def sweep_rows_in_vmem(plan, drift_ref, speed_ref, one_ref, two_ref):
-    cols, pitch = plan.cols, plan.pitch
-
-    @pl.loop(0, plan.coarse_rows)
-    def _(r4):
-        point = pl.multiple_of((plan.coarse_rows + r4) * cols, cols)
-        courant = speed_ref[1:2, :] + drift_ref[pl.ds(point, cols), :]
-        for dr in range(COARSE):
-            base = pl.multiple_of((r4 * COARSE + dr + 1) * pitch + 8, 8)
-            above = pl.multiple_of(base - pitch, 8)
-            below = pl.multiple_of(base + pitch, 8)
-            one_ref[pl.ds(base, cols), :] = upwind(
-                two_ref[pl.ds(base, cols), :],
-                two_ref[pl.ds(above, cols), :],
-                two_ref[pl.ds(below, cols), :],
-                courant,
-            )
-
-
-def land_kernel(plan, came_ref, grid_ref, drift_ref, spot_ref, cell_ref, piece_ref, smem_ref, sem):
-    places(plan, came_ref, spot_ref)
-    copy = pltpu.make_async_copy(spot_ref, smem_ref, sem)
-    copy.start()
+            return upwind(center, before, after, speed) * wet
+
+        def coarse(r4, held):
+            above, here = held
+            east, north = courant(0, r4), courant(1, r4)
+            later = courant(0, jnp.minimum(r4 + 1, last))
+            for dr in range(COARSE):
+                row = r4 * COARSE + dr
+                below = along(row + 1, east if dr < COARSE - 1 else later)
+                two_ref[pl.ds(at(row), wide), :] = upwind(here, above, below, north)
+                above, here = here, below
+            return above, here
+
+        lax.fori_loop(
+            0, plan.coarse_rows, coarse, (jnp.zeros((wide, LANES), F32), along(0, courant(0, 0)))
+        )
+
+
+def land_kernel(plan, place_ref, came_ref, grid_ref, drift_ref, cell_ref, piece_ref):
     clear(plan, grid_ref)
     spread_drift(plan, came_ref, piece_ref, drift_ref)
-    turn_in(plan, came_ref, cell_ref, piece_ref)
-    copy.wait()
-    scatter(plan, smem_ref, cell_ref, grid_ref)
+    turn_in(plan, plan.blocks[0], came_ref, cell_ref, piece_ref)
+    scatter(plan, 0, place_ref, cell_ref, grid_ref)
 
 
 def sweep_kernel(
     plan,
-    came_ref, spot0_ref, speed_ref, grid_ref, drift_ref,
-    out_ref, swept_ref, spot_ref,
-    cell_ref, one_ref, two_ref, wide_ref, piece_ref, smem_ref, sems,
+    place_ref, came_ref, speed_ref, grid_ref, drift_ref, out_ref, swept_ref,
+    cell_ref, one_ref, two_ref, wide_ref, piece_ref, sems,
 ):
     get_grid = pltpu.make_async_copy(grid_ref, one_ref, sems.at[0])
     get_drift = pltpu.make_async_copy(drift_ref, wide_ref, sems.at[1])
     get_grid.start()
     get_drift.start()
-    places(plan, came_ref, spot_ref)
-    get_spot = pltpu.make_async_copy(spot_ref, smem_ref, sems.at[2])
-    get_spot.start()
-    for edge in (0, plan.grid_rows + 1):
-        two_ref[edge * plan.pitch : (edge + 1) * plan.pitch, :] = jnp.zeros((plan.pitch, LANES), F32)
-    turn_in(plan, came_ref, cell_ref, piece_ref)
-    get_spot.wait()
+    turn_in(plan, plan.blocks[1], came_ref, cell_ref, piece_ref)
     get_grid.wait()
-    scatter(plan, smem_ref, cell_ref, one_ref)
+    scatter(plan, 1, place_ref, cell_ref, one_ref)
     get_drift.wait()
-    sweep_columns(plan, wide_ref, speed_ref, one_ref, two_ref)
-    sweep_rows_in_vmem(plan, wide_ref, speed_ref, one_ref, two_ref)
-    put_grid = pltpu.make_async_copy(one_ref, swept_ref, sems.at[0])
+    sweep(plan, wide_ref, speed_ref, one_ref, two_ref)
+    put_grid = pltpu.make_async_copy(two_ref, swept_ref, sems.at[2])
     put_grid.start()
-    gather(plan, spot0_ref, cell_ref, one_ref)
+    gather(plan, 0, place_ref, cell_ref, two_ref)
     turn_out(plan, cell_ref, out_ref)
     put_grid.wait()
 
 
-def take_kernel(plan, spot_ref, grid_ref, out_ref, cell_ref):
-    gather(plan, spot_ref, cell_ref, grid_ref)
+def take_kernel(plan, place_ref, grid_ref, out_ref, cell_ref):
+    gather(plan, 1, place_ref, cell_ref, grid_ref)
     turn_out(plan, cell_ref, out_ref)
 
 
@@ -537,7 +547,7 @@
     part, tiles, size = plan.part, plan.tiles, plan.size
     source, east_speed, north_speed = wave_tables()
     table = jnp.asarray(source)
-    block_rows, data_rows = shares * plan.block, shares * plan.data
+    data_rows = shares * plan.data
     drift_rows = 2 * plan.coarse_rows * plan.cols
 
     def kernel(body, *, vmem, flops, traffic, **options):
@@ -551,7 +561,7 @@
     width = points + max(LANES, plan.force * LANES)
     parcel = kernel(
         functools.partial(pack_kernel, plan),
-        vmem=8 * MIB, flops=0, traffic=4 * shares * 2 * width,
+        vmem=WHOLE_VMEM, flops=0, traffic=4 * shares * 2 * width,
         out_shape=jax.ShapeDtypeStruct((shares, 2, width), F32),
         in_specs=[SMEM, VMEM, VMEM, VMEM],
         out_specs=VMEM,
@@ -570,20 +580,26 @@
     cp = cell_point.reshape(1, rows)
     coup = coupling.T
     h_flops, h_traffic = 2 * part * spec * spec, 8 * part * spec
-    h_scratch = [pltpu.VMEM((spec, part), F32), pltpu.VMEM((spec, part), BF16)]
+    h_scratch = [
+        pltpu.VMEM((spec, spec), BF16),
+        pltpu.VMEM((spec, part), F32),
+        pltpu.VMEM((spec, part), BF16),
+        pltpu.SemaphoreType.DMA,
+    ]
 
     def first(chunk):
+        rows_sent = plan.blocks[min(chunk, 1)]
         block = kernel(
             functools.partial(first_kernel, plan, chunk),
-            vmem=28 * MIB, flops=h_flops, traffic=h_traffic,
-            out_shape=jax.ShapeDtypeStruct((block_rows, LANES), F32),
-            in_specs=[VMEM] * 6,
+            vmem=WHOLE_VMEM, flops=h_flops, traffic=h_traffic,
+            out_shape=jax.ShapeDtypeStruct((shares * rows_sent, LANES), F32),
+            in_specs=[VMEM] * 5 + [ANY],
             out_specs=VMEM,
-            scratch_shapes=[pltpu.VMEM((data_rows + plan.block, LANES), F32)] + h_scratch,
+            scratch_shapes=[pltpu.VMEM((data_rows, LANES), F32)] + h_scratch,
             name=f"first_half_{chunk}",
         )(energy, cp, parcel, names, table, coup)
-        block = block.reshape(shares, plan.block, LANES)
-        return lax.all_to_all(block, "space", 0, 0, tiled=True).reshape(block_rows, LANES)
+        block = block.reshape(shares, rows_sent, LANES)
+        return lax.all_to_all(block, "space", 0, 0, tiled=True).reshape(-1, LANES)
 
     def home(block):
         block = block.reshape(shares, plan.depth, tiles, LANES)
@@ -592,58 +608,57 @@
     cells = pltpu.VMEM((shares * part, LANES), F32)
     piece = pltpu.VMEM((LANES, LANES), F32)
     grid_shape = jax.ShapeDtypeStruct((size, LANES), F32)
-    spot_shape = jax.ShapeDtypeStruct((shares * tiles, LANES), jnp.int32)
-    smem = pltpu.SMEM((shares * tiles, LANES), jnp.int32)
     block_shape = jax.ShapeDtypeStruct((data_rows, LANES), F32)
 
     came = [first(chunk) for chunk in range(CHUNKS)]
-    grid, drift, spot0 = kernel(
+    place = came[0].reshape(shares, plan.blocks[0], LANES)[:, plan.data : plan.data + plan.all_tiles]
+    place = place.astype(jnp.int32).reshape(-1)
+    grid, drift = kernel(
         functools.partial(land_kernel, plan),
-        vmem=GRID_VMEM, flops=0, traffic=8 * size * LANES,
-        out_shape=[grid_shape, jax.ShapeDtypeStruct((drift_rows, LANES), F32), spot_shape],
-        in_specs=[VMEM],
-        out_specs=[VMEM, VMEM, VMEM],
-        scratch_shapes=[cells, piece, smem, pltpu.SemaphoreType.DMA],
+        vmem=WHOLE_VMEM, flops=0, traffic=8 * size * LANES,
+        out_shape=[grid_shape, jax.ShapeDtypeStruct((drift_rows, LANES), F32)],
+        in_specs=[SMEM, VMEM],
+        out_specs=[VMEM, VMEM],
+        scratch_shapes=[cells, piece],
         name="land",
-    )(came[0])
-    out0, swept, spot1 = kernel(
+    )(place, came[0])
+    out0, swept = kernel(
         functools.partial(sweep_kernel, plan),
-        vmem=GRID_VMEM, flops=20 * size * LANES, traffic=16 * size * LANES,
-        out_shape=[block_shape, grid_shape, spot_shape],
-        in_specs=[VMEM, SMEM, VMEM, ANY, ANY],
-        out_specs=[VMEM, ANY, VMEM],
+        vmem=WHOLE_VMEM, flops=20 * size * LANES, traffic=16 * size * LANES,
+        out_shape=[block_shape, grid_shape],
+        in_specs=[SMEM, VMEM, VMEM, ANY, ANY],
+        out_specs=[VMEM, ANY],
         scratch_shapes=[
             cells,
             pltpu.VMEM((size, LANES), F32),
             pltpu.VMEM((size, LANES), F32),
             pltpu.VMEM((drift_rows, LANES), F32),
             piece,
-            smem,
             pltpu.SemaphoreType.DMA((3,)),
         ],
         name="sweeps",
-    )(came[1], spot0, speed, grid, drift)
+    )(place, came[1], speed, grid, drift)
     back0 = home(out0)
     out1 = kernel(
         functools.partial(take_kernel, plan),
-        vmem=GRID_VMEM, flops=0, traffic=8 * size * LANES,
+        vmem=WHOLE_VMEM, flops=0, traffic=8 * size * LANES,
         out_shape=block_shape,
         in_specs=[SMEM, VMEM],
         out_specs=VMEM,
         scratch_shapes=[cells],
         name="take",
-    )(spot1, swept)
+    )(place, swept)
     back1 = home(out1)
 
     result = jnp.zeros((8, LANES), F32)
     for chunk, back in enumerate((back0, back1)):
         result = kernel(
             functools.partial(last_kernel, plan, chunk),
-            vmem=28 * MIB, flops=h_flops, traffic=h_traffic,
+            vmem=WHOLE_VMEM, flops=h_flops, traffic=h_traffic,
             out_shape=jax.ShapeDtypeStruct((spec, rows), F32),
-            in_specs=[VMEM] * 5 + [ANY],
+            in_specs=[VMEM] * 4 + [ANY] * 2,
             out_specs=ANY,
-            scratch_shapes=[pltpu.VMEM((spec, part), F32)] + h_scratch + [pltpu.SemaphoreType.DMA((8,))],
+            scratch_shapes=[pltpu.VMEM((spec, part), F32), pltpu.SemaphoreType.DMA((8,))] + h_scratch,
             input_output_aliases={5: 0} if chunk else {},
             name=f"last_half_{chunk}",
         )(back, cp, parcel, table, coup, result)

time: 216 us -> 209 us (0.968)
  local copies, waits for them, and re-layouts: 24.3 us -> 11.4 us
  waiting for transfers between devices: 73.7 us -> 84.1 us
  Pallas kernels: 89.9 us -> 84.6 us
    unnamed x35 -> x15, local copies, waits for them, and re-layouts: 23.5 us -> 8.86 us
    pallas_call x8, Pallas kernels: 89.9 us -> 84.6 us  [the longest x1 28.8 us: on_spectrum(): kernel(functools.partial(sweep_kernel, plan), vmem=WHOLE_VMEM, flops=20 *...]
    all_to_all x2, waiting for transfers between devices: 38.2 us -> 43.4 us  [home(): lax.all_to_all(block, 'space', 0, 0, tiled=True).reshape(data_rows, LANES)]
    all_to_all x2, waiting for transfers between devices: 35.5 us -> 40.6 us  [first(): return lax.all_to_all(block, 'space', 0, 0, tiled=True).reshape(-1, LANES)]
  transfers between devices with their start and end apart: 5 -> 5, of which waited for: 4 -> 4; matrix products, arithmetic and copies ran while one was open for 3% -> 4% of each run, Pallas kernels for 21% -> 19%
where the time goes in v4:
time: 209 us; the launch traced here: 208 us
  Pallas kernels  84.6 us (40%)
  waiting for transfers between devices  84.1 us (40%)
  starting transfers between devices  27.2 us (13%)
  local copies, waits for them, and re-layouts  11.4 us (5%)
    all_to_all x2, waiting for transfers between devices, home(): lax.all_to_all(block, 'space', 0, 0, tiled=True).reshape(data_rows, LANES)  43.4 us
    all_to_all x2, waiting for transfers between devices, first(): return lax.all_to_all(block, 'space', 0, 0, tiled=True).reshape(-1, LANES)  40.6 us
    pallas_call x1, Pallas kernels, on_spectrum(): kernel(functools.partial(sweep_kernel, plan), vmem=WHOLE_VMEM, flops=20 *...  28.8 us
    pallas_call x2, Pallas kernels, first(): kernel(functools.partial(first_kernel, plan, chunk), vmem=WHOLE_VMEM, flo...  16 us
    pallas_call x2, Pallas kernels, on_spectrum(): kernel(functools.partial(last_kernel, plan, chunk), vmem=WHOLE_VMEM, flop...  14.1 us
    pallas_call x1, Pallas kernels, on_spectrum(): kernel(functools.partial(land_kernel, plan), vmem=WHOLE_VMEM, flops=0, tr...  13.4 us
    all_to_all x2, starting transfers between devices, first(): return lax.all_to_all(block, 'space', 0, 0, tiled=True).reshape(-1, LANES)  10.9 us
    pallas_call x1, Pallas kernels, on_spectrum(): kernel(functools.partial(take_kernel, plan), vmem=WHOLE_VMEM, flops=0, tr...  10.7 us
  transfers between devices with their start and end apart: 5, of which 4 were waited for; matrix products, arithmetic and copies ran while one was open for 4% of the time, Pallas kernels for 19%

profile of v4, /device:TPU:15, one launch (start us, length us, event | category | flops | bytes accessed | tf_op | source)
XLA Modules:
  0.0 208.0 jit_solution(13790871414275408794)
XLA Ops:
  0.0 1.5 pack.1
  1.5 6.6 %all-to-all-start = ((f32[16,2,1152]{2,1,0:T(2,128)}), f32[16,2,1152]{2,1,0:T(2,128)S(1)}, u32[]{:S(2)}, u32[]{:S(2)}) async-start(f32[16,2,1152]{2,1,0:T(2,128)} %pack.1), calls=%async_computation | async-start | bytes 294912 | tf_op jit(solution)/shard_map/all_to_all | solution.py:570
  8.0 0.0 copy-start.5
  8.0 0.0 copy-start.6
  8.1 6.0 %copy.14 = bf16[1296,1296]{0,1:T(8,128)(2,1)} copy(bf16[1296,1296]{1,0:T(8,128)(2,1)} %param.18) | data formatting | bytes 6718464 | tf_op args[5]
  14.1 0.0 copy-done.5
  14.1 0.0 copy-done.6
  14.1 0.1 bitcast_select_fusion
  14.2 0.6 pad.8.names_ref
  14.8 0.0 all-to-all-done.parcel_ref
  14.8 0.0 copy-start.4
  14.8 0.7 copy-done.4
  15.4 8.1 %first_half_0.1 = f32[2688,128]{1,0:T(8,128)} custom-call(f32[1296,512]{1,0:T(8,128)} %bitcast.20, s32[1,512]{1,0:T(1,128)} %bitcast.33, f32[16,2,1152]{2,1,0:T(2,128)} %copy-done.4, s32[16,128]{1,0:T(8,128)} %pad.8.names_ref, f32[1296,8]{1,0:T(8,128)} %constant.21.clone.table_ref, bf16[1296,1296]{1,0:T(8,128)(2,1)} %bitcast.16), custom_call_target="tpu_custom_call" | custom-call | flops 859963392 | bytes 2654208 | tf_op jit(solution)/shard_map/first_half_0/pallas_call | solution.py:592
  23.5 6.0 %all-to-all-start.1 = ((f32[16,168,128]{2,1,0:T(8,128)}), f32[16,168,128]{2,1,0:T(8,128)S(1)}, u32[]{:S(2)}, u32[]{:S(2)}) async-start(f32[16,168,128]{2,1,0:T(8,128)} %bitcast.24), calls=%async_computation.1 | async-start | bytes 2752512 | tf_op jit(solution)/shard_map/all_to_all | solution.py:602
  29.6 7.9 %first_half_1.1 = f32[2688,128]{1,0:T(8,128)} custom-call(f32[1296,512]{1,0:T(8,128)} %bitcast.21, s32[1,512]{1,0:T(1,128)} %bitcast.34, f32[16,2,1152]{2,1,0:T(2,128)} %copy-done.4, s32[16,128]{1,0:T(8,128)} %pad.8.names_ref, f32[1296,8]{1,0:T(8,128)} %constant.21.clone.table_ref, bf16[1296,1296]{1,0:T(8,128)(2,1)} %bitcast.17), custom_call_target="tpu_custom_call" | custom-call | flops 859963392 | bytes 2654208 | tf_op jit(solution)/shard_map/first_half_1/pallas_call | solution.py:592
  37.5 24.1 %all-to-all-done.1 = f32[16,168,128]{2,1,0:T(8,128)S(1)} async-done(((f32[16,168,128]{2,1,0:T(8,128)}), f32[16,168,128]{2,1,0:T(8,128)S(1)}, u32[]{:S(2)}, u32[]{:S(2)}) %all-to-all-start.1) | async-done | bytes 1376288 | tf_op jit(solution)/shard_map/all_to_all | solution.py:602
  61.5 0.0 copy-start
  61.6 4.9 %all-to-all-start.2 = ((f32[16,168,128]{2,1,0:T(8,128)}), f32[16,168,128]{2,1,0:T(8,128)S(1)}, u32[]{:S(2)}, u32[]{:S(2)}) async-start(f32[16,168,128]{2,1,0:T(8,128)} %bitcast.23), calls=%async_computation.2 | async-start | bytes 2752512 | tf_op jit(solution)/shard_map/all_to_all | solution.py:602
  66.4 1.4 constant_dynamic-slice_fusion.speed_ref
  67.8 0.0 copy-done
  67.8 0.6 slice_convert_fusion
  68.4 13.4 %land.1 = (f32[17792,128]{1,0:T(8,128)}, f32[8192,128]{1,0:T(8,128)}) custom-call(s32[8192]{0:T(1024)} %bitcast.30, f32[2688,128]{1,0:T(8,128)} %bitcast.22), custom_call_target="tpu_custom_call" | custom-call | bytes 18219008 | tf_op jit(solution)/shard_map/land/pallas_call | solution.py:616
  81.8 16.6 %all-to-all-done.2 = f32[16,168,128]{2,1,0:T(8,128)S(1)} async-done(((f32[16,168,128]{2,1,0:T(8,128)}), f32[16,168,128]{2,1,0:T(8,128)S(1)}, u32[]{:S(2)}, u32[]{:S(2)}) %all-to-all-start.2) | async-done | bytes 1376288 | tf_op jit(solution)/shard_map/all_to_all | solution.py:602
  98.4 0.0 copy-start.1
  98.4 1.1 copy-done.1
  99.5 28.8 %sweeps.1 = (f32[2592,128]{1,0:T(8,128)}, f32[17792,128]{1,0:T(8,128)}) custom-call(s32[8192]{0:T(1024)} %bitcast.31, f32[2688,128]{1,0:T(8,128)} %bitcast.25, f32[8,128]{1,0:T(8,128)} %constant_dynamic-slice_fusion.speed_ref, f32[17792,128]{1,0:T(8,128)} %get-tuple-element.9.grid_ref, f32[8192,128]{1,0:T(8,128)} %get-tuple-element.10.drift_ref), custom_call_target="tpu_custom_call" | custom-call | flops 45547520 | bytes 36438016 | tf_op jit(solution)/shard_map/sweeps/pallas_call | solution.py:625
  128.3 4.9 %all-to-all-start.4 = ((f32[16,81,2,128]{3,2,1,0:T(2,128)}), f32[16,81,2,128]{3,2,1,0:T(2,128)S(1)}, u32[]{:S(2)}, u32[]{:S(2)}) async-start(f32[16,81,2,128]{3,2,1,0:T(2,128)} %bitcast.29), calls=%async_computation.4 | async-start | bytes 2654208 | tf_op jit(solution)/shard_map/all_to_all | solution.py:606
  133.2 10.7 %take.1 = f32[2592,128]{1,0:T(8,128)} custom-call(s32[8192]{0:T(1024)} %bitcast.32, f32[17792,128]{1,0:T(8,128)} %get-tuple-element.11.grid_ref), custom_call_target="tpu_custom_call" | custom-call | bytes 18219008 | tf_op jit(solution)/shard_map/take/pallas_call | solution.py:642
  143.9 20.2 %all-to-all-done.4 = f32[16,81,2,128]{3,2,1,0:T(2,128)S(1)} async-done(((f32[16,81,2,128]{3,2,1,0:T(2,128)}), f32[16,81,2,128]{3,2,1,0:T(2,128)S(1)}, u32[]{:S(2)}, u32[]{:S(2)}) %all-to-all-start.4) | async-done | bytes 1327136 | tf_op jit(solution)/shard_map/all_to_all | solution.py:606
  164.1 0.0 copy-start.2
  164.1 4.9 %all-to-all-start.3 = ((f32[16,81,2,128]{3,2,1,0:T(2,128)}), f32[16,81,2,128]{3,2,1,0:T(2,128)S(1)}, u32[]{:S(2)}, u32[]{:S(2)}) async-start(f32[16,81,2,128]{3,2,1,0:T(2,128)} %bitcast.26), calls=%async_computation.3 | async-start | bytes 2654208 | tf_op jit(solution)/shard_map/all_to_all | solution.py:606
  169.0 0.6 broadcast_in_dim.9.held_ref
  169.6 0.0 copy-done.2
  169.6 7.1 %last_half_0.1.held_ref = f32[1296,512]{1,0:T(8,128)} custom-call(f32[2592,128]{1,0:T(8,128)} %bitcast.27, s32[1,512]{1,0:T(1,128)} %bitcast.35, f32[16,2,1152]{2,1,0:T(2,128)} %copy-done.4, f32[1296,8]{1,0:T(8,128)} %constant.21.clone.table_ref, bf16[1296,1296]{1,0:T(8,128)(2,1)} %bitcast.18, f32[8,128]{1,0:T(8,128)} %broadcast_in_dim.9.held_ref), custom_call_target="tpu_custom_call" | custom-call | flops 859963392 | bytes 2654208 | tf_op jit(solution)/shard_map/last_half_0/pallas_call | solution.py:655
  176.6 23.2 %all-to-all-done.3 = f32[16,81,2,128]{3,2,1,0:T(2,128)S(1)} async-done(((f32[16,81,2,128]{3,2,1,0:T(2,128)}), f32[16,81,2,128]{3,2,1,0:T(2,128)S(1)}, u32[]{:S(2)}, u32[]{:S(2)}) %all-to-all-start.3) | async-done | bytes 1327136 | tf_op jit(solution)/shard_map/all_to_all | solution.py:606
  199.9 0.0 copy-start.3
  199.9 1.1 copy-done.3
  201.0 7.1 %last_half_1.1 = f32[1296,512]{1,0:T(8,128)} custom-call(f32[2592,128]{1,0:T(8,128)} %bitcast.28, s32[1,512]{1,0:T(1,128)} %bitcast.36, f32[16,2,1152]{2,1,0:T(2,128)} %copy-done.4, f32[1296,8]{1,0:T(8,128)} %constant.21.clone.table_ref, bf16[1296,1296]{1,0:T(8,128)(2,1)} %bitcast.19, f32[1296,512]{1,0:T(8,128)} %last_half_0.1.held_ref), custom_call_target="tpu_custom_call", output_to_operand_aliasing={{}: (5, {})} | custom-call | flops 859963392 | bytes 2654208 | tf_op jit(solution)/shard_map/last_half_1/pallas_call | solution.py:655
Async XLA Ops:
  1.5 13.3 %all-to-all-start = ((f32[16,2,1152]{2,1,0:T(2,128)}), f32[16,2,1152]{2,1,0:T(2,128)S(1)}, u32[]{:S(2)}, u32[]{:S(2)}) async-start(f32[16,2,1152]{2,1,0:T(2,128)} %pack.1), calls=%async_computation | async-start | bytes 294912 | tf_op jit(solution)/shard_map/all_to_all | solution.py:570
  8.0 6.0 %copy-start.5 = (s32[1,16,64]{2,1,0:T(8,128)S(1)}, s32[1,16,64]{2,1,0:T(8,128)}, u32[]{:S(2)}) copy-start(s32[1,16,64]{2,1,0:T(8,128)} %param.19) | copy-start | bytes 12292
  8.0 6.0 %copy-start.6 = (s32[1,16]{1,0:T(1,128)S(1)}, s32[1,16]{1,0:T(1,128)}, u32[]{:S(2)}) copy-start(s32[1,16]{1,0:T(1,128)} %param.20) | copy-start | bytes 196
  14.8 0.7 copy-start.4
  23.5 38.0 %all-to-all-start.1 = ((f32[16,168,128]{2,1,0:T(8,128)}), f32[16,168,128]{2,1,0:T(8,128)S(1)}, u32[]{:S(2)}, u32[]{:S(2)}) async-start(f32[16,168,128]{2,1,0:T(8,128)} %bitcast.24), calls=%async_computation.1 | async-start | bytes 2752512 | tf_op jit(solution)/shard_map/all_to_all | solution.py:602
  61.5 6.2 %copy-start = (f32[16,168,128]{2,1,0:T(8,128)}, f32[16,168,128]{2,1,0:T(8,128)S(1)}, u32[]{:S(2)}) copy-start(f32[16,168,128]{2,1,0:T(8,128)S(1)} %all-to-all-done.1) | copy-start | bytes 4128772
  61.6 36.8 %all-to-all-start.2 = ((f32[16,168,128]{2,1,0:T(8,128)}), f32[16,168,128]{2,1,0:T(8,128)S(1)}, u32[]{:S(2)}, u32[]{:S(2)}) async-start(f32[16,168,128]{2,1,0:T(8,128)} %bitcast.23), calls=%async_computation.2 | async-start | bytes 2752512 | tf_op jit(solution)/shard_map/all_to_all | solution.py:602
  98.4 1.1 copy-start.1
  128.3 35.8 %all-to-all-start.4 = ((f32[16,81,2,128]{3,2,1,0:T(2,128)}), f32[16,81,2,128]{3,2,1,0:T(2,128)S(1)}, u32[]{:S(2)}, u32[]{:S(2)}) async-start(f32[16,81,2,128]{3,2,1,0:T(2,128)} %bitcast.29), calls=%async_computation.4 | async-start | bytes 2654208 | tf_op jit(solution)/shard_map/all_to_all | solution.py:606
  164.1 5.5 %copy-start.2 = (f32[16,81,2,128]{3,2,1,0:T(2,128)}, f32[16,81,2,128]{3,2,1,0:T(2,128)S(1)}, u32[]{:S(2)}) copy-start(f32[16,81,2,128]{3,2,1,0:T(2,128)S(1)} %all-to-all-done.4) | copy-start | bytes 3981316
  164.1 35.8 %all-to-all-start.3 = ((f32[16,81,2,128]{3,2,1,0:T(2,128)}), f32[16,81,2,128]{3,2,1,0:T(2,128)S(1)}, u32[]{:S(2)}, u32[]{:S(2)}) async-start(f32[16,81,2,128]{3,2,1,0:T(2,128)} %bitcast.26), calls=%async_computation.3 | async-start | bytes 2654208 | tf_op jit(solution)/shard_map/all_to_all | solution.py:606
  199.9 1.1 copy-start.3

commit v5 on v0

--- a/solution.py
+++ b/solution.py
@@ -1,8 +1,12 @@
+import functools
 import math
 
 import jax
 import jax.numpy as jnp
+import numpy as np
 from jax import lax
+from jax.experimental import pallas as pl
+from jax.experimental.pallas import tpu as pltpu
 from jax.sharding import PartitionSpec as P
 
 DIRS = 36
@@ -94,7 +98,7 @@
     return rows_idx[:, None] // COARSE * (col_count // COARSE) + cols_idx[None, :] // COARSE
 
 
-def on_device(
+def on_strips(
     spectra,
     wind_files,
     current_files,
@@ -155,6 +159,553 @@
     return result
 
 
+LANES = 128
+SUBS = 8
+F32 = jnp.float32
+BF16 = jnp.bfloat16
+MIB = 1024 * 1024
+WHOLE_VMEM = 60 * MIB
+DRY = 1e30
+PARTS = 4
+
+
+def wave_tables():
+    direction = 2.0 * np.pi / DIRS * np.arange(DIRS)
+    frequency = base_freq * freq_ratio ** (np.arange(FREQS) * (freq_span / (FREQS - 1)))
+    angular = 2.0 * np.pi * frequency
+    phase = gravity / angular
+    group = 0.5 * phase
+    cos_dir, sin_dir = np.cos(direction)[:, None], np.sin(direction)[:, None]
+    flat = lambda t: np.broadcast_to(t, (DIRS, FREQS)).reshape(-1)
+    source = np.zeros((DIRS * FREQS, 8), np.float32)
+    source[:, 0] = flat(wind_gain * cos_dir / phase)
+    source[:, 1] = flat(wind_gain * sin_dir / phase)
+    source[:, 2] = flat(half_length * input_coef * angular)
+    source[:, 3] = flat(half_length * dissip_coef * angular)
+    east = flat(courant_scale * cos_dir * group).astype(np.float32)
+    north = flat(courant_scale * sin_dir * group).astype(np.float32)
+    return source, east, north
+
+
+def ceil_to(value, step):
+    return -(-value // step) * step
+
+
+def largest_step(size, step, most):
+    return max(s for s in range(step, most + 1, step) if size % s == 0)
+
+
+class Plan:
+    def __init__(self, shares, rows, spec, cap, strip_rows, cols, points):
+        self.shares, self.rows, self.spec, self.cap = shares, rows, spec, cap
+        self.cols, self.points = cols, points
+        self.depth = spec // shares
+        self.tiles = rows // LANES
+        self.data = self.depth * self.tiles
+        self.force = 2 * points // (LANES * shares)
+        self.block = ceil_to(self.data + self.tiles + self.force, SUBS)
+        self.tall = ceil_to(self.depth, SUBS)
+        self.strip = strip_rows * cols
+        self.grid_rows = strip_rows * shares
+        self.coarse_rows = self.grid_rows // COARSE
+        self.vregs = cols // SUBS
+        self.size = (self.grid_rows + 2) * cols
+
+    def fits(self):
+        if self.spec % self.shares or self.depth > LANES or self.rows % (2 * LANES):
+            return False
+        if 2 * self.points % (LANES * self.shares) or self.points % LANES or self.cap > LANES:
+            return False
+        if 2 * self.points // LANES > LANES or self.cols != LANES or self.shares % PARTS:
+            return False
+        held = 2 * self.size + 2 * self.points + self.shares * (self.block + self.data)
+        return 4 * LANES * held + 4 * MIB < 32 * MIB
+
+
+def pack_kernel(plan, turn_ref, wind_ref, current_ref, recv_ref, out_ref):
+    me = lax.axis_index("space")
+    half = lambda at: jnp.where(turn_ref[at] == me, 0.5, 0.0)
+    mine = half(0) + half(1)
+    wind = mine * wind_ref[0]
+    points, width, cap = plan.points, plan.force * LANES, plan.cap
+    for s in range(plan.shares):
+        out_ref[s, :, 0:points] = wind
+        out_ref[s, :, points:] = jnp.zeros((2, out_ref.shape[2] - points), F32)
+        out_ref[s, 0:1, points : points + cap] = recv_ref[0, s : s + 1, :].astype(F32)
+        which, first = divmod(s * width, points)
+        out_ref[s, 1:2, points : points + width] = (
+            mine * current_ref[0, which : which + 1, first : first + width]
+        )
+
+
+def cell_winds(wind, cp):
+    points, rows = wind.shape[1], cp.shape[1]
+    high = wind.astype(BF16).astype(F32)
+    middle = (wind - high).astype(BF16).astype(F32)
+    low = wind - high - middle
+    parts = jnp.concatenate([high, middle, low, jnp.zeros((10, points), F32)], axis=0)
+    point = lax.broadcasted_iota(jnp.int32, (points, rows), 0)
+    hit = jnp.where(point == cp, 1.0, 0.0).astype(BF16)
+    picked = jnp.dot(parts.astype(BF16), hit, preferred_element_type=F32)
+    both = picked[0:2] + picked[2:4] + picked[4:6]
+    return both[0:1], both[1:2]
+
+
+def half_step(
+    plan, energy_hbm, energy_ref, load, parcel_ref, cp_ref, table_ref, coup_hbm, coup_ref,
+    loc_ref, locb_ref, sems, store,
+):
+    spec, rows = plan.spec, plan.rows
+    tall = largest_step(spec, 16, 512)
+    thirds = spec // tall
+    tall_rows = energy_ref.shape[0] // thirds
+    arrive = [
+        pltpu.make_async_copy(
+            energy_hbm.at[pl.ds(q * tall_rows, tall_rows), :],
+            energy_ref.at[pl.ds(q * tall_rows, tall_rows), :],
+            sems.at[q],
+        )
+        for q in range(thirds)
+    ]
+    fetch = pltpu.make_async_copy(coup_hbm, coup_ref, sems.at[thirds])
+    for copy in arrive:
+        copy.start()
+    fetch.start()
+    east, north = cell_winds(jnp.sum(parcel_ref[:, :, 0 : plan.points], axis=0), cp_ref[...])
+    step = largest_step(tall, 16, 64)
+
+    def squares(i, total):
+        piece = load(pl.multiple_of(i * step, step), step)
+        return total + jnp.sum((piece * piece).reshape(step // SUBS, SUBS, rows), axis=0)
+
+    total = jnp.zeros((SUBS, rows), F32)
+    for q in range(thirds):
+        arrive[q].wait()
+        total = lax.fori_loop(q * tall // step, (q + 1) * tall // step, squares, total)
+    mean_square = jnp.sum(total, axis=0, keepdims=True) * (1.0 / spec)
+
+    @pl.loop(0, spec // step)
+    def _(i):
+        first = pl.multiple_of(i * step, step)
+        at = pl.ds(first, step)
+        table = table_ref[at, :]
+        along = east * table[:, 0:1] + north * table[:, 1:2]
+        gain = 1.0 + table[:, 2:3] * jnp.maximum(along - 1.0, 0.0)
+        loss = 1.0 + table[:, 3:4] * mean_square
+        local = load(first, step) * gain / loss
+        loc_ref[at, :] = local
+        locb_ref[at, :] = local.astype(BF16)
+
+    fetch.wait()
+    for q in range(thirds):
+        at = slice(q * tall, (q + 1) * tall)
+        store(
+            q * tall,
+            loc_ref[at, :]
+            + jnp.dot(coup_ref[at, :], locb_ref[...], preferred_element_type=F32),
+        )
+
+
+def own_places(plan, parcel_ref, names_ref):
+    points, cols, vregs = plan.points, plan.cols, plan.vregs
+    landing = jnp.concatenate(
+        [parcel_ref[b, 0:1, points : points + LANES] for b in range(plan.shares)], axis=0
+    ).astype(jnp.int32)
+    cell = landing + plan.strip * lax.broadcasted_iota(jnp.int32, (plan.shares, LANES), 0)
+    column = lax.rem(cell, cols)
+    place = cell - column + cols + lax.rem(column, vregs) * SUBS + lax.div(column, vregs)
+    place = place.astype(F32)
+    rows = []
+    for j in range(plan.tiles):
+        own = lax.broadcasted_iota(jnp.int32, (LANES, LANES), 0) + j * LANES
+        found = jnp.zeros((LANES, LANES), F32)
+        for b in range(plan.shares):
+            found += jnp.where(names_ref[b : b + 1, :] == own, place[b : b + 1, :], 0.0)
+        found = jnp.broadcast_to(jnp.sum(found, axis=1, keepdims=True), (LANES, LANES))
+        rows.append(found.T[0:1, :])
+    return rows
+
+
+def first_kernel(
+    plan,
+    cp_ref, parcel_ref, names_ref, table_ref, energy_hbm, coup_hbm, out_hbm,
+    out_ref, buf_ref, out_sems, energy_ref, coup_ref, loc_ref, locb_ref, sems,
+):
+    tiles, shares, points, block, data = plan.tiles, plan.shares, plan.points, plan.block, plan.data
+    width = plan.force * LANES
+    current = jnp.sum(parcel_ref[:, :, points : points + width], axis=0)
+    spare = own_places(plan, parcel_ref, names_ref)
+    spare += [current[1:2, f * LANES : (f + 1) * LANES] for f in range(plan.force)]
+    if block > data + len(spare):
+        spare.append(jnp.zeros((block - data - len(spare), LANES), F32))
+    for d in range(shares):
+        out_ref[d * block + data : (d + 1) * block, :] = jnp.concatenate(spare, axis=0)
+    sent, copies = [0], []
+
+    def store(first, values):
+        for j in range(tiles):
+            buf_ref[pl.ds(first * tiles + j, values.shape[0], stride=tiles), :] = values[
+                :, j * LANES : (j + 1) * LANES
+            ]
+        upto = (first + values.shape[0]) // plan.depth
+        for d in range(sent[0], upto):
+            out_ref[d * block : d * block + data, :] = buf_ref[d * data : (d + 1) * data, :]
+        at = slice(sent[0] * block, upto * block)
+        copies.append(
+            pltpu.make_async_copy(out_ref.at[at, :], out_hbm.at[at, :], out_sems.at[len(copies)])
+        )
+        copies[-1].start()
+        sent[0] = upto
+
+    half_step(
+        plan, energy_hbm, energy_ref, lambda first, count: energy_ref[pl.ds(first, count), :],
+        parcel_ref, cp_ref, table_ref, coup_hbm, coup_ref, loc_ref, locb_ref, sems, store,
+    )
+    for copy in copies:
+        copy.wait()
+
+
+def last_kernel(
+    plan,
+    cp_ref, parcel_ref, table_ref, came_hbm, coup_hbm, out_hbm,
+    res_ref, out_sems, came_ref, coup_ref, loc_ref, locb_ref, sems,
+):
+    tiles = plan.tiles
+    copies = []
+
+    def load(first, count):
+        start = pl.multiple_of(first * tiles, SUBS)
+        return jnp.concatenate(
+            [came_ref[pl.ds(start + j, count, stride=tiles), :] for j in range(tiles)], axis=1
+        )
+
+    def store(first, values):
+        at = slice(first, first + values.shape[0])
+        res_ref[at, :] = values
+        copies.append(
+            pltpu.make_async_copy(res_ref.at[at, :], out_hbm.at[at, :], out_sems.at[len(copies)])
+        )
+        copies[-1].start()
+
+    half_step(
+        plan, came_hbm, came_ref, load,
+        parcel_ref, cp_ref, table_ref, coup_hbm, coup_ref, loc_ref, locb_ref, sems, store,
+    )
+    for copy in copies:
+        copy.wait()
+
+
+def scatter(plan, place_ref, came_ref, grid_ref, piece_refs, arrived):
+    depth, tiles, tall, block = plan.depth, plan.tiles, plan.tall, plan.block
+    blocks = plan.shares * tiles
+    sub = lax.broadcasted_iota(jnp.int32, (SUBS, LANES), 0)
+
+    def turn(i, piece_ref):
+        s, j = i // tiles, i % tiles
+        values = came_ref[pl.ds(s * block + j, depth, stride=tiles), :]
+        if tall > depth:
+            values = jnp.concatenate([values, jnp.zeros((tall - depth, LANES), F32)], axis=0)
+        piece_ref[:, 0:tall] = values.T
+
+    def put(i, piece_ref):
+        for g in range(LANES // SUBS):
+            values = piece_ref[g * SUBS : (g + 1) * SUBS, :]
+            for t in range(SUBS):
+                spot = place_ref[i * LANES + g * SUBS + t]
+                pltpu.store(grid_ref.at[pl.ds(spot - t, SUBS), :], values, mask=sub == t)
+
+    even_ref, odd_ref = piece_refs
+    arrived(0)
+    turn(0, even_ref)
+    per = blocks // (2 * PARTS)
+
+    @pl.loop(0, PARTS)
+    def _(part):
+        @pl.loop(0, per)
+        def _(i):
+            at = (part * per + i) * 2
+            turn(at + 1, odd_ref)
+            put(at, even_ref)
+
+            @pl.when(jnp.logical_and(i == per - 1, part < PARTS - 1))
+            def _():
+                arrived(part + 1)
+
+            turn(jnp.minimum(at + 2, blocks - 1), even_ref)
+            put(at + 1, odd_ref)
+
+
+def gather(plan, place_ref, out_ref, grid_ref, piece_refs, finished):
+    depth, tiles, tall = plan.depth, plan.tiles, plan.tall
+    blocks = plan.shares * tiles
+    sub = lax.broadcasted_iota(jnp.int32, (SUBS, LANES), 0)
+
+    def turn(i, piece_ref):
+        s, j = i // tiles, i % tiles
+        turned = piece_ref[:, 0:tall].T
+        out_ref[pl.ds(s * plan.data + j, depth, stride=tiles), :] = turned[0:depth, :]
+
+    def get(i, piece_ref):
+        for g in range(LANES // SUBS):
+            first = i * LANES + g * SUBS
+            values = grid_ref[pl.ds(place_ref[first], SUBS), :]
+            for t in range(1, SUBS):
+                shifted = grid_ref[pl.ds(place_ref[first + t] - t, SUBS), :]
+                values = jnp.where(sub == t, shifted, values)
+            piece_ref[g * SUBS : (g + 1) * SUBS, :] = values
+
+    even_ref, odd_ref = piece_refs
+    get(0, even_ref)
+    per = blocks // (2 * PARTS)
+
+    @pl.loop(0, PARTS)
+    def _(part):
+        @pl.loop(0, per)
+        def _(i):
+            at = (part * per + i) * 2
+            get(at + 1, odd_ref)
+            turn(at, even_ref)
+            get(jnp.minimum(at + 2, blocks - 1), even_ref)
+            turn(at + 1, odd_ref)
+
+        finished(part)
+
+
+def spread_drift(plan, came_ref, piece_ref, wide_ref, drift_ref):
+    piece_ref[...] = jnp.zeros((LANES, LANES), F32)
+    for s in range(plan.shares):
+        first = s * plan.block + plan.data + plan.tiles
+        piece_ref[s * plan.force : (s + 1) * plan.force, :] = came_ref[
+            first : first + plan.force, :
+        ]
+    turned = (courant_scale * piece_ref[...]).T
+    groups = plan.vregs // COARSE
+    for q in range(plan.shares * plan.force):
+        wide_ref[...] = jnp.broadcast_to(turned[:, q : q + 1], (LANES, LANES))
+        for a in range(LANES // (groups * SUBS)):
+            for m in range(groups):
+                to = q * LANES + (a * groups + m) * SUBS
+                drift_ref[to : to + SUBS, :] = wide_ref[
+                    pl.ds(a * groups * SUBS + m, SUBS, stride=groups), :
+                ]
+
+
+def sweep(plan, drift_ref, speed_ref, one_ref, two_ref):
+    cols, last = plan.cols, plan.coarse_rows - 1
+    groups = plan.vregs // COARSE
+    sub = lax.broadcasted_iota(jnp.int32, (SUBS, LANES), 0)
+    speeds = [jnp.broadcast_to(speed_ref[d : d + 1, :], (SUBS, LANES)) for d in range(2)]
+
+    for m in range(groups):
+
+        def courant(which, r4):
+            at = pl.multiple_of(((which * plan.coarse_rows + r4) * groups + m) * SUBS, SUBS)
+            value = speeds[which] + drift_ref[pl.ds(at, SUBS), :]
+            return value > 0.0, jnp.abs(value)
+
+        def at(row, q):
+            return pl.ds(pl.multiple_of((row + 1) * cols + q * SUBS, SUBS), SUBS)
+
+        def along(row, speed):
+            ahead, size = speed
+            base = pl.multiple_of((row + 1) * cols, SUBS)
+            first, count = m * COARSE, COARSE
+            line = [one_ref[at(row, q), :] for q in range(first, first + count)]
+            if first:
+                before = one_ref[at(row, first - 1), :]
+            else:
+                before = one_ref[pl.ds(base + cols - SUBS - 1, SUBS), :]
+                before = jnp.where(sub == 0, DRY, before)
+            if first + count < plan.vregs:
+                after = one_ref[at(row, first + count), :]
+            else:
+                after = jnp.where(sub == SUBS - 1, DRY, one_ref[pl.ds(base + 1, SUBS), :])
+            line = [before] + line + [after]
+            swept = []
+            for q in range(1, count + 1):
+                pick = jnp.where(ahead, line[q - 1], line[q + 1])
+                pick = jnp.where(pick < DRY, pick, 0.0)
+                moved = line[q] + size * (pick - line[q])
+                swept.append(jnp.where(line[q] < DRY, moved, 0.0))
+            return swept
+
+        def coarse(r4, held):
+            above, here = held
+            east = courant(0, r4)
+            ahead, size = courant(1, r4)
+            later = courant(0, jnp.minimum(r4 + 1, last))
+            for dr in range(COARSE):
+                row = r4 * COARSE + dr
+                below = along(row + 1, east if dr < COARSE - 1 else later)
+                for q in range(COARSE):
+                    pick = jnp.where(ahead, above[q], below[q])
+                    two_ref[at(row, m * COARSE + q), :] = here[q] + size * (pick - here[q])
+                above, here = here, below
+            return above, here
+
+        zero = [jnp.zeros((SUBS, LANES), F32)] * COARSE
+        lax.fori_loop(0, plan.coarse_rows, coarse, (zero, along(0, courant(0, 0))))
+
+
+def middle_kernel(
+    plan,
+    place_ref, speed_ref, came_hbm, out_hbm,
+    came_ref, out_ref, one_ref, two_ref, drift_ref, even_ref, odd_ref, in_sems, out_sems,
+):
+    shares, block, data = plan.shares, plan.block, plan.data
+    part_in, part_out = shares // PARTS * block, shares // PARTS * data
+
+    def copy_in(part):
+        at = pl.ds(pl.multiple_of(part * part_in, SUBS), part_in)
+        return pltpu.make_async_copy(came_hbm.at[at, :], came_ref.at[at, :], in_sems.at[part])
+
+    def copy_out(part):
+        at = pl.ds(pl.multiple_of(part * part_out, SUBS), part_out)
+        return pltpu.make_async_copy(out_ref.at[at, :], out_hbm.at[at, :], out_sems.at[part])
+
+    for part in range(PARTS):
+        copy_in(part).start()
+
+    @pl.loop(0, plan.size // LANES)
+    def _(i):
+        at = pl.ds(pl.multiple_of(i * LANES, LANES), LANES)
+        one_ref[at, :] = jnp.full((LANES, LANES), DRY, F32)
+
+    pieces = (even_ref, odd_ref)
+    scatter(plan, place_ref, came_ref, one_ref, pieces, lambda part: copy_in(part).wait())
+    spread_drift(plan, came_ref, even_ref, odd_ref, drift_ref)
+    me = lax.axis_index("space")
+    sweep(plan, drift_ref, speed_ref.at[me], one_ref, two_ref)
+    gather(plan, place_ref, out_ref, two_ref, pieces, lambda part: copy_out(part).start())
+    for part in range(PARTS):
+        copy_out(part).wait()
+
+
+VMEM = pl.BlockSpec(memory_space=pltpu.VMEM)
+SMEM = pl.BlockSpec(memory_space=pltpu.SMEM)
+ANY = pl.BlockSpec(memory_space=pl.ANY)
+
+
+def on_spectrum(
+    plan,
+    spectra,
+    wind_files,
+    current_files,
+    reader_turn,
+    cell_point,
+    coupling,
+    send_list,
+    send_count,
+    recv_list,
+):
+    shares, rows, spec, points = plan.shares, plan.rows, plan.spec, plan.points
+    tiles, depth, size, data_rows = plan.tiles, plan.depth, plan.size, plan.shares * plan.data
+    source, east_speed, north_speed = wave_tables()
+    table = jnp.asarray(source)
+    speed = np.zeros((shares, SUBS, LANES), np.float32)
+    speed[:, 0, :depth] = east_speed.reshape(shares, depth)
+    speed[:, 1, :depth] = north_speed.reshape(shares, depth)
+
+    def kernel(body, *, flops, traffic, vmem=WHOLE_VMEM, **options):
+        return pl.pallas_call(
+            body,
+            compiler_params=pltpu.CompilerParams(vmem_limit_bytes=vmem),
+            cost_estimate=pl.CostEstimate(flops=flops, bytes_accessed=traffic, transcendentals=0),
+            **options,
+        )
+
+    width = points + max(LANES, plan.force * LANES)
+    parcel = kernel(
+        functools.partial(pack_kernel, plan),
+        flops=0, traffic=4 * shares * 2 * width,
+        out_shape=jax.ShapeDtypeStruct((shares, 2, width), F32),
+        in_specs=[SMEM, VMEM, VMEM, VMEM],
+        out_specs=VMEM,
+        name="pack",
+    )(reader_turn, wind_files, current_files, recv_list)
+    parcel = lax.all_to_all(parcel, "space", 0, 0, tiled=True)
+
+    slot = jnp.arange(plan.cap, dtype=jnp.int32)[None, :]
+    names = jnp.where(slot < send_count[0][:, None], send_list[0], -1)
+    names = jnp.pad(names, ((0, 0), (0, LANES - plan.cap)), constant_values=-1)
+
+    cp = cell_point.reshape(1, rows)
+    coup = coupling.T
+    h_cost = dict(flops=2 * rows * spec * spec, traffic=12 * rows * spec)
+    h_scratch = [
+        pltpu.VMEM((spec, spec), BF16),
+        pltpu.VMEM((spec, rows), F32),
+        pltpu.VMEM((spec, rows), BF16),
+        pltpu.SemaphoreType.DMA((8,)),
+    ]
+    sent = kernel(
+        functools.partial(first_kernel, plan),
+        **h_cost,
+        out_shape=jax.ShapeDtypeStruct((shares * plan.block, LANES), F32),
+        in_specs=[VMEM] * 4 + [ANY] * 2,
+        out_specs=ANY,
+        scratch_shapes=[
+            pltpu.VMEM((shares * plan.block, LANES), F32),
+            pltpu.VMEM((data_rows, LANES), F32),
+            pltpu.SemaphoreType.DMA((8,)),
+            pltpu.VMEM((spec, rows), F32),
+        ]
+        + h_scratch,
+        name="first_half",
+    )(cp, parcel, names, table, spectra.T, coup)
+    came = lax.all_to_all(
+        sent.reshape(shares, plan.block, LANES), "space", 0, 0, tiled=True
+    )
+    place = came[:, plan.data : plan.data + tiles].astype(jnp.int32).reshape(-1)
+    swept = kernel(
+        functools.partial(middle_kernel, plan),
+        flops=24 * size * LANES, traffic=8 * rows * spec, vmem=32 * MIB,
+        out_shape=jax.ShapeDtypeStruct((data_rows, LANES), F32),
+        in_specs=[SMEM, VMEM, ANY],
+        out_specs=ANY,
+        scratch_shapes=[
+            pltpu.VMEM((shares * plan.block, LANES), F32),
+            pltpu.VMEM((data_rows, LANES), F32),
+            pltpu.VMEM((size, LANES), F32),
+            pltpu.VMEM((size, LANES), F32),
+            pltpu.VMEM((2 * points, LANES), F32),
+            pltpu.VMEM((LANES, LANES), F32),
+            pltpu.VMEM((LANES, LANES), F32),
+            pltpu.SemaphoreType.DMA((PARTS,)),
+            pltpu.SemaphoreType.DMA((PARTS,)),
+        ],
+        name="sweeps",
+    )(place, jnp.asarray(speed), came.reshape(-1, LANES))
+    back = lax.all_to_all(
+        swept.reshape(shares, depth, tiles, LANES), "space", 0, 0, tiled=True
+    )
+    result = kernel(
+        functools.partial(last_kernel, plan),
+        vmem=24 * MIB, **h_cost,
+        out_shape=jax.ShapeDtypeStruct((spec, rows), F32),
+        in_specs=[VMEM] * 3 + [ANY] * 2,
+        out_specs=ANY,
+        scratch_shapes=[
+            pltpu.VMEM((spec, rows), F32),
+            pltpu.SemaphoreType.DMA((8,)),
+            pltpu.VMEM((data_rows, LANES), F32),
+        ]
+        + h_scratch,
+        name="last_half",
+    )(cp, parcel, table, back.reshape(data_rows, LANES), coup)
+    return result.T
+
+
+def on_device(*args):
+    spectra, wind_files, send_list, wet_mask = args[0], args[1], args[6], args[9]
+    plan = Plan(
+        lax.axis_size("space"), *spectra.shape, send_list.shape[2], *wet_mask.shape, wind_files.shape[2]
+    )
+    if plan.fits():
+        return on_spectrum(plan, *args[:9])
+    return on_strips(*args)
+
+
 def solution(mesh):
     placed = (
         P(("members", "space"), None),

time: 473 us -> 197 us (0.42)
  waiting for transfers between devices: 260 us -> 0.01 us
  blocking collectives: 44.6 us -> 132 us
  other arithmetic: 56.8 us -> 0.08 us
  Pallas kernels: 0 us -> 46.8 us
  local copies, waits for them, and re-layouts: 52.2 us -> 7.32 us
  starting transfers between devices: 35 us -> 6.55 us
  matrix products: 21.6 us -> 0 us
    all_to_all x2 -> x1, waiting for transfers between devices: 249 us -> 0.01 us  [on_spectrum(): parcel = lax.all_to_all(parcel, 'space', 0, 0, tiled=True)]
    all_to_all x0 -> x2, blocking collectives: none -> 132 us  [the longest x1 67.5 us: on_spectrum(): lax.all_to_all(sent.reshape(shares, plan.block, LANES), 'space', 0, 0, ti...]
    pallas_call x0 -> x4, Pallas kernels: none -> 46.8 us  [the longest x1 27.3 us: on_spectrum(): kernel(functools.partial(middle_kernel, plan), flops=24 * size * LANES, t...]
    psum x1 -> x0, blocking collectives: 44.6 us -> none  [from_root(): return lax.psum(jnp.where(mine, array, jnp.zeros_like(array)), axis)]
    scatter-add x2 -> x0, other arithmetic: 26.8 us -> none  [the longest x1 14.5 us: on_device(): energy_grid = jnp.zeros((row_count * col_count, spec_width), jnp.float32)...]
    mul x12 -> x0, other arithmetic: 23.8 us -> none  [the longest x1 7.97 us: sweep_rows(): advect(energy_grid, row_above, row_below, courant) * wet_field[:, :, None]]
    all_to_all x2 -> x1, starting transfers between devices: 29.5 us -> 6.55 us  [on_spectrum(): parcel = lax.all_to_all(parcel, 'space', 0, 0, tiled=True)]
    dot_general x2 -> x0, matrix products: 21.6 us -> none  [source_half(): jnp.dot(local_part.astype(jnp.bfloat16), coupling, preferred_element_type...]
  transfers between devices with their start and end apart: 4 -> 1, of which waited for: 4 -> 0; matrix products, arithmetic and copies ran while one was open for 1% -> 3% of each run, Pallas kernels for 0% -> 0%
where the time goes in v5:
time: 197 us; the launch traced here: 193 us
  blocking collectives  132 us (67%)
  Pallas kernels  46.8 us (24%)
  local copies, waits for them, and re-layouts  7.32 us (4%)
  starting transfers between devices  6.55 us (3%)
    all_to_all x1, blocking collectives, on_spectrum(): lax.all_to_all(sent.reshape(shares, plan.block, LANES), 'space', 0, 0, ti...  67.5 us
    all_to_all x1, blocking collectives, on_spectrum(): lax.all_to_all(swept.reshape(shares, depth, tiles, LANES), 'space', 0, 0,...  64.8 us
    pallas_call x1, Pallas kernels, on_spectrum(): kernel(functools.partial(middle_kernel, plan), flops=24 * size * LANES, t...  27.3 us
    pallas_call x1, Pallas kernels, on_spectrum(): kernel(functools.partial(first_kernel, plan), **h_cost, out_shape=jax.Sha...  9.71 us
    pallas_call x1, Pallas kernels, on_spectrum(): kernel(functools.partial(last_kernel, plan), vmem=24 * MIB, **h_cost, out...  8.23 us
    unnamed x17, local copies, waits for them, and re-layouts  6.72 us
    all_to_all x1, starting transfers between devices, on_spectrum(): parcel = lax.all_to_all(parcel, 'space', 0, 0, tiled=True)  6.55 us
  transfers between devices with their start and end apart: 1, of which 0 were waited for; matrix products, arithmetic and copies ran while one was open for 3% of the time, Pallas kernels for 0%

profile of v5, /device:TPU:15, one launch (start us, length us, event | category | flops | bytes accessed | tf_op | source)
XLA Modules:
  0.0 193.1 jit_solution(17943073685160015062)
XLA Ops:
  0.0 1.5 pack.1
  1.5 6.6 %all-to-all-start = ((f32[16,2,1152]{2,1,0:T(2,128)}), f32[16,2,1152]{2,1,0:T(2,128)S(1)}, u32[]{:S(2)}, u32[]{:S(2)}) async-start(f32[16,2,1152]{2,1,0:T(2,128)} %pack.1), calls=%async_computation | async-start | bytes 294912 | tf_op jit(solution)/shard_map/all_to_all | solution.py:626
  8.0 0.0 copy-start.6
  8.0 0.0 copy-start.7
  8.1 6.0 %copy.12 = bf16[1296,1296]{0,1:T(8,128)(2,1)} copy(bf16[1296,1296]{1,0:T(8,128)(2,1)} %param.17) | data formatting | bytes 6718464 | tf_op args[5]
  14.1 0.0 copy-done.6
  14.1 0.0 copy-done.7
  14.1 0.1 bitcast_select_fusion
  14.2 0.6 pad.4.names_ref
  14.8 0.0 all-to-all-done.parcel_ref
  14.8 0.0 copy-start.2
  14.8 0.7 copy-done.2
  15.4 9.7 %first_half.1 = f32[5376,128]{1,0:T(8,128)} custom-call(s32[1,512]{1,0:T(1,128)} %bitcast.18, f32[16,2,1152]{2,1,0:T(2,128)} %copy-done.2, s32[16,128]{1,0:T(8,128)} %pad.4.names_ref, f32[1296,8]{1,0:T(8,128)} %constant.6.clone.table_ref, f32[1296,512]{1,0:T(8,128)} %bitcast.21, bf16[1296,1296]{1,0:T(8,128)(2,1)} %bitcast.12), custom_call_target="tpu_custom_call" | custom-call | flops 1719926784 | bytes 7962624 | tf_op jit(solution)/shard_map/first_half/pallas_call | solution.py:641
  25.1 0.0 copy-start.4
  25.2 67.5 %all_to_all.15 = f32[16,336,128]{2,1,0:T(8,128)S(1)} all-to-all(f32[16,336,128]{2,1,0:T(8,128)} %bitcast.20), channel_id=1, replica_groups=mesh['members'=2,'space'=16] {'space'}, dimensions={0} | all-to-all | bytes 5505024 | tf_op jit(solution)/shard_map/all_to_all | solution.py:656
  92.7 0.0 copy-done.4
  92.7 27.3 %sweeps.1 = f32[5184,128]{1,0:T(8,128)S(1)} custom-call(s32[8192]{0:T(1024)S(1)} %bitcast.17, f32[16,8,128]{2,1,0:T(8,128)S(1)} %copy-done.4, f32[5376,128]{1,0:T(8,128)S(1)} %bitcast.14), custom_call_target="tpu_custom_call" | custom-call | flops 51118080 | bytes 5308416 | tf_op jit(solution)/shard_map/sweeps/pallas_call | solution.py:660
  120.0 0.0 copy-start
  120.1 0.0 copy-start.1
  120.1 0.0 copy-start.3
  120.1 0.0 copy-start.5
  120.1 64.8 %all_to_all.16 = f32[16,81,4,128]{3,2,1,0:T(4,128)S(1)} all-to-all(f32[16,81,4,128]{3,2,1,0:T(4,128)S(1)} %bitcast.16), channel_id=1, replica_groups=mesh['members'=2,'space'=16] {'space'}, dimensions={0} | all-to-all | bytes 5308416 | tf_op jit(solution)/shard_map/all_to_all | solution.py:679
  184.9 0.0 copy-done
  184.9 0.0 copy-done.1
  184.9 0.0 copy-done.3
  184.9 0.0 copy-done.5
  184.9 8.2 %last_half.1 = f32[1296,512]{1,0:T(8,128)} custom-call(s32[1,512]{1,0:T(1,128)S(1)} %bitcast.19, f32[16,2,1152]{2,1,0:T(2,128)S(1)} %copy-done.3, f32[1296,8]{1,0:T(8,128)S(1)} %copy-done.1, f32[5184,128]{1,0:T(8,128)S(1)} %bitcast.15, bf16[1296,1296]{1,0:T(8,128)(2,1)S(1)} %bitcast.13), custom_call_target="tpu_custom_call" | custom-call | flops 1719926784 | bytes 7962624 | tf_op jit(solution)/shard_map/last_half/pallas_call | solution.py:682
  (1 shorter events, 0.0 us)
Async XLA Ops:
  1.5 13.3 %all-to-all-start = ((f32[16,2,1152]{2,1,0:T(2,128)}), f32[16,2,1152]{2,1,0:T(2,128)S(1)}, u32[]{:S(2)}, u32[]{:S(2)}) async-start(f32[16,2,1152]{2,1,0:T(2,128)} %pack.1), calls=%async_computation | async-start | bytes 294912 | tf_op jit(solution)/shard_map/all_to_all | solution.py:626
  8.0 6.0 %copy-start.6 = (s32[1,16,64]{2,1,0:T(8,128)S(1)}, s32[1,16,64]{2,1,0:T(8,128)}, u32[]{:S(2)}) copy-start(s32[1,16,64]{2,1,0:T(8,128)} %param.18) | copy-start | bytes 12292
  8.0 6.0 %copy-start.7 = (s32[1,16]{1,0:T(1,128)S(1)}, s32[1,16]{1,0:T(1,128)}, u32[]{:S(2)}) copy-start(s32[1,16]{1,0:T(1,128)} %param.19) | copy-start | bytes 196
  14.8 0.7 copy-start.2
  25.1 67.5 %copy-start.4 = (f32[16,8,128]{2,1,0:T(8,128)S(1)}, f32[16,8,128]{2,1,0:T(8,128)}, u32[]{:S(2)}) copy-start(f32[16,8,128]{2,1,0:T(8,128)} %constant.7.clone.speed_ref) | copy-start | bytes 196612
  120.0 64.8 %copy-start = (bf16[1296,1296]{0,1:T(8,128)(2,1)S(1)}, bf16[1296,1296]{0,1:T(8,128)(2,1)}, u32[]{:S(2)}) copy-start(bf16[1296,1296]{0,1:T(8,128)(2,1)} %copy.12) | copy-start | bytes 10077700
  120.1 64.8 %copy-start.1 = (f32[1296,8]{1,0:T(8,128)S(1)}, f32[1296,8]{1,0:T(8,128)}, u32[]{:S(2)}) copy-start(f32[1296,8]{1,0:T(8,128)} %constant.6.clone.table_ref) | copy-start | bytes 124420
  120.1 64.8 %copy-start.3 = (f32[16,2,1152]{2,1,0:T(2,128)S(1)}, f32[16,2,1152]{2,1,0:T(2,128)}, u32[]{:S(2)}) copy-start(f32[16,2,1152]{2,1,0:T(2,128)} %copy-done.2) | copy-start | bytes 442372
  120.1 64.8 %copy-start.5 = (s32[512]{0:T(512)S(1)}, s32[512]{0:T(512)}, u32[]{:S(2)}) copy-start(s32[512]{0:T(512)} %param.16) | copy-start | bytes 6148

commit v6 on v5

--- a/solution.py
+++ b/solution.py
@@ -167,6 +167,7 @@
 WHOLE_VMEM = 60 * MIB
 DRY = 1e30
 PARTS = 4
+PERIOD = 4 * FREQS
 
 
 def wave_tables():
@@ -177,10 +178,11 @@
     group = 0.5 * phase
     cos_dir, sin_dir = np.cos(direction)[:, None], np.sin(direction)[:, None]
     flat = lambda t: np.broadcast_to(t, (DIRS, FREQS)).reshape(-1)
+    growth = half_length * input_coef * angular
     source = np.zeros((DIRS * FREQS, 8), np.float32)
-    source[:, 0] = flat(wind_gain * cos_dir / phase)
-    source[:, 1] = flat(wind_gain * sin_dir / phase)
-    source[:, 2] = flat(half_length * input_coef * angular)
+    source[:, 0] = flat(growth * wind_gain * cos_dir / phase)
+    source[:, 1] = flat(growth * wind_gain * sin_dir / phase)
+    source[:, 2] = flat(1.0 - growth)
     source[:, 3] = flat(half_length * dissip_coef * angular)
     east = flat(courant_scale * cos_dir * group).astype(np.float32)
     north = flat(courant_scale * sin_dir * group).astype(np.float32)
@@ -210,6 +212,8 @@
         self.coarse_rows = self.grid_rows // COARSE
         self.vregs = cols // SUBS
         self.size = (self.grid_rows + 2) * cols
+        self.tall_step = largest_step(spec, PERIOD, 512)
+        self.thirds = spec // self.tall_step
 
     def fits(self):
         if self.spec % self.shares or self.depth > LANES or self.rows % (2 * LANES):
@@ -251,76 +255,95 @@
     return both[0:1], both[1:2]
 
 
-def half_step(
-    plan, energy_hbm, energy_ref, load, parcel_ref, cp_ref, table_ref, coup_hbm, coup_ref,
-    loc_ref, locb_ref, sems, store,
-):
-    spec, rows = plan.spec, plan.rows
-    tall = largest_step(spec, 16, 512)
-    thirds = spec // tall
-    tall_rows = energy_ref.shape[0] // thirds
-    arrive = [
+def fetch(source, target, sems, parts):
+    size = target.shape[0] // parts
+    copies = [
         pltpu.make_async_copy(
-            energy_hbm.at[pl.ds(q * tall_rows, tall_rows), :],
-            energy_ref.at[pl.ds(q * tall_rows, tall_rows), :],
-            sems.at[q],
+            source.at[pl.ds(q * size, size), :], target.at[pl.ds(q * size, size), :], sems.at[q]
         )
-        for q in range(thirds)
+        for q in range(parts)
     ]
-    fetch = pltpu.make_async_copy(coup_hbm, coup_ref, sems.at[thirds])
-    for copy in arrive:
+    for copy in copies:
         copy.start()
-    fetch.start()
-    east, north = cell_winds(jnp.sum(parcel_ref[:, :, 0 : plan.points], axis=0), cp_ref[...])
-    step = largest_step(tall, 16, 64)
+    return copies
+
+
+def unit_loss(plan, load, arrive, table_ref, unit_ref):
+    tall = plan.spec // len(arrive)
 
     def squares(i, total):
-        piece = load(pl.multiple_of(i * step, step), step)
-        return total + jnp.sum((piece * piece).reshape(step // SUBS, SUBS, rows), axis=0)
-
-    total = jnp.zeros((SUBS, rows), F32)
-    for q in range(thirds):
-        arrive[q].wait()
-        total = lax.fori_loop(q * tall // step, (q + 1) * tall // step, squares, total)
-    mean_square = jnp.sum(total, axis=0, keepdims=True) * (1.0 / spec)
-
-    @pl.loop(0, spec // step)
-    def _(i):
-        first = pl.multiple_of(i * step, step)
-        at = pl.ds(first, step)
-        table = table_ref[at, :]
-        along = east * table[:, 0:1] + north * table[:, 1:2]
-        gain = 1.0 + table[:, 2:3] * jnp.maximum(along - 1.0, 0.0)
-        loss = 1.0 + table[:, 3:4] * mean_square
-        local = load(first, step) * gain / loss
-        loc_ref[at, :] = local
-        locb_ref[at, :] = local.astype(BF16)
-
-    fetch.wait()
-    for q in range(thirds):
-        at = slice(q * tall, (q + 1) * tall)
+        piece = load(pl.multiple_of(i * 48, 48), 48)
+        return total + jnp.sum((piece * piece).reshape(48 // SUBS, SUBS, plan.rows), axis=0)
+
+    total = jnp.zeros((SUBS, plan.rows), F32)
+    for q, copy in enumerate(arrive):
+        copy.wait()
+        total = lax.fori_loop(q * tall // 48, (q + 1) * tall // 48, squares, total)
+    mean_square = jnp.sum(total, axis=0, keepdims=True) * (1.0 / plan.spec)
+    unit_ref[...] = 1.0 / (1.0 + table_ref[0:PERIOD, 3:4] * mean_square)
+
+
+def growth_step(first, east, north, table_ref):
+    table = table_ref[pl.ds(first, PERIOD), :]
+    return jnp.maximum(east * table[:, 0:1] + north * table[:, 1:2] + table[:, 2:3], 1.0)
+
+
+def coupled(plan, coup_ref, loc_ref, locb_ref, store):
+    for q in range(plan.thirds):
+        at = slice(q * plan.tall_step, (q + 1) * plan.tall_step)
         store(
-            q * tall,
+            q * plan.tall_step,
             loc_ref[at, :]
             + jnp.dot(coup_ref[at, :], locb_ref[...], preferred_element_type=F32),
         )
 
 
-def own_places(plan, parcel_ref, names_ref):
-    points, cols, vregs = plan.points, plan.cols, plan.vregs
+def ready_kernel(
+    plan, table_ref, coup_hbm, energy_hbm, turned_hbm, base_hbm,
+    coup_ref, turned_ref, energy_ref, unit_ref, sems, coup_sem, out_sems,
+):
+    spec = plan.spec
+    get = pltpu.make_async_copy(coup_hbm, coup_ref, coup_sem)
+    get.start()
+    arrive = fetch(energy_hbm, energy_ref, sems, plan.thirds)
+    unit_loss(plan, lambda first, count: energy_ref[pl.ds(first, count), :], arrive, table_ref, unit_ref)
+
+    @pl.loop(0, spec // PERIOD)
+    def _(i):
+        at = pl.ds(pl.multiple_of(i * PERIOD, PERIOD), PERIOD)
+        energy_ref[at, :] = energy_ref[at, :] * unit_ref[...]
+
+    put_base = pltpu.make_async_copy(energy_ref, base_hbm, out_sems.at[0])
+    put_base.start()
+    get.wait()
+    for first in range(0, spec, LANES):
+        at = slice(first, min(first + LANES, spec))
+        turned_ref[at, :] = coup_ref[:, at].T
+    put_turned = pltpu.make_async_copy(turned_ref, turned_hbm, out_sems.at[1])
+    put_turned.start()
+    put_base.wait()
+    put_turned.wait()
+
+
+def own_places(plan, parcel_ref, send_ref, count_ref):
+    points, cols, vregs, cap = plan.points, plan.cols, plan.vregs, plan.cap
     landing = jnp.concatenate(
-        [parcel_ref[b, 0:1, points : points + LANES] for b in range(plan.shares)], axis=0
+        [parcel_ref[b, 0:1, points : points + cap] for b in range(plan.shares)], axis=0
     ).astype(jnp.int32)
-    cell = landing + plan.strip * lax.broadcasted_iota(jnp.int32, (plan.shares, LANES), 0)
+    cell = landing + plan.strip * lax.broadcasted_iota(jnp.int32, (plan.shares, cap), 0)
     column = lax.rem(cell, cols)
     place = cell - column + cols + lax.rem(column, vregs) * SUBS + lax.div(column, vregs)
     place = place.astype(F32)
+    slot = lax.broadcasted_iota(jnp.int32, (1, cap), 1)
+    names = [
+        jnp.where(slot < count_ref[0, b], send_ref[0, b : b + 1, :], -1) for b in range(plan.shares)
+    ]
     rows = []
     for j in range(plan.tiles):
-        own = lax.broadcasted_iota(jnp.int32, (LANES, LANES), 0) + j * LANES
-        found = jnp.zeros((LANES, LANES), F32)
+        own = lax.broadcasted_iota(jnp.int32, (LANES, cap), 0) + j * LANES
+        found = jnp.zeros((LANES, cap), F32)
         for b in range(plan.shares):
-            found += jnp.where(names_ref[b : b + 1, :] == own, place[b : b + 1, :], 0.0)
+            found += jnp.where(names[b] == own, place[b : b + 1, :], 0.0)
         found = jnp.broadcast_to(jnp.sum(found, axis=1, keepdims=True), (LANES, LANES))
         rows.append(found.T[0:1, :])
     return rows
@@ -328,18 +351,37 @@
 
 def first_kernel(
     plan,
-    cp_ref, parcel_ref, names_ref, table_ref, energy_hbm, coup_hbm, out_hbm,
-    out_ref, buf_ref, out_sems, energy_ref, coup_ref, loc_ref, locb_ref, sems,
+    count_ref, cp_ref, parcel_ref, send_ref, table_ref, base_hbm, coup_hbm, winds_ref, out_hbm,
+    out_ref, buf_ref, base_ref, coup_ref, locb_ref, sems, coup_sem, out_sems,
 ):
     tiles, shares, points, block, data = plan.tiles, plan.shares, plan.points, plan.block, plan.data
+    arrive = fetch(base_hbm, base_ref, sems, plan.thirds)
+    get = pltpu.make_async_copy(coup_hbm, coup_ref, coup_sem)
+    get.start()
     width = plan.force * LANES
     current = jnp.sum(parcel_ref[:, :, points : points + width], axis=0)
-    spare = own_places(plan, parcel_ref, names_ref)
+    spare = own_places(plan, parcel_ref, send_ref, count_ref)
     spare += [current[1:2, f * LANES : (f + 1) * LANES] for f in range(plan.force)]
     if block > data + len(spare):
         spare.append(jnp.zeros((block - data - len(spare), LANES), F32))
     for d in range(shares):
         out_ref[d * block + data : (d + 1) * block, :] = jnp.concatenate(spare, axis=0)
+    east, north = cell_winds(jnp.sum(parcel_ref[:, :, 0:points], axis=0), cp_ref[...])
+    winds_ref[0:1, :] = east
+    winds_ref[1:2, :] = north
+    per = plan.tall_step // PERIOD
+    for q in range(plan.thirds):
+        arrive[q].wait()
+
+        @pl.loop(q * per, (q + 1) * per)
+        def _(i):
+            first = pl.multiple_of(i * PERIOD, PERIOD)
+            at = pl.ds(first, PERIOD)
+            local = base_ref[at, :] * growth_step(first, east, north, table_ref)
+            base_ref[at, :] = local
+            locb_ref[at, :] = local.astype(BF16)
+
+    get.wait()
     sent, copies = [0], []
 
     def store(first, values):
@@ -357,21 +399,21 @@
         copies[-1].start()
         sent[0] = upto
 
-    half_step(
-        plan, energy_hbm, energy_ref, lambda first, count: energy_ref[pl.ds(first, count), :],
-        parcel_ref, cp_ref, table_ref, coup_hbm, coup_ref, loc_ref, locb_ref, sems, store,
-    )
+    coupled(plan, coup_ref, base_ref, locb_ref, store)
     for copy in copies:
         copy.wait()
 
 
 def last_kernel(
     plan,
-    cp_ref, parcel_ref, table_ref, came_hbm, coup_hbm, out_hbm,
-    res_ref, out_sems, came_ref, coup_ref, loc_ref, locb_ref, sems,
+    winds_ref, table_ref, came_hbm, coup_hbm, out_hbm,
+    came_ref, coup_ref, loc_ref, locb_ref, unit_ref, sems, coup_sem, out_sems,
 ):
     tiles = plan.tiles
     copies = []
+    arrive = fetch(came_hbm, came_ref, sems, plan.thirds)
+    get = pltpu.make_async_copy(coup_hbm, coup_ref, coup_sem)
+    get.start()
 
     def load(first, count):
         start = pl.multiple_of(first * tiles, SUBS)
@@ -379,18 +421,27 @@
             [came_ref[pl.ds(start + j, count, stride=tiles), :] for j in range(tiles)], axis=1
         )
 
+    unit_loss(plan, load, arrive, table_ref, unit_ref)
+    east, north = winds_ref[0:1, :], winds_ref[1:2, :]
+
+    @pl.loop(0, plan.spec // PERIOD)
+    def _(i):
+        first = pl.multiple_of(i * PERIOD, PERIOD)
+        at = pl.ds(first, PERIOD)
+        local = load(first, PERIOD) * unit_ref[...] * growth_step(first, east, north, table_ref)
+        loc_ref[at, :] = local
+        locb_ref[at, :] = local.astype(BF16)
+
     def store(first, values):
         at = slice(first, first + values.shape[0])
-        res_ref[at, :] = values
+        loc_ref[at, :] = values
         copies.append(
-            pltpu.make_async_copy(res_ref.at[at, :], out_hbm.at[at, :], out_sems.at[len(copies)])
+            pltpu.make_async_copy(loc_ref.at[at, :], out_hbm.at[at, :], out_sems.at[len(copies)])
         )
         copies[-1].start()
 
-    half_step(
-        plan, came_hbm, came_ref, load,
-        parcel_ref, cp_ref, table_ref, coup_hbm, coup_ref, loc_ref, locb_ref, sems, store,
-    )
+    get.wait()
+    coupled(plan, coup_ref, loc_ref, locb_ref, store)
     for copy in copies:
         copy.wait()
 
@@ -625,34 +676,40 @@
     )(reader_turn, wind_files, current_files, recv_list)
     parcel = lax.all_to_all(parcel, "space", 0, 0, tiled=True)
 
-    slot = jnp.arange(plan.cap, dtype=jnp.int32)[None, :]
-    names = jnp.where(slot < send_count[0][:, None], send_list[0], -1)
-    names = jnp.pad(names, ((0, 0), (0, LANES - plan.cap)), constant_values=-1)
-
     cp = cell_point.reshape(1, rows)
-    coup = coupling.T
     h_cost = dict(flops=2 * rows * spec * spec, traffic=12 * rows * spec)
-    h_scratch = [
-        pltpu.VMEM((spec, spec), BF16),
-        pltpu.VMEM((spec, rows), F32),
-        pltpu.VMEM((spec, rows), BF16),
-        pltpu.SemaphoreType.DMA((8,)),
-    ]
-    sent = kernel(
+    whole = pltpu.VMEM((spec, rows), F32)
+    rounded = pltpu.VMEM((spec, rows), BF16)
+    square = pltpu.VMEM((spec, spec), BF16)
+    unit = pltpu.VMEM((PERIOD, rows), F32)
+    dma = pltpu.SemaphoreType.DMA
+    coup, base = kernel(
+        functools.partial(ready_kernel, plan),
+        flops=0, traffic=12 * rows * spec,
+        out_shape=[
+            jax.ShapeDtypeStruct((spec, spec), BF16), jax.ShapeDtypeStruct((spec, rows), F32)
+        ],
+        in_specs=[VMEM, ANY, ANY],
+        out_specs=[ANY, ANY],
+        scratch_shapes=[square, square, whole, unit, dma((plan.thirds,)), dma, dma((2,))],
+        name="ready",
+    )(table, coupling, spectra.T)
+    winds, sent = kernel(
         functools.partial(first_kernel, plan),
         **h_cost,
-        out_shape=jax.ShapeDtypeStruct((shares * plan.block, LANES), F32),
-        in_specs=[VMEM] * 4 + [ANY] * 2,
-        out_specs=ANY,
+        out_shape=[
+            jax.ShapeDtypeStruct((SUBS, rows), F32),
+            jax.ShapeDtypeStruct((shares * plan.block, LANES), F32),
+        ],
+        in_specs=[SMEM] + [VMEM] * 4 + [ANY] * 2,
+        out_specs=[VMEM, ANY],
         scratch_shapes=[
             pltpu.VMEM((shares * plan.block, LANES), F32),
             pltpu.VMEM((data_rows, LANES), F32),
-            pltpu.SemaphoreType.DMA((8,)),
-            pltpu.VMEM((spec, rows), F32),
-        ]
-        + h_scratch,
+            whole, square, rounded, dma((plan.thirds,)), dma, dma((plan.thirds,)),
+        ],
         name="first_half",
-    )(cp, parcel, names, table, spectra.T, coup)
+    )(send_count, cp, parcel, send_list, table, base, coup)
     came = lax.all_to_all(
         sent.reshape(shares, plan.block, LANES), "space", 0, 0, tiled=True
     )
@@ -683,16 +740,14 @@
         functools.partial(last_kernel, plan),
         vmem=24 * MIB, **h_cost,
         out_shape=jax.ShapeDtypeStruct((spec, rows), F32),
-        in_specs=[VMEM] * 3 + [ANY] * 2,
+        in_specs=[VMEM] * 2 + [ANY] * 2,
         out_specs=ANY,
         scratch_shapes=[
-            pltpu.VMEM((spec, rows), F32),
-            pltpu.SemaphoreType.DMA((8,)),
             pltpu.VMEM((data_rows, LANES), F32),
-        ]
-        + h_scratch,
+            square, whole, rounded, unit, dma((plan.thirds,)), dma, dma((plan.thirds,)),
+        ],
         name="last_half",
-    )(cp, parcel, table, back.reshape(data_rows, LANES), coup)
+    )(winds, table, back.reshape(data_rows, LANES), coup)
     return result.T
 
 

time: 197 us -> 194 us (0.985)
  local copies, waits for them, and re-layouts: 7.32 us -> 0.67 us
  Pallas kernels: 46.8 us -> 50.8 us
    pallas_call x1 -> x2, Pallas kernels: 9.71 us -> 16 us  [the longest x1 8.54 us: on_spectrum(): kernel(functools.partial(first_kernel, plan), **h_cost, out_shape=[jax.Sh...]
    unnamed x17 -> x10, local copies, waits for them, and re-layouts: 6.72 us -> 0.67 us
    pallas_call x1, Pallas kernels: 8.23 us -> 6.05 us  [on_spectrum(): kernel(functools.partial(last_kernel, plan), vmem=24 * MIB, **h_cost, out...]
  transfers between devices with their start and end apart: 1 -> 1, of which waited for: 0 -> 0; matrix products, arithmetic and copies ran while one was open for 3% -> 0% of each run, Pallas kernels for 0% -> 4%
where the time goes in v6:
time: 194 us; the launch traced here: 190 us
  blocking collectives  132 us (68%)
  Pallas kernels  50.8 us (26%)
  starting transfers between devices  6.55 us (3%)
    all_to_all x1, blocking collectives, on_spectrum(): lax.all_to_all(sent.reshape(shares, plan.block, LANES), 'space', 0, 0, ti...  67.5 us
    all_to_all x1, blocking collectives, on_spectrum(): lax.all_to_all(swept.reshape(shares, depth, tiles, LANES), 'space', 0, 0,...  64.8 us
    pallas_call x1, Pallas kernels, on_spectrum(): kernel(functools.partial(middle_kernel, plan), flops=24 * size * LANES, t...  27.4 us
    pallas_call x1, Pallas kernels, on_spectrum(): kernel(functools.partial(first_kernel, plan), **h_cost, out_shape=[jax.Sh...  8.54 us
    pallas_call x1, Pallas kernels, on_spectrum(): kernel(functools.partial(ready_kernel, plan), flops=0, traffic=12 * rows...  7.43 us
    all_to_all x1, starting transfers between devices, on_spectrum(): parcel = lax.all_to_all(parcel, 'space', 0, 0, tiled=True)  6.55 us
    pallas_call x1, Pallas kernels, on_spectrum(): kernel(functools.partial(last_kernel, plan), vmem=24 * MIB, **h_cost, out...  6.05 us
  transfers between devices with their start and end apart: 1, of which 0 were waited for; matrix products, arithmetic and copies ran while one was open for 0% of the time, Pallas kernels for 4%

profile of v6, /device:TPU:15, one launch (start us, length us, event | category | flops | bytes accessed | tf_op | source)
XLA Modules:
  0.0 190.5 jit_solution(16713937721163834010)
XLA Ops:
  0.0 1.5 pack.1
  1.5 6.6 %all-to-all-start = ((f32[16,2,1152]{2,1,0:T(2,128)}), f32[16,2,1152]{2,1,0:T(2,128)S(1)}, u32[]{:S(2)}, u32[]{:S(2)}) async-start(f32[16,2,1152]{2,1,0:T(2,128)} %pack.1), calls=%async_computation | async-start | bytes 294912 | tf_op jit(solution)/shard_map/all_to_all | solution.py:677
  8.0 7.4 %ready.1 = (bf16[1296,1296]{1,0:T(8,128)(2,1)}, f32[1296,512]{1,0:T(8,128)}) custom-call(f32[1296,8]{1,0:T(8,128)} %constant.4.clone.table_ref, bf16[1296,1296]{1,0:T(8,128)(2,1)} %coup_hbm.1, f32[1296,512]{1,0:T(8,128)} %bitcast.13), custom_call_target="tpu_custom_call" | custom-call | bytes 7962624 | tf_op jit(solution)/shard_map/ready/pallas_call | solution.py:686
  15.5 0.0 all-to-all-done.parcel_ref
  15.5 0.0 copy-start.4
  15.5 0.6 copy-done.4
  16.1 8.5 %first_half.1 = (f32[8,512]{1,0:T(8,128)}, f32[5376,128]{1,0:T(8,128)}) custom-call(s32[1,16]{1,0:T(1,128)} %count_ref.1, s32[1,512]{1,0:T(1,128)} %bitcast.14, f32[16,2,1152]{2,1,0:T(2,128)} %copy-done.4, s32[1,16,64]{2,1,0:T(8,128)} %send_ref.1, f32[1296,8]{1,0:T(8,128)} %constant.4.clone.table_ref, f32[1296,512]{1,0:T(8,128)} %get-tuple-element.9.base_hbm, ...), custom_call_target="tpu_custom_call" | custom-call | flops 1719926784 | bytes 7962624 | tf_op jit(solution)/shard_map/first_half/pallas_call | solution.py:697
  24.7 0.0 copy-start.2
  24.7 67.5 %all_to_all.15 = f32[16,336,128]{2,1,0:T(8,128)S(1)} all-to-all(f32[16,336,128]{2,1,0:T(8,128)} %bitcast.12), channel_id=1, replica_groups=mesh['members'=2,'space'=16] {'space'}, dimensions={0} | all-to-all | bytes 5505024 | tf_op jit(solution)/shard_map/all_to_all | solution.py:713
  92.2 0.0 copy-done.2
  92.2 27.4 %sweeps.1 = f32[5184,128]{1,0:T(8,128)S(1)} custom-call(s32[8192]{0:T(1024)S(1)} %bitcast.11, f32[16,8,128]{2,1,0:T(8,128)S(1)} %copy-done.2, f32[5376,128]{1,0:T(8,128)S(1)} %bitcast.8), custom_call_target="tpu_custom_call" | custom-call | flops 51118080 | bytes 5308416 | tf_op jit(solution)/shard_map/sweeps/pallas_call | solution.py:717
  119.6 0.0 copy-start
  119.6 0.0 copy-start.1
  119.6 0.0 copy-start.3
  119.6 64.8 %all_to_all.16 = f32[16,81,4,128]{3,2,1,0:T(4,128)S(1)} all-to-all(f32[16,81,4,128]{3,2,1,0:T(4,128)S(1)} %bitcast.10), channel_id=1, replica_groups=mesh['members'=2,'space'=16] {'space'}, dimensions={0} | all-to-all | bytes 5308416 | tf_op jit(solution)/shard_map/all_to_all | solution.py:736
  184.4 0.0 copy-done
  184.4 0.0 copy-done.1
  184.4 0.0 copy-done.3
  184.4 6.0 %last_half.1 = f32[1296,512]{1,0:T(8,128)} custom-call(f32[8,512]{1,0:T(8,128)S(1)} %copy-done.3, f32[1296,8]{1,0:T(8,128)S(1)} %copy-done.1, f32[5184,128]{1,0:T(8,128)S(1)} %bitcast.9, bf16[1296,1296]{1,0:T(8,128)(2,1)S(1)} %copy-done), custom_call_target="tpu_custom_call" | custom-call | flops 1719926784 | bytes 7962624 | tf_op jit(solution)/shard_map/last_half/pallas_call | solution.py:739
  (1 shorter events, 0.0 us)
Async XLA Ops:
  1.5 14.0 %all-to-all-start = ((f32[16,2,1152]{2,1,0:T(2,128)}), f32[16,2,1152]{2,1,0:T(2,128)S(1)}, u32[]{:S(2)}, u32[]{:S(2)}) async-start(f32[16,2,1152]{2,1,0:T(2,128)} %pack.1), calls=%async_computation | async-start | bytes 294912 | tf_op jit(solution)/shard_map/all_to_all | solution.py:677
  15.5 0.7 copy-start.4
  24.7 67.5 %copy-start.2 = (f32[16,8,128]{2,1,0:T(8,128)S(1)}, f32[16,8,128]{2,1,0:T(8,128)}, u32[]{:S(2)}) copy-start(f32[16,8,128]{2,1,0:T(8,128)} %constant.5.clone.speed_ref) | copy-start | bytes 196612
  119.6 64.8 %copy-start = (bf16[1296,1296]{1,0:T(8,128)(2,1)S(1)}, bf16[1296,1296]{1,0:T(8,128)(2,1)}, u32[]{:S(2)}) copy-start(bf16[1296,1296]{1,0:T(8,128)(2,1)} %get-tuple-element.10.coup_hbm) | copy-start | bytes 10077700
  119.6 64.8 %copy-start.1 = (f32[1296,8]{1,0:T(8,128)S(1)}, f32[1296,8]{1,0:T(8,128)}, u32[]{:S(2)}) copy-start(f32[1296,8]{1,0:T(8,128)} %constant.4.clone.table_ref) | copy-start | bytes 124420
  119.6 64.8 %copy-start.3 = (f32[8,512]{1,0:T(8,128)S(1)}, f32[8,512]{1,0:T(8,128)}, u32[]{:S(2)}) copy-start(f32[8,512]{1,0:T(8,128)} %get-tuple-element.11.winds_ref) | copy-start | bytes 49156

commit v7 on v6

--- a/solution.py
+++ b/solution.py
@@ -446,99 +446,87 @@
         copy.wait()
 
 
-def scatter(plan, place_ref, came_ref, grid_ref, piece_refs, arrived):
+def scatter(plan, place_ref, came_ref, grid_ref, piece_ref, arrived):
     depth, tiles, tall, block = plan.depth, plan.tiles, plan.tall, plan.block
     blocks = plan.shares * tiles
-    sub = lax.broadcasted_iota(jnp.int32, (SUBS, LANES), 0)
-
-    def turn(i, piece_ref):
+
+    def turn(i):
         s, j = i // tiles, i % tiles
         values = came_ref[pl.ds(s * block + j, depth, stride=tiles), :]
         if tall > depth:
             values = jnp.concatenate([values, jnp.zeros((tall - depth, LANES), F32)], axis=0)
-        piece_ref[:, 0:tall] = values.T
-
-    def put(i, piece_ref):
-        for g in range(LANES // SUBS):
-            values = piece_ref[g * SUBS : (g + 1) * SUBS, :]
-            for t in range(SUBS):
-                spot = place_ref[i * LANES + g * SUBS + t]
-                pltpu.store(grid_ref.at[pl.ds(spot - t, SUBS), :], values, mask=sub == t)
-
-    even_ref, odd_ref = piece_refs
+        to = pl.ds(pl.multiple_of(i % 2 * LANES, LANES), LANES)
+        piece_ref[to, 0:tall] = values.T
+
+    def put(i):
+        base = i % 2 * LANES
+        for t in range(LANES):
+            spot = place_ref[i * LANES + t]
+            grid_ref[pl.ds(spot, 1), :] = piece_ref[pl.ds(base + t, 1), :]
+
     arrived(0)
-    turn(0, even_ref)
-    per = blocks // (2 * PARTS)
-
-    @pl.loop(0, PARTS)
-    def _(part):
-        @pl.loop(0, per)
-        def _(i):
-            at = (part * per + i) * 2
-            turn(at + 1, odd_ref)
-            put(at, even_ref)
-
-            @pl.when(jnp.logical_and(i == per - 1, part < PARTS - 1))
-            def _():
-                arrived(part + 1)
-
-            turn(jnp.minimum(at + 2, blocks - 1), even_ref)
-            put(at + 1, odd_ref)
-
-
-def gather(plan, place_ref, out_ref, grid_ref, piece_refs, finished):
+    turn(0)
+    per = blocks // PARTS
+
+    @pl.loop(0, blocks)
+    def _(i):
+        @pl.when(jnp.logical_and(i % per == per - 1, i < blocks - 1))
+        def _():
+            arrived(i // per + 1)
+
+        put(i)
+        turn(jnp.minimum(i + 1, blocks - 1))
+
+
+def gather(plan, place_ref, out_ref, grid_ref, piece_ref, finished):
     depth, tiles, tall = plan.depth, plan.tiles, plan.tall
     blocks = plan.shares * tiles
-    sub = lax.broadcasted_iota(jnp.int32, (SUBS, LANES), 0)
-
-    def turn(i, piece_ref):
+
+    def turn(i):
         s, j = i // tiles, i % tiles
-        turned = piece_ref[:, 0:tall].T
+        at = pl.ds(pl.multiple_of(i % 2 * LANES, LANES), LANES)
+        turned = piece_ref[at, 0:tall].T
         out_ref[pl.ds(s * plan.data + j, depth, stride=tiles), :] = turned[0:depth, :]
 
-    def get(i, piece_ref):
-        for g in range(LANES // SUBS):
-            first = i * LANES + g * SUBS
-            values = grid_ref[pl.ds(place_ref[first], SUBS), :]
-            for t in range(1, SUBS):
-                shifted = grid_ref[pl.ds(place_ref[first + t] - t, SUBS), :]
-                values = jnp.where(sub == t, shifted, values)
-            piece_ref[g * SUBS : (g + 1) * SUBS, :] = values
-
-    even_ref, odd_ref = piece_refs
-    get(0, even_ref)
-    per = blocks // (2 * PARTS)
-
-    @pl.loop(0, PARTS)
-    def _(part):
-        @pl.loop(0, per)
-        def _(i):
-            at = (part * per + i) * 2
-            get(at + 1, odd_ref)
-            turn(at, even_ref)
-            get(jnp.minimum(at + 2, blocks - 1), even_ref)
-            turn(at + 1, odd_ref)
-
-        finished(part)
-
-
-def spread_drift(plan, came_ref, piece_ref, wide_ref, drift_ref):
-    piece_ref[...] = jnp.zeros((LANES, LANES), F32)
+    def get(i, row):
+        base = i % 2 * LANES
+        for t in range(LANES):
+            spot = place_ref[row * LANES + t]
+            piece_ref[pl.ds(base + t, 1), :] = grid_ref[pl.ds(spot, 1), :]
+
+    get(0, 0)
+    per = blocks // PARTS
+
+    @pl.loop(0, blocks)
+    def _(i):
+        turn(i)
+        get(i + 1, jnp.minimum(i + 1, blocks - 1))
+
+        @pl.when(i % per == per - 1)
+        def _():
+            finished(i // per)
+
+
+def spread_drift(plan, came_ref, piece_ref, drift_ref):
+    held, turned = piece_ref.at[0:LANES], piece_ref.at[LANES : 2 * LANES]
+    held[...] = jnp.zeros((LANES, LANES), F32)
     for s in range(plan.shares):
         first = s * plan.block + plan.data + plan.tiles
-        piece_ref[s * plan.force : (s + 1) * plan.force, :] = came_ref[
-            first : first + plan.force, :
-        ]
-    turned = (courant_scale * piece_ref[...]).T
+        held[s * plan.force : (s + 1) * plan.force, :] = came_ref[first : first + plan.force, :]
+    turned[...] = (courant_scale * held[...]).T
     groups = plan.vregs // COARSE
+    ordered = jnp.concatenate(
+        [
+            turned[pl.ds(a * groups * SUBS + m, SUBS, stride=groups), :]
+            for a in range(LANES // (groups * SUBS))
+            for m in range(groups)
+        ],
+        axis=0,
+    )
     for q in range(plan.shares * plan.force):
-        wide_ref[...] = jnp.broadcast_to(turned[:, q : q + 1], (LANES, LANES))
-        for a in range(LANES // (groups * SUBS)):
-            for m in range(groups):
-                to = q * LANES + (a * groups + m) * SUBS
-                drift_ref[to : to + SUBS, :] = wide_ref[
-                    pl.ds(a * groups * SUBS + m, SUBS, stride=groups), :
-                ]
+        drift_ref[q * LANES : (q + 1) * LANES, :] = jnp.broadcast_to(
+            ordered[:, q : q + 1], (LANES, LANES)
+        )
 
 
 def sweep(plan, drift_ref, speed_ref, one_ref, two_ref):
@@ -595,13 +583,13 @@
             return above, here
 
         zero = [jnp.zeros((SUBS, LANES), F32)] * COARSE
-        lax.fori_loop(0, plan.coarse_rows, coarse, (zero, along(0, courant(0, 0))))
+        lax.fori_loop(0, plan.coarse_rows, coarse, (zero, along(0, courant(0, 0))), unroll=2)
 
 
 def middle_kernel(
     plan,
     place_ref, speed_ref, came_hbm, out_hbm,
-    came_ref, out_ref, one_ref, two_ref, drift_ref, even_ref, odd_ref, in_sems, out_sems,
+    came_ref, out_ref, one_ref, two_ref, drift_ref, piece_ref, in_sems, out_sems,
 ):
     shares, block, data = plan.shares, plan.block, plan.data
     part_in, part_out = shares // PARTS * block, shares // PARTS * data
@@ -622,12 +610,11 @@
         at = pl.ds(pl.multiple_of(i * LANES, LANES), LANES)
         one_ref[at, :] = jnp.full((LANES, LANES), DRY, F32)
 
-    pieces = (even_ref, odd_ref)
-    scatter(plan, place_ref, came_ref, one_ref, pieces, lambda part: copy_in(part).wait())
-    spread_drift(plan, came_ref, even_ref, odd_ref, drift_ref)
+    scatter(plan, place_ref, came_ref, one_ref, piece_ref, lambda part: copy_in(part).wait())
+    spread_drift(plan, came_ref, piece_ref, drift_ref)
     me = lax.axis_index("space")
     sweep(plan, drift_ref, speed_ref.at[me], one_ref, two_ref)
-    gather(plan, place_ref, out_ref, two_ref, pieces, lambda part: copy_out(part).start())
+    gather(plan, place_ref, out_ref, two_ref, piece_ref, lambda part: copy_out(part).start())
     for part in range(PARTS):
         copy_out(part).wait()
 
@@ -726,8 +713,7 @@
             pltpu.VMEM((size, LANES), F32),
             pltpu.VMEM((size, LANES), F32),
             pltpu.VMEM((2 * points, LANES), F32),
-            pltpu.VMEM((LANES, LANES), F32),
-            pltpu.VMEM((LANES, LANES), F32),
+            pltpu.VMEM((2 * LANES, LANES), F32),
             pltpu.SemaphoreType.DMA((PARTS,)),
             pltpu.SemaphoreType.DMA((PARTS,)),
         ],

time: 194 us -> 198 us (1.021)
  Pallas kernels: 50.8 us -> 54.5 us
    pallas_call x1, Pallas kernels: 27.4 us -> 31.1 us  [on_spectrum(): kernel(functools.partial(middle_kernel, plan), flops=24 * size * LANES, t...]
where the time goes in v7:
time: 198 us; the launch traced here: 194 us
  blocking collectives  132 us (67%)
  Pallas kernels  54.5 us (28%)
  starting transfers between devices  6.55 us (3%)
    all_to_all x1, blocking collectives, on_spectrum(): lax.all_to_all(sent.reshape(shares, plan.block, LANES), 'space', 0, 0, ti...  67.5 us
    all_to_all x1, blocking collectives, on_spectrum(): lax.all_to_all(swept.reshape(shares, depth, tiles, LANES), 'space', 0, 0,...  64.8 us
    pallas_call x1, Pallas kernels, on_spectrum(): kernel(functools.partial(middle_kernel, plan), flops=24 * size * LANES, t...  31.1 us
    pallas_call x1, Pallas kernels, on_spectrum(): kernel(functools.partial(first_kernel, plan), **h_cost, out_shape=[jax.Sh...  8.54 us
    pallas_call x1, Pallas kernels, on_spectrum(): kernel(functools.partial(ready_kernel, plan), flops=0, traffic=12 * rows...  7.43 us
    all_to_all x1, starting transfers between devices, on_spectrum(): parcel = lax.all_to_all(parcel, 'space', 0, 0, tiled=True)  6.55 us
    pallas_call x1, Pallas kernels, on_spectrum(): kernel(functools.partial(last_kernel, plan), vmem=24 * MIB, **h_cost, out...  6.05 us
  transfers between devices with their start and end apart: 1, of which 0 were waited for; matrix products, arithmetic and copies ran while one was open for 0% of the time, Pallas kernels for 4%

profile of v7, /device:TPU:15, one launch (start us, length us, event | category | flops | bytes accessed | tf_op | source)
XLA Modules:
  0.0 194.2 jit_solution(5793281579032501495)
XLA Ops:
  0.0 1.5 pack.1
  1.5 6.6 %all-to-all-start = ((f32[16,2,1152]{2,1,0:T(2,128)}), f32[16,2,1152]{2,1,0:T(2,128)S(1)}, u32[]{:S(2)}, u32[]{:S(2)}) async-start(f32[16,2,1152]{2,1,0:T(2,128)} %pack.1), calls=%async_computation | async-start | bytes 294912 | tf_op jit(solution)/shard_map/all_to_all | solution.py:664
  8.0 7.4 %ready.1 = (bf16[1296,1296]{1,0:T(8,128)(2,1)}, f32[1296,512]{1,0:T(8,128)}) custom-call(f32[1296,8]{1,0:T(8,128)} %constant.4.clone.table_ref, bf16[1296,1296]{1,0:T(8,128)(2,1)} %coup_hbm.1, f32[1296,512]{1,0:T(8,128)} %bitcast.13), custom_call_target="tpu_custom_call" | custom-call | bytes 7962624 | tf_op jit(solution)/shard_map/ready/pallas_call | solution.py:673
  15.5 0.0 all-to-all-done.parcel_ref
  15.5 0.0 copy-start.4
  15.5 0.6 copy-done.4
  16.1 8.5 %first_half.1 = (f32[8,512]{1,0:T(8,128)}, f32[5376,128]{1,0:T(8,128)}) custom-call(s32[1,16]{1,0:T(1,128)} %count_ref.1, s32[1,512]{1,0:T(1,128)} %bitcast.14, f32[16,2,1152]{2,1,0:T(2,128)} %copy-done.4, s32[1,16,64]{2,1,0:T(8,128)} %send_ref.1, f32[1296,8]{1,0:T(8,128)} %constant.4.clone.table_ref, f32[1296,512]{1,0:T(8,128)} %get-tuple-element.9.base_hbm, ...), custom_call_target="tpu_custom_call" | custom-call | flops 1719926784 | bytes 7962624 | tf_op jit(solution)/shard_map/first_half/pallas_call | solution.py:684
  24.7 0.0 copy-start.2
  24.7 67.5 %all_to_all.15 = f32[16,336,128]{2,1,0:T(8,128)S(1)} all-to-all(f32[16,336,128]{2,1,0:T(8,128)} %bitcast.12), channel_id=1, replica_groups=mesh['members'=2,'space'=16] {'space'}, dimensions={0} | all-to-all | bytes 5505024 | tf_op jit(solution)/shard_map/all_to_all | solution.py:700
  92.2 0.0 copy-done.2
  92.2 31.1 %sweeps.1 = f32[5184,128]{1,0:T(8,128)S(1)} custom-call(s32[8192]{0:T(1024)S(1)} %bitcast.11, f32[16,8,128]{2,1,0:T(8,128)S(1)} %copy-done.2, f32[5376,128]{1,0:T(8,128)S(1)} %bitcast.8), custom_call_target="tpu_custom_call" | custom-call | flops 51118080 | bytes 5308416 | tf_op jit(solution)/shard_map/sweeps/pallas_call | solution.py:704
  123.3 0.0 copy-start
  123.3 0.0 copy-start.1
  123.3 0.0 copy-start.3
  123.3 64.8 %all_to_all.16 = f32[16,81,4,128]{3,2,1,0:T(4,128)S(1)} all-to-all(f32[16,81,4,128]{3,2,1,0:T(4,128)S(1)} %bitcast.10), channel_id=1, replica_groups=mesh['members'=2,'space'=16] {'space'}, dimensions={0} | all-to-all | bytes 5308416 | tf_op jit(solution)/shard_map/all_to_all | solution.py:722
  188.1 0.0 copy-done
  188.1 0.0 copy-done.1
  188.1 0.0 copy-done.3
  188.1 6.0 %last_half.1 = f32[1296,512]{1,0:T(8,128)} custom-call(f32[8,512]{1,0:T(8,128)S(1)} %copy-done.3, f32[1296,8]{1,0:T(8,128)S(1)} %copy-done.1, f32[5184,128]{1,0:T(8,128)S(1)} %bitcast.9, bf16[1296,1296]{1,0:T(8,128)(2,1)S(1)} %copy-done), custom_call_target="tpu_custom_call" | custom-call | flops 1719926784 | bytes 7962624 | tf_op jit(solution)/shard_map/last_half/pallas_call | solution.py:725
  (1 shorter events, 0.0 us)
Async XLA Ops:
  1.5 14.0 %all-to-all-start = ((f32[16,2,1152]{2,1,0:T(2,128)}), f32[16,2,1152]{2,1,0:T(2,128)S(1)}, u32[]{:S(2)}, u32[]{:S(2)}) async-start(f32[16,2,1152]{2,1,0:T(2,128)} %pack.1), calls=%async_computation | async-start | bytes 294912 | tf_op jit(solution)/shard_map/all_to_all | solution.py:664
  15.5 0.7 copy-start.4
  24.7 67.5 %copy-start.2 = (f32[16,8,128]{2,1,0:T(8,128)S(1)}, f32[16,8,128]{2,1,0:T(8,128)}, u32[]{:S(2)}) copy-start(f32[16,8,128]{2,1,0:T(8,128)} %constant.5.clone.speed_ref) | copy-start | bytes 196612
  123.3 64.8 %copy-start = (bf16[1296,1296]{1,0:T(8,128)(2,1)S(1)}, bf16[1296,1296]{1,0:T(8,128)(2,1)}, u32[]{:S(2)}) copy-start(bf16[1296,1296]{1,0:T(8,128)(2,1)} %get-tuple-element.10.coup_hbm) | copy-start | bytes 10077700
  123.3 64.8 %copy-start.1 = (f32[1296,8]{1,0:T(8,128)S(1)}, f32[1296,8]{1,0:T(8,128)}, u32[]{:S(2)}) copy-start(f32[1296,8]{1,0:T(8,128)} %constant.4.clone.table_ref) | copy-start | bytes 124420
  123.3 64.8 %copy-start.3 = (f32[8,512]{1,0:T(8,128)S(1)}, f32[8,512]{1,0:T(8,128)}, u32[]{:S(2)}) copy-start(f32[8,512]{1,0:T(8,128)} %get-tuple-element.11.winds_ref) | copy-start | bytes 49156

commit v8 on v6

--- a/solution.py
+++ b/solution.py
@@ -299,8 +299,8 @@
 
 
 def ready_kernel(
-    plan, table_ref, coup_hbm, energy_hbm, turned_hbm, base_hbm,
-    coup_ref, turned_ref, energy_ref, unit_ref, sems, coup_sem, out_sems,
+    plan, table_ref, coup_hbm, energy_hbm, turned_ref, base_ref,
+    coup_ref, energy_ref, unit_ref, sems, coup_sem,
 ):
     spec = plan.spec
     get = pltpu.make_async_copy(coup_hbm, coup_ref, coup_sem)
@@ -311,18 +311,12 @@
     @pl.loop(0, spec // PERIOD)
     def _(i):
         at = pl.ds(pl.multiple_of(i * PERIOD, PERIOD), PERIOD)
-        energy_ref[at, :] = energy_ref[at, :] * unit_ref[...]
-
-    put_base = pltpu.make_async_copy(energy_ref, base_hbm, out_sems.at[0])
-    put_base.start()
+        base_ref[at, :] = energy_ref[at, :] * unit_ref[...]
+
     get.wait()
     for first in range(0, spec, LANES):
         at = slice(first, min(first + LANES, spec))
         turned_ref[at, :] = coup_ref[:, at].T
-    put_turned = pltpu.make_async_copy(turned_ref, turned_hbm, out_sems.at[1])
-    put_turned.start()
-    put_base.wait()
-    put_turned.wait()
 
 
 def own_places(plan, parcel_ref, send_ref, count_ref):
@@ -344,20 +338,18 @@
         found = jnp.zeros((LANES, cap), F32)
         for b in range(plan.shares):
             found += jnp.where(names[b] == own, place[b : b + 1, :], 0.0)
-        found = jnp.broadcast_to(jnp.sum(found, axis=1, keepdims=True), (LANES, LANES))
-        rows.append(found.T[0:1, :])
+        found = jnp.broadcast_to(jnp.sum(found, axis=1, keepdims=True), (LANES, LANES)).T
+        shift = lax.rem(lax.broadcasted_iota(jnp.int32, (1, LANES), 1), SUBS).astype(F32)
+        rows.append(found[0:1, :] - shift)
     return rows
 
 
 def first_kernel(
     plan,
-    count_ref, cp_ref, parcel_ref, send_ref, table_ref, base_hbm, coup_hbm, winds_ref, out_hbm,
-    out_ref, buf_ref, base_ref, coup_ref, locb_ref, sems, coup_sem, out_sems,
+    count_ref, cp_ref, parcel_ref, send_ref, table_ref, base_ref, coup_ref, winds_ref, out_hbm,
+    out_ref, buf_ref, loc_ref, locb_ref, out_sems,
 ):
     tiles, shares, points, block, data = plan.tiles, plan.shares, plan.points, plan.block, plan.data
-    arrive = fetch(base_hbm, base_ref, sems, plan.thirds)
-    get = pltpu.make_async_copy(coup_hbm, coup_ref, coup_sem)
-    get.start()
     width = plan.force * LANES
     current = jnp.sum(parcel_ref[:, :, points : points + width], axis=0)
     spare = own_places(plan, parcel_ref, send_ref, count_ref)
@@ -369,19 +361,15 @@
     east, north = cell_winds(jnp.sum(parcel_ref[:, :, 0:points], axis=0), cp_ref[...])
     winds_ref[0:1, :] = east
     winds_ref[1:2, :] = north
-    per = plan.tall_step // PERIOD
-    for q in range(plan.thirds):
-        arrive[q].wait()
-
-        @pl.loop(q * per, (q + 1) * per)
-        def _(i):
-            first = pl.multiple_of(i * PERIOD, PERIOD)
-            at = pl.ds(first, PERIOD)
-            local = base_ref[at, :] * growth_step(first, east, north, table_ref)
-            base_ref[at, :] = local
-            locb_ref[at, :] = local.astype(BF16)
-
-    get.wait()
+
+    @pl.loop(0, plan.spec // PERIOD)
+    def _(i):
+        first = pl.multiple_of(i * PERIOD, PERIOD)
+        at = pl.ds(first, PERIOD)
+        local = base_ref[at, :] * growth_step(first, east, north, table_ref)
+        loc_ref[at, :] = local
+        locb_ref[at, :] = local.astype(BF16)
+
     sent, copies = [0], []
 
     def store(first, values):
@@ -399,7 +387,7 @@
         copies[-1].start()
         sent[0] = upto
 
-    coupled(plan, coup_ref, base_ref, locb_ref, store)
+    coupled(plan, coup_ref, loc_ref, locb_ref, store)
     for copy in copies:
         copy.wait()
 
@@ -463,7 +451,7 @@
             values = piece_ref[g * SUBS : (g + 1) * SUBS, :]
             for t in range(SUBS):
                 spot = place_ref[i * LANES + g * SUBS + t]
-                pltpu.store(grid_ref.at[pl.ds(spot - t, SUBS), :], values, mask=sub == t)
+                pltpu.store(grid_ref.at[pl.ds(spot, SUBS), :], values, mask=sub == t)
 
     even_ref, odd_ref = piece_refs
     arrived(0)
@@ -501,7 +489,7 @@
             first = i * LANES + g * SUBS
             values = grid_ref[pl.ds(place_ref[first], SUBS), :]
             for t in range(1, SUBS):
-                shifted = grid_ref[pl.ds(place_ref[first + t] - t, SUBS), :]
+                shifted = grid_ref[pl.ds(place_ref[first + t], SUBS), :]
                 values = jnp.where(sub == t, shifted, values)
             piece_ref[g * SUBS : (g + 1) * SUBS, :] = values
 
@@ -522,23 +510,25 @@
         finished(part)
 
 
-def spread_drift(plan, came_ref, piece_ref, wide_ref, drift_ref):
-    piece_ref[...] = jnp.zeros((LANES, LANES), F32)
+def spread_drift(plan, came_ref, held, turned, drift_ref):
+    held[...] = jnp.zeros((LANES, LANES), F32)
     for s in range(plan.shares):
         first = s * plan.block + plan.data + plan.tiles
-        piece_ref[s * plan.force : (s + 1) * plan.force, :] = came_ref[
-            first : first + plan.force, :
-        ]
-    turned = (courant_scale * piece_ref[...]).T
+        held[s * plan.force : (s + 1) * plan.force, :] = came_ref[first : first + plan.force, :]
+    turned[...] = (courant_scale * held[...]).T
     groups = plan.vregs // COARSE
+    ordered = jnp.concatenate(
+        [
+            turned[pl.ds(a * groups * SUBS + m, SUBS, stride=groups), :]
+            for a in range(LANES // (groups * SUBS))
+            for m in range(groups)
+        ],
+        axis=0,
+    )
     for q in range(plan.shares * plan.force):
-        wide_ref[...] = jnp.broadcast_to(turned[:, q : q + 1], (LANES, LANES))
-        for a in range(LANES // (groups * SUBS)):
-            for m in range(groups):
-                to = q * LANES + (a * groups + m) * SUBS
-                drift_ref[to : to + SUBS, :] = wide_ref[
-                    pl.ds(a * groups * SUBS + m, SUBS, stride=groups), :
-                ]
+        drift_ref[q * LANES : (q + 1) * LANES, :] = jnp.broadcast_to(
+            ordered[:, q : q + 1], (LANES, LANES)
+        )
 
 
 def sweep(plan, drift_ref, speed_ref, one_ref, two_ref):
@@ -595,7 +585,7 @@
             return above, here
 
         zero = [jnp.zeros((SUBS, LANES), F32)] * COARSE
-        lax.fori_loop(0, plan.coarse_rows, coarse, (zero, along(0, courant(0, 0))))
+        lax.fori_loop(0, plan.coarse_rows, coarse, (zero, along(0, courant(0, 0))), unroll=2)
 
 
 def middle_kernel(
@@ -622,12 +612,11 @@
         at = pl.ds(pl.multiple_of(i * LANES, LANES), LANES)
         one_ref[at, :] = jnp.full((LANES, LANES), DRY, F32)
 
-    pieces = (even_ref, odd_ref)
-    scatter(plan, place_ref, came_ref, one_ref, pieces, lambda part: copy_in(part).wait())
+    scatter(plan, place_ref, came_ref, one_ref, (even_ref, odd_ref), lambda part: copy_in(part).wait())
     spread_drift(plan, came_ref, even_ref, odd_ref, drift_ref)
     me = lax.axis_index("space")
     sweep(plan, drift_ref, speed_ref.at[me], one_ref, two_ref)
-    gather(plan, place_ref, out_ref, two_ref, pieces, lambda part: copy_out(part).start())
+    gather(plan, place_ref, out_ref, two_ref, (even_ref, odd_ref), lambda part: copy_out(part).start())
     for part in range(PARTS):
         copy_out(part).wait()
 
@@ -685,28 +674,28 @@
     dma = pltpu.SemaphoreType.DMA
     coup, base = kernel(
         functools.partial(ready_kernel, plan),
-        flops=0, traffic=12 * rows * spec,
+        flops=0, traffic=12 * rows * spec, vmem=20 * MIB,
         out_shape=[
             jax.ShapeDtypeStruct((spec, spec), BF16), jax.ShapeDtypeStruct((spec, rows), F32)
         ],
         in_specs=[VMEM, ANY, ANY],
-        out_specs=[ANY, ANY],
-        scratch_shapes=[square, square, whole, unit, dma((plan.thirds,)), dma, dma((2,))],
+        out_specs=[VMEM, VMEM],
+        scratch_shapes=[square, whole, unit, dma((plan.thirds,)), dma],
         name="ready",
     )(table, coupling, spectra.T)
     winds, sent = kernel(
         functools.partial(first_kernel, plan),
-        **h_cost,
+        vmem=24 * MIB, **h_cost,
         out_shape=[
             jax.ShapeDtypeStruct((SUBS, rows), F32),
             jax.ShapeDtypeStruct((shares * plan.block, LANES), F32),
         ],
-        in_specs=[SMEM] + [VMEM] * 4 + [ANY] * 2,
+        in_specs=[SMEM] + [VMEM] * 6,
         out_specs=[VMEM, ANY],
         scratch_shapes=[
             pltpu.VMEM((shares * plan.block, LANES), F32),
             pltpu.VMEM((data_rows, LANES), F32),
-            whole, square, rounded, dma((plan.thirds,)), dma, dma((plan.thirds,)),
+            whole, rounded, dma((plan.thirds,)),
         ],
         name="first_half",
     )(send_count, cp, parcel, send_list, table, base, coup)

time: 194 us -> 194 us (level)
  local copies, waits for them, and re-layouts: 0.67 us -> 8.69 us
  Pallas kernels: 50.8 us -> 43.5 us
    unnamed x10 -> x22, local copies, waits for them, and re-layouts: 0.67 us -> 8.69 us
    pallas_call x1, Pallas kernels: 7.43 us -> 3.03 us  [on_spectrum(): kernel(functools.partial(ready_kernel, plan), flops=0, traffic=12 * rows...]
    pallas_call x1, Pallas kernels: 8.54 us -> 6.15 us  [on_spectrum(): kernel(functools.partial(first_kernel, plan), vmem=24 * MIB, **h_cost, ou...]
  transfers between devices with their start and end apart: 1 -> 1, of which waited for: 0 -> 0; matrix products, arithmetic and copies ran while one was open for 0% -> 0% of each run, Pallas kernels for 4% -> 2%
where the time goes in v8:
time: 194 us; the launch traced here: 191 us
  blocking collectives  132 us (68%)
  Pallas kernels  43.5 us (22%)
  local copies, waits for them, and re-layouts  8.69 us (4%)
  starting transfers between devices  6.55 us (3%)
    all_to_all x1, blocking collectives, on_spectrum(): lax.all_to_all(sent.reshape(shares, plan.block, LANES), 'space', 0, 0, ti...  67.3 us
    all_to_all x1, blocking collectives, on_spectrum(): lax.all_to_all(swept.reshape(shares, depth, tiles, LANES), 'space', 0, 0,...  64.8 us
    pallas_call x1, Pallas kernels, on_spectrum(): kernel(functools.partial(middle_kernel, plan), flops=24 * size * LANES, t...  26.8 us
    unnamed x22, local copies, waits for them, and re-layouts  8.69 us
    all_to_all x1, starting transfers between devices, on_spectrum(): parcel = lax.all_to_all(parcel, 'space', 0, 0, tiled=True)  6.55 us
    pallas_call x1, Pallas kernels, on_spectrum(): kernel(functools.partial(first_kernel, plan), vmem=24 * MIB, **h_cost, ou...  6.15 us
    pallas_call x1, Pallas kernels, on_spectrum(): kernel(functools.partial(last_kernel, plan), vmem=24 * MIB, **h_cost, out...  6.04 us
  transfers between devices with their start and end apart: 1, of which 0 were waited for; matrix products, arithmetic and copies ran while one was open for 0% of the time, Pallas kernels for 2%

profile of v8, /device:TPU:15, one launch (start us, length us, event | category | flops | bytes accessed | tf_op | source)
XLA Modules:
  0.0 191.0 jit_solution(3218377122259189237)
XLA Ops:
  0.0 1.5 pack.1
  1.5 6.6 %all-to-all-start = ((f32[16,2,1152]{2,1,0:T(2,128)}), f32[16,2,1152]{2,1,0:T(2,128)S(1)}, u32[]{:S(2)}, u32[]{:S(2)}) async-start(f32[16,2,1152]{2,1,0:T(2,128)} %pack.1), calls=%async_computation | async-start | bytes 294912 | tf_op jit(solution)/shard_map/all_to_all | solution.py:666
  8.0 0.0 copy-start.3
  8.1 1.1 copy-done.3
  9.1 0.0 copy-start.5
  9.1 2.0 %copy-done.5 = bf16[1296,1296]{1,0:T(8,128)(2,1)S(1)} copy-done((bf16[1296,1296]{1,0:T(8,128)(2,1)S(1)}, bf16[1296,1296]{1,0:T(8,128)(2,1)}, u32[]{:S(2)}) %copy-start.5) | copy-done | bytes 3359256
  11.2 0.0 copy-start.6
  11.2 1.7 copy-done.6
  12.9 0.0 copy-start.4
  12.9 0.0 copy-start.8
  12.9 0.0 copy-start.9
  12.9 0.0 copy-start.10
  12.9 3.0 %ready.1 = (bf16[1296,1296]{1,0:T(8,128)(2,1)S(1)}, f32[1296,512]{1,0:T(8,128)S(1)}) custom-call(f32[1296,8]{1,0:T(8,128)S(1)} %copy-done.3, bf16[1296,1296]{1,0:T(8,128)(2,1)S(1)} %copy-done.5, f32[1296,512]{1,0:T(8,128)S(1)} %bitcast.12), custom_call_target="tpu_custom_call" | custom-call | bytes 7962624 | tf_op jit(solution)/shard_map/ready/pallas_call | solution.py:675
  16.0 0.0 copy-start
  16.0 1.8 copy-done
  17.7 0.0 all-to-all-done.parcel_ref
  17.8 0.0 copy-done.4
  17.8 0.0 copy-done.8
  17.8 0.0 copy-done.9
  17.8 0.0 copy-done.10
  17.8 0.0 copy-start.1
  17.8 2.0 %copy-done.1 = bf16[1296,1296]{1,0:T(8,128)(2,1)S(1)} copy-done((bf16[1296,1296]{1,0:T(8,128)(2,1)S(1)}, bf16[1296,1296]{1,0:T(8,128)(2,1)}, u32[]{:S(2)}) %copy-start.1) | copy-done | bytes 3359256
  19.8 6.2 %first_half.1 = (f32[8,512]{1,0:T(8,128)S(1)}, f32[5376,128]{1,0:T(8,128)S(1)}) custom-call(s32[1,16]{1,0:T(1,128)S(1)} %copy-done.10, s32[1,512]{1,0:T(1,128)S(1)} %bitcast.14, f32[16,2,1152]{2,1,0:T(2,128)S(1)} %all-to-all-done.parcel_ref, s32[1,16,64]{2,1,0:T(8,128)S(1)} %copy-done.8, f32[1296,8]{1,0:T(8,128)S(1)} %copy-done.4, ...), custom_call_target="tpu_custom_call" | custom-call | flops 1719926784 | bytes 7962624 | tf_op jit(solution)/shard_map/first_half/pallas_call | solution.py:686
  26.0 0.0 copy-start.7
  26.0 67.3 %all_to_all.15 = f32[16,336,128]{2,1,0:T(8,128)S(1)} all-to-all(f32[16,336,128]{2,1,0:T(8,128)S(1)} %bitcast.11), channel_id=1, replica_groups=mesh['members'=2,'space'=16] {'space'}, dimensions={0} | all-to-all | bytes 5505024 | tf_op jit(solution)/shard_map/all_to_all | solution.py:702
  93.3 0.0 copy-done.7
  93.3 26.8 %sweeps.1 = f32[5184,128]{1,0:T(8,128)S(1)} custom-call(s32[8192]{0:T(1024)S(1)} %bitcast.13, f32[16,8,128]{2,1,0:T(8,128)S(1)} %copy-done.7, f32[5376,128]{1,0:T(8,128)S(1)} %bitcast.8), custom_call_target="tpu_custom_call" | custom-call | flops 51118080 | bytes 5308416 | tf_op jit(solution)/shard_map/sweeps/pallas_call | solution.py:706
  120.1 0.0 copy-start.2
  120.1 64.8 %all_to_all.16 = f32[16,81,4,128]{3,2,1,0:T(4,128)S(1)} all-to-all(f32[16,81,4,128]{3,2,1,0:T(4,128)S(1)} %bitcast.10), channel_id=1, replica_groups=mesh['members'=2,'space'=16] {'space'}, dimensions={0} | all-to-all | bytes 5308416 | tf_op jit(solution)/shard_map/all_to_all | solution.py:725
  184.9 0.0 copy-done.2
  184.9 6.0 %last_half.1 = f32[1296,512]{1,0:T(8,128)} custom-call(f32[8,512]{1,0:T(8,128)S(1)} %get-tuple-element.11.winds_ref, f32[1296,8]{1,0:T(8,128)S(1)} %copy-done.4, f32[5184,128]{1,0:T(8,128)S(1)} %bitcast.9, bf16[1296,1296]{1,0:T(8,128)(2,1)S(1)} %copy-done.2), custom_call_target="tpu_custom_call" | custom-call | flops 1719926784 | bytes 7962624 | tf_op jit(solution)/shard_map/last_half/pallas_call | solution.py:728
  (1 shorter events, 0.0 us)
Async XLA Ops:
  1.5 16.3 %all-to-all-start = ((f32[16,2,1152]{2,1,0:T(2,128)}), f32[16,2,1152]{2,1,0:T(2,128)S(1)}, u32[]{:S(2)}, u32[]{:S(2)}) async-start(f32[16,2,1152]{2,1,0:T(2,128)} %pack.1), calls=%async_computation | async-start | bytes 294912 | tf_op jit(solution)/shard_map/all_to_all | solution.py:666
  8.0 1.1 copy-start.3
  9.1 2.0 %copy-start.5 = (bf16[1296,1296]{1,0:T(8,128)(2,1)S(1)}, bf16[1296,1296]{1,0:T(8,128)(2,1)}, u32[]{:S(2)}) copy-start(bf16[1296,1296]{1,0:T(8,128)(2,1)} %coup_hbm.1) | copy-start | bytes 10077700
  11.2 1.7 copy-start.6
  12.9 4.8 %copy-start.4 = (f32[1296,8]{1,0:T(8,128)S(1)}, f32[1296,8]{1,0:T(8,128)}, u32[]{:S(2)}) copy-start(f32[1296,8]{1,0:T(8,128)} %constant.4.clone.table_ref) | copy-start | bytes 124420
  12.9 4.8 %copy-start.8 = (s32[1,16,64]{2,1,0:T(8,128)S(1)}, s32[1,16,64]{2,1,0:T(8,128)}, u32[]{:S(2)}) copy-start(s32[1,16,64]{2,1,0:T(8,128)} %send_ref.1) | copy-start | bytes 12292
  12.9 4.8 %copy-start.9 = (s32[512]{0:T(512)S(1)}, s32[512]{0:T(512)}, u32[]{:S(2)}) copy-start(s32[512]{0:T(512)} %param.16) | copy-start | bytes 6148
  12.9 4.9 %copy-start.10 = (s32[1,16]{1,0:T(1,128)S(1)}, s32[1,16]{1,0:T(1,128)}, u32[]{:S(2)}) copy-start(s32[1,16]{1,0:T(1,128)} %count_ref.1) | copy-start | bytes 196
  16.0 1.8 copy-start
  17.8 2.0 %copy-start.1 = (bf16[1296,1296]{1,0:T(8,128)(2,1)S(1)}, bf16[1296,1296]{1,0:T(8,128)(2,1)}, u32[]{:S(2)}) copy-start(bf16[1296,1296]{1,0:T(8,128)(2,1)} %copy-done) | copy-start | bytes 10077700
  26.0 67.3 %copy-start.7 = (f32[16,8,128]{2,1,0:T(8,128)S(1)}, f32[16,8,128]{2,1,0:T(8,128)}, u32[]{:S(2)}) copy-start(f32[16,8,128]{2,1,0:T(8,128)} %constant.5.clone.speed_ref) | copy-start | bytes 196612
  120.1 64.8 %copy-start.2 = (bf16[1296,1296]{1,0:T(8,128)(2,1)S(1)}, bf16[1296,1296]{1,0:T(8,128)(2,1)}, u32[]{:S(2)}) copy-start(bf16[1296,1296]{1,0:T(8,128)(2,1)} %copy-done) | copy-start | bytes 10077700

commit v9 on v8

--- a/solution.py
+++ b/solution.py
@@ -206,7 +206,6 @@
         self.data = self.depth * self.tiles
         self.force = 2 * points // (LANES * shares)
         self.block = ceil_to(self.data + self.tiles + self.force, SUBS)
-        self.tall = ceil_to(self.depth, SUBS)
         self.strip = strip_rows * cols
         self.grid_rows = strip_rows * shares
         self.coarse_rows = self.grid_rows // COARSE
@@ -299,24 +298,29 @@
 
 
 def ready_kernel(
-    plan, table_ref, coup_hbm, energy_hbm, turned_ref, base_ref,
-    coup_ref, energy_ref, unit_ref, sems, coup_sem,
+    plan, table_ref, coup_hbm, energy_hbm, unit_ref, turned_hbm,
+    coup_ref, turned_ref, energy_ref, sems, coup_sem, out_sems,
 ):
     spec = plan.spec
+    arrive = fetch(energy_hbm, energy_ref, sems, plan.thirds)
     get = pltpu.make_async_copy(coup_hbm, coup_ref, coup_sem)
     get.start()
-    arrive = fetch(energy_hbm, energy_ref, sems, plan.thirds)
     unit_loss(plan, lambda first, count: energy_ref[pl.ds(first, count), :], arrive, table_ref, unit_ref)
-
-    @pl.loop(0, spec // PERIOD)
-    def _(i):
-        at = pl.ds(pl.multiple_of(i * PERIOD, PERIOD), PERIOD)
-        base_ref[at, :] = energy_ref[at, :] * unit_ref[...]
-
     get.wait()
+    copies, wide = [], 3 * LANES
     for first in range(0, spec, LANES):
         at = slice(first, min(first + LANES, spec))
         turned_ref[at, :] = coup_ref[:, at].T
+        if at.stop % wide == 0 or at.stop == spec:
+            done = slice((at.stop - 1) // wide * wide, at.stop)
+            copies.append(
+                pltpu.make_async_copy(
+                    turned_ref.at[done, :], turned_hbm.at[done, :], out_sems.at[len(copies)]
+                )
+            )
+            copies[-1].start()
+    for copy in copies:
+        copy.wait()
 
 
 def own_places(plan, parcel_ref, send_ref, count_ref):
@@ -346,10 +350,13 @@
 
 def first_kernel(
     plan,
-    count_ref, cp_ref, parcel_ref, send_ref, table_ref, base_ref, coup_ref, winds_ref, out_hbm,
-    out_ref, buf_ref, loc_ref, locb_ref, out_sems,
+    count_ref, cp_ref, parcel_ref, send_ref, table_ref, unit_ref, energy_hbm, coup_hbm, winds_ref, out_hbm,
+    out_ref, buf_ref, loc_ref, coup_ref, locb_ref, sems, coup_sem, out_sems,
 ):
     tiles, shares, points, block, data = plan.tiles, plan.shares, plan.points, plan.block, plan.data
+    arrive = fetch(energy_hbm, loc_ref, sems, plan.thirds)
+    get = pltpu.make_async_copy(coup_hbm, coup_ref, coup_sem)
+    get.start()
     width = plan.force * LANES
     current = jnp.sum(parcel_ref[:, :, points : points + width], axis=0)
     spare = own_places(plan, parcel_ref, send_ref, count_ref)
@@ -361,15 +368,19 @@
     east, north = cell_winds(jnp.sum(parcel_ref[:, :, 0:points], axis=0), cp_ref[...])
     winds_ref[0:1, :] = east
     winds_ref[1:2, :] = north
-
-    @pl.loop(0, plan.spec // PERIOD)
-    def _(i):
-        first = pl.multiple_of(i * PERIOD, PERIOD)
-        at = pl.ds(first, PERIOD)
-        local = base_ref[at, :] * growth_step(first, east, north, table_ref)
-        loc_ref[at, :] = local
-        locb_ref[at, :] = local.astype(BF16)
-
+    per = plan.tall_step // PERIOD
+    for q in range(plan.thirds):
+        arrive[q].wait()
+
+        @pl.loop(q * per, (q + 1) * per)
+        def _(i):
+            first = pl.multiple_of(i * PERIOD, PERIOD)
+            at = pl.ds(first, PERIOD)
+            local = loc_ref[at, :] * unit_ref[...] * growth_step(first, east, north, table_ref)
+            loc_ref[at, :] = local
+            locb_ref[at, :] = local.astype(BF16)
+
+    get.wait()
     sent, copies = [0], []
 
     def store(first, values):
@@ -434,17 +445,28 @@
         copy.wait()
 
 
-def scatter(plan, place_ref, came_ref, grid_ref, piece_refs, arrived):
-    depth, tiles, tall, block = plan.depth, plan.tiles, plan.tall, plan.block
+def turned_block(values, one_ref):
+    high = values.astype(BF16)
+    low = (values - high.astype(F32)).astype(BF16)
+    return lax.dot_general(
+        one_ref[...],
+        jnp.concatenate([high, low], axis=1),
+        (((1,), (1,)), ((), ())),
+        preferred_element_type=F32,
+    )
+
+
+def scatter(plan, place_ref, came_ref, grid_ref, piece_refs, eye_ref, arrived):
+    depth, tiles, block = plan.depth, plan.tiles, plan.block
     blocks = plan.shares * tiles
     sub = lax.broadcasted_iota(jnp.int32, (SUBS, LANES), 0)
 
     def turn(i, piece_ref):
         s, j = i // tiles, i % tiles
         values = came_ref[pl.ds(s * block + j, depth, stride=tiles), :]
-        if tall > depth:
-            values = jnp.concatenate([values, jnp.zeros((tall - depth, LANES), F32)], axis=0)
-        piece_ref[:, 0:tall] = values.T
+        if LANES > depth:
+            values = jnp.concatenate([values, jnp.zeros((LANES - depth, LANES), F32)], axis=0)
+        piece_ref[...] = turned_block(values, eye_ref)
 
     def put(i, piece_ref):
         for g in range(LANES // SUBS):
@@ -474,14 +496,14 @@
             put(at + 1, odd_ref)
 
 
-def gather(plan, place_ref, out_ref, grid_ref, piece_refs, finished):
-    depth, tiles, tall = plan.depth, plan.tiles, plan.tall
+def gather(plan, place_ref, out_ref, grid_ref, piece_refs, eye_ref, finished):
+    depth, tiles = plan.depth, plan.tiles
     blocks = plan.shares * tiles
     sub = lax.broadcasted_iota(jnp.int32, (SUBS, LANES), 0)
 
     def turn(i, piece_ref):
         s, j = i // tiles, i % tiles
-        turned = piece_ref[:, 0:tall].T
+        turned = turned_block(piece_ref[...], eye_ref)
         out_ref[pl.ds(s * plan.data + j, depth, stride=tiles), :] = turned[0:depth, :]
 
     def get(i, piece_ref):
@@ -591,7 +613,7 @@
 def middle_kernel(
     plan,
     place_ref, speed_ref, came_hbm, out_hbm,
-    came_ref, out_ref, one_ref, two_ref, drift_ref, even_ref, odd_ref, in_sems, out_sems,
+    came_ref, out_ref, one_ref, two_ref, drift_ref, even_ref, odd_ref, eye_ref, in_sems, out_sems,
 ):
     shares, block, data = plan.shares, plan.block, plan.data
     part_in, part_out = shares // PARTS * block, shares // PARTS * data
@@ -606,17 +628,23 @@
 
     for part in range(PARTS):
         copy_in(part).start()
+
+    row = lax.broadcasted_iota(jnp.int32, (LANES, LANES), 0)
+    lane = lax.broadcasted_iota(jnp.int32, (LANES, LANES), 1)
+    eye = jnp.where(row == lane, 1.0, 0.0).astype(BF16)
+    eye_ref[:, 0:LANES] = eye
+    eye_ref[:, LANES : 2 * LANES] = eye
 
     @pl.loop(0, plan.size // LANES)
     def _(i):
         at = pl.ds(pl.multiple_of(i * LANES, LANES), LANES)
         one_ref[at, :] = jnp.full((LANES, LANES), DRY, F32)
 
-    scatter(plan, place_ref, came_ref, one_ref, (even_ref, odd_ref), lambda part: copy_in(part).wait())
+    scatter(plan, place_ref, came_ref, one_ref, (even_ref, odd_ref), eye_ref, lambda part: copy_in(part).wait())
     spread_drift(plan, came_ref, even_ref, odd_ref, drift_ref)
     me = lax.axis_index("space")
     sweep(plan, drift_ref, speed_ref.at[me], one_ref, two_ref)
-    gather(plan, place_ref, out_ref, two_ref, (even_ref, odd_ref), lambda part: copy_out(part).start())
+    gather(plan, place_ref, out_ref, two_ref, (even_ref, odd_ref), eye_ref, lambda part: copy_out(part).start())
     for part in range(PARTS):
         copy_out(part).wait()
 
@@ -672,33 +700,33 @@
     square = pltpu.VMEM((spec, spec), BF16)
     unit = pltpu.VMEM((PERIOD, rows), F32)
     dma = pltpu.SemaphoreType.DMA
-    coup, base = kernel(
+    unit_loss_held, coup = kernel(
         functools.partial(ready_kernel, plan),
-        flops=0, traffic=12 * rows * spec, vmem=20 * MIB,
+        flops=0, traffic=12 * rows * spec,
         out_shape=[
-            jax.ShapeDtypeStruct((spec, spec), BF16), jax.ShapeDtypeStruct((spec, rows), F32)
+            jax.ShapeDtypeStruct((PERIOD, rows), F32), jax.ShapeDtypeStruct((spec, spec), BF16)
         ],
         in_specs=[VMEM, ANY, ANY],
-        out_specs=[VMEM, VMEM],
-        scratch_shapes=[square, whole, unit, dma((plan.thirds,)), dma],
+        out_specs=[VMEM, ANY],
+        scratch_shapes=[square, square, whole, dma((plan.thirds,)), dma, dma((8,))],
         name="ready",
     )(table, coupling, spectra.T)
     winds, sent = kernel(
         functools.partial(first_kernel, plan),
-        vmem=24 * MIB, **h_cost,
+        **h_cost,
         out_shape=[
             jax.ShapeDtypeStruct((SUBS, rows), F32),
             jax.ShapeDtypeStruct((shares * plan.block, LANES), F32),
         ],
-        in_specs=[SMEM] + [VMEM] * 6,
+        in_specs=[SMEM] + [VMEM] * 5 + [ANY] * 2,
         out_specs=[VMEM, ANY],
         scratch_shapes=[
             pltpu.VMEM((shares * plan.block, LANES), F32),
             pltpu.VMEM((data_rows, LANES), F32),
-            whole, rounded, dma((plan.thirds,)),
+            whole, square, rounded, dma((plan.thirds,)), dma, dma((plan.thirds,)),
         ],
         name="first_half",
-    )(send_count, cp, parcel, send_list, table, base, coup)
+    )(send_count, cp, parcel, send_list, table, unit_loss_held, spectra.T, coup)
     came = lax.all_to_all(
         sent.reshape(shares, plan.block, LANES), "space", 0, 0, tiled=True
     )
@@ -717,6 +745,7 @@
             pltpu.VMEM((2 * points, LANES), F32),
             pltpu.VMEM((LANES, LANES), F32),
             pltpu.VMEM((LANES, LANES), F32),
+            pltpu.VMEM((LANES, 2 * LANES), BF16),
             pltpu.SemaphoreType.DMA((PARTS,)),
             pltpu.SemaphoreType.DMA((PARTS,)),
         ],

time: 194 us -> 201 us (1.036)
  Pallas kernels: 43.5 us -> 58.3 us
  local copies, waits for them, and re-layouts: 8.69 us -> 0.67 us
    pallas_call x1, Pallas kernels: 26.8 us -> 35.3 us  [on_spectrum(): kernel(functools.partial(middle_kernel, plan), flops=24 * size * LANES, t...]
    unnamed x22 -> x10, local copies, waits for them, and re-layouts: 8.69 us -> 0.67 us
    pallas_call x1, Pallas kernels: 3.03 us -> 6.88 us  [on_spectrum(): kernel(functools.partial(ready_kernel, plan), flops=0, traffic=12 * rows...]
    pallas_call x1, Pallas kernels: 6.15 us -> 8.61 us  [on_spectrum(): kernel(functools.partial(first_kernel, plan), **h_cost, out_shape=[jax.Sh...]
  transfers between devices with their start and end apart: 1 -> 1, of which waited for: 0 -> 0; matrix products, arithmetic and copies ran while one was open for 0% -> 0% of each run, Pallas kernels for 2% -> 3%
where the time goes in v9:
time: 201 us; the launch traced here: 198 us
  blocking collectives  132 us (66%)
  Pallas kernels  58.3 us (29%)
  starting transfers between devices  6.55 us (3%)
    all_to_all x1, blocking collectives, on_spectrum(): lax.all_to_all(sent.reshape(shares, plan.block, LANES), 'space', 0, 0, ti...  67.5 us
    all_to_all x1, blocking collectives, on_spectrum(): lax.all_to_all(swept.reshape(shares, depth, tiles, LANES), 'space', 0, 0,...  64.8 us
    pallas_call x1, Pallas kernels, on_spectrum(): kernel(functools.partial(middle_kernel, plan), flops=24 * size * LANES, t...  35.3 us
    pallas_call x1, Pallas kernels, on_spectrum(): kernel(functools.partial(first_kernel, plan), **h_cost, out_shape=[jax.Sh...  8.61 us
    pallas_call x1, Pallas kernels, on_spectrum(): kernel(functools.partial(ready_kernel, plan), flops=0, traffic=12 * rows...  6.88 us
    all_to_all x1, starting transfers between devices, on_spectrum(): parcel = lax.all_to_all(parcel, 'space', 0, 0, tiled=True)  6.55 us
    pallas_call x1, Pallas kernels, on_spectrum(): kernel(functools.partial(last_kernel, plan), vmem=24 * MIB, **h_cost, out...  6.05 us
  transfers between devices with their start and end apart: 1, of which 0 were waited for; matrix products, arithmetic and copies ran while one was open for 0% of the time, Pallas kernels for 3%

profile of v9, /device:TPU:15, one launch (start us, length us, event | category | flops | bytes accessed | tf_op | source)
XLA Modules:
  0.0 198.0 jit_solution(12104913421778293735)
XLA Ops:
  0.0 1.5 pack.1
  1.5 6.6 %all-to-all-start = ((f32[16,2,1152]{2,1,0:T(2,128)}), f32[16,2,1152]{2,1,0:T(2,128)S(1)}, u32[]{:S(2)}, u32[]{:S(2)}) async-start(f32[16,2,1152]{2,1,0:T(2,128)} %pack.1), calls=%async_computation | async-start | bytes 294912 | tf_op jit(solution)/shard_map/all_to_all | solution.py:694
  8.0 6.9 %ready.1 = (f32[144,512]{1,0:T(8,128)}, bf16[1296,1296]{1,0:T(8,128)(2,1)}) custom-call(f32[1296,8]{1,0:T(8,128)} %constant.4.clone.table_ref, bf16[1296,1296]{1,0:T(8,128)(2,1)} %coup_hbm.1, f32[1296,512]{1,0:T(8,128)} %bitcast.12), custom_call_target="tpu_custom_call" | custom-call | bytes 7962624 | tf_op jit(solution)/shard_map/ready/pallas_call | solution.py:703
  14.9 0.0 all-to-all-done.parcel_ref
  14.9 0.0 copy-start.4
  14.9 0.6 copy-done.4
  15.6 8.6 %first_half.1 = (f32[8,512]{1,0:T(8,128)}, f32[5376,128]{1,0:T(8,128)}) custom-call(s32[1,16]{1,0:T(1,128)} %count_ref.1, s32[1,512]{1,0:T(1,128)} %bitcast.15, f32[16,2,1152]{2,1,0:T(2,128)} %copy-done.4, s32[1,16,64]{2,1,0:T(8,128)} %send_ref.1, f32[1296,8]{1,0:T(8,128)} %constant.4.clone.table_ref, f32[144,512]{1,0:T(8,128)} %get-tuple-element.9.unit_ref, ...), custom_call_target="tpu_custom_call" | custom-call | flops 1719926784 | bytes 7962624 | tf_op jit(solution)/shard_map/first_half/pallas_call | solution.py:714
  24.2 0.0 copy-start.2
  24.2 67.5 %all_to_all.15 = f32[16,336,128]{2,1,0:T(8,128)S(1)} all-to-all(f32[16,336,128]{2,1,0:T(8,128)} %bitcast.14), channel_id=1, replica_groups=mesh['members'=2,'space'=16] {'space'}, dimensions={0} | all-to-all | bytes 5505024 | tf_op jit(solution)/shard_map/all_to_all | solution.py:730
  91.7 0.0 copy-done.2
  91.7 35.3 %sweeps.1 = f32[5184,128]{1,0:T(8,128)S(1)} custom-call(s32[8192]{0:T(1024)S(1)} %bitcast.11, f32[16,8,128]{2,1,0:T(8,128)S(1)} %copy-done.2, f32[5376,128]{1,0:T(8,128)S(1)} %bitcast.8), custom_call_target="tpu_custom_call" | custom-call | flops 51118080 | bytes 5308416 | tf_op jit(solution)/shard_map/sweeps/pallas_call | solution.py:734
  127.1 0.0 copy-start
  127.1 0.0 copy-start.1
  127.1 0.0 copy-start.3
  127.1 64.8 %all_to_all.16 = f32[16,81,4,128]{3,2,1,0:T(4,128)S(1)} all-to-all(f32[16,81,4,128]{3,2,1,0:T(4,128)S(1)} %bitcast.10), channel_id=1, replica_groups=mesh['members'=2,'space'=16] {'space'}, dimensions={0} | all-to-all | bytes 5308416 | tf_op jit(solution)/shard_map/all_to_all | solution.py:754
  191.9 0.0 copy-done
  191.9 0.0 copy-done.1
  191.9 0.0 copy-done.3
  191.9 6.0 %last_half.1 = f32[1296,512]{1,0:T(8,128)} custom-call(f32[8,512]{1,0:T(8,128)S(1)} %copy-done.3, f32[1296,8]{1,0:T(8,128)S(1)} %copy-done.1, f32[5184,128]{1,0:T(8,128)S(1)} %bitcast.9, bf16[1296,1296]{1,0:T(8,128)(2,1)S(1)} %copy-done), custom_call_target="tpu_custom_call" | custom-call | flops 1719926784 | bytes 7962624 | tf_op jit(solution)/shard_map/last_half/pallas_call | solution.py:757
  (1 shorter events, 0.0 us)
Async XLA Ops:
  1.5 13.4 %all-to-all-start = ((f32[16,2,1152]{2,1,0:T(2,128)}), f32[16,2,1152]{2,1,0:T(2,128)S(1)}, u32[]{:S(2)}, u32[]{:S(2)}) async-start(f32[16,2,1152]{2,1,0:T(2,128)} %pack.1), calls=%async_computation | async-start | bytes 294912 | tf_op jit(solution)/shard_map/all_to_all | solution.py:694
  14.9 0.7 copy-start.4
  24.2 67.5 %copy-start.2 = (f32[16,8,128]{2,1,0:T(8,128)S(1)}, f32[16,8,128]{2,1,0:T(8,128)}, u32[]{:S(2)}) copy-start(f32[16,8,128]{2,1,0:T(8,128)} %constant.5.clone.speed_ref) | copy-start | bytes 196612
  127.1 64.8 %copy-start = (bf16[1296,1296]{1,0:T(8,128)(2,1)S(1)}, bf16[1296,1296]{1,0:T(8,128)(2,1)}, u32[]{:S(2)}) copy-start(bf16[1296,1296]{1,0:T(8,128)(2,1)} %get-tuple-element.10.coup_hbm) | copy-start | bytes 10077700
  127.1 64.8 %copy-start.1 = (f32[1296,8]{1,0:T(8,128)S(1)}, f32[1296,8]{1,0:T(8,128)}, u32[]{:S(2)}) copy-start(f32[1296,8]{1,0:T(8,128)} %constant.4.clone.table_ref) | copy-start | bytes 124420
  127.1 64.8 %copy-start.3 = (f32[8,512]{1,0:T(8,128)S(1)}, f32[8,512]{1,0:T(8,128)}, u32[]{:S(2)}) copy-start(f32[8,512]{1,0:T(8,128)} %get-tuple-element.11.winds_ref) | copy-start | bytes 49156

commit v10 on v9

--- a/solution.py
+++ b/solution.py
@@ -206,6 +206,7 @@
         self.data = self.depth * self.tiles
         self.force = 2 * points // (LANES * shares)
         self.block = ceil_to(self.data + self.tiles + self.force, SUBS)
+        self.tall = ceil_to(self.depth, SUBS)
         self.strip = strip_rows * cols
         self.grid_rows = strip_rows * shares
         self.coarse_rows = self.grid_rows // COARSE
@@ -445,91 +446,60 @@
         copy.wait()
 
 
-def turned_block(values, one_ref):
-    high = values.astype(BF16)
-    low = (values - high.astype(F32)).astype(BF16)
-    return lax.dot_general(
-        one_ref[...],
-        jnp.concatenate([high, low], axis=1),
-        (((1,), (1,)), ((), ())),
-        preferred_element_type=F32,
-    )
-
-
-def scatter(plan, place_ref, came_ref, grid_ref, piece_refs, eye_ref, arrived):
-    depth, tiles, block = plan.depth, plan.tiles, plan.block
-    blocks = plan.shares * tiles
+def scatter(plan, place_ref, came_ref, grid_ref, cell_ref, arrived):
+    depth, tiles, tall = plan.depth, plan.tiles, plan.tall
     sub = lax.broadcasted_iota(jnp.int32, (SUBS, LANES), 0)
-
-    def turn(i, piece_ref):
-        s, j = i // tiles, i % tiles
-        values = came_ref[pl.ds(s * block + j, depth, stride=tiles), :]
-        if LANES > depth:
-            values = jnp.concatenate([values, jnp.zeros((LANES - depth, LANES), F32)], axis=0)
-        piece_ref[...] = turned_block(values, eye_ref)
-
-    def put(i, piece_ref):
-        for g in range(LANES // SUBS):
-            values = piece_ref[g * SUBS : (g + 1) * SUBS, :]
-            for t in range(SUBS):
-                spot = place_ref[i * LANES + g * SUBS + t]
-                pltpu.store(grid_ref.at[pl.ds(spot, SUBS), :], values, mask=sub == t)
-
-    even_ref, odd_ref = piece_refs
-    arrived(0)
-    turn(0, even_ref)
-    per = blocks // (2 * PARTS)
-
-    @pl.loop(0, PARTS)
-    def _(part):
-        @pl.loop(0, per)
-        def _(i):
-            at = (part * per + i) * 2
-            turn(at + 1, odd_ref)
-            put(at, even_ref)
-
-            @pl.when(jnp.logical_and(i == per - 1, part < PARTS - 1))
-            def _():
-                arrived(part + 1)
-
-            turn(jnp.minimum(at + 2, blocks - 1), even_ref)
-            put(at + 1, odd_ref)
-
-
-def gather(plan, place_ref, out_ref, grid_ref, piece_refs, eye_ref, finished):
-    depth, tiles = plan.depth, plan.tiles
-    blocks = plan.shares * tiles
+    fill = [jnp.zeros((tall - depth, LANES), F32)] if tall > depth else []
+    per = plan.shares // PARTS
+
+    @pl.loop(0, plan.shares)
+    def _(s):
+        @pl.when(s % per == 0)
+        def _():
+            arrived(s // per)
+
+        blocks = [
+            came_ref[pl.ds(s * plan.block + j, depth, stride=tiles), :] for j in range(tiles)
+        ]
+        turned = [jnp.concatenate([block] + fill, axis=0).T for block in blocks]
+        for j in range(tiles):
+            cell_ref[j * LANES : (j + 1) * LANES, 0:tall] = turned[j]
+
+        @pl.loop(0, tiles)
+        def _(j):
+            first = s * plan.rows + j * LANES
+            for g in range(LANES // SUBS):
+                at = pl.ds(pl.multiple_of(j * LANES + g * SUBS, SUBS), SUBS)
+                values = cell_ref[at, :]
+                for t in range(SUBS):
+                    spot = place_ref[first + g * SUBS + t]
+                    pltpu.store(grid_ref.at[pl.ds(spot, SUBS), :], values, mask=sub == t)
+
+
+def gather(plan, place_ref, out_ref, grid_ref, cell_ref, finished):
+    depth, tiles, tall = plan.depth, plan.tiles, plan.tall
     sub = lax.broadcasted_iota(jnp.int32, (SUBS, LANES), 0)
-
-    def turn(i, piece_ref):
-        s, j = i // tiles, i % tiles
-        turned = turned_block(piece_ref[...], eye_ref)
-        out_ref[pl.ds(s * plan.data + j, depth, stride=tiles), :] = turned[0:depth, :]
-
-    def get(i, piece_ref):
-        for g in range(LANES // SUBS):
-            first = i * LANES + g * SUBS
-            values = grid_ref[pl.ds(place_ref[first], SUBS), :]
-            for t in range(1, SUBS):
-                shifted = grid_ref[pl.ds(place_ref[first + t], SUBS), :]
-                values = jnp.where(sub == t, shifted, values)
-            piece_ref[g * SUBS : (g + 1) * SUBS, :] = values
-
-    even_ref, odd_ref = piece_refs
-    get(0, even_ref)
-    per = blocks // (2 * PARTS)
-
-    @pl.loop(0, PARTS)
-    def _(part):
-        @pl.loop(0, per)
-        def _(i):
-            at = (part * per + i) * 2
-            get(at + 1, odd_ref)
-            turn(at, even_ref)
-            get(jnp.minimum(at + 2, blocks - 1), even_ref)
-            turn(at + 1, odd_ref)
-
-        finished(part)
+    per = plan.shares // PARTS
+
+    @pl.loop(0, plan.shares)
+    def _(s):
+        @pl.loop(0, tiles)
+        def _(j):
+            first = s * plan.rows + j * LANES
+            for g in range(LANES // SUBS):
+                values = grid_ref[pl.ds(place_ref[first + g * SUBS], SUBS), :]
+                for t in range(1, SUBS):
+                    shifted = grid_ref[pl.ds(place_ref[first + g * SUBS + t], SUBS), :]
+                    values = jnp.where(sub == t, shifted, values)
+                cell_ref[pl.ds(pl.multiple_of(j * LANES + g * SUBS, SUBS), SUBS), :] = values
+
+        turned = [cell_ref[j * LANES : (j + 1) * LANES, 0:tall].T for j in range(tiles)]
+        for j in range(tiles):
+            out_ref[pl.ds(s * plan.data + j, depth, stride=tiles), :] = turned[j][0:depth, :]
+
+        @pl.when(s % per == per - 1)
+        def _():
+            finished(s // per)
 
 
 def spread_drift(plan, came_ref, held, turned, drift_ref):
@@ -613,7 +583,7 @@
 def middle_kernel(
     plan,
     place_ref, speed_ref, came_hbm, out_hbm,
-    came_ref, out_ref, one_ref, two_ref, drift_ref, even_ref, odd_ref, eye_ref, in_sems, out_sems,
+    came_ref, out_ref, one_ref, two_ref, drift_ref, cell_ref, in_sems, out_sems,
 ):
     shares, block, data = plan.shares, plan.block, plan.data
     part_in, part_out = shares // PARTS * block, shares // PARTS * data
@@ -628,23 +598,17 @@
 
     for part in range(PARTS):
         copy_in(part).start()
-
-    row = lax.broadcasted_iota(jnp.int32, (LANES, LANES), 0)
-    lane = lax.broadcasted_iota(jnp.int32, (LANES, LANES), 1)
-    eye = jnp.where(row == lane, 1.0, 0.0).astype(BF16)
-    eye_ref[:, 0:LANES] = eye
-    eye_ref[:, LANES : 2 * LANES] = eye
 
     @pl.loop(0, plan.size // LANES)
     def _(i):
         at = pl.ds(pl.multiple_of(i * LANES, LANES), LANES)
         one_ref[at, :] = jnp.full((LANES, LANES), DRY, F32)
 
-    scatter(plan, place_ref, came_ref, one_ref, (even_ref, odd_ref), eye_ref, lambda part: copy_in(part).wait())
-    spread_drift(plan, came_ref, even_ref, odd_ref, drift_ref)
+    scatter(plan, place_ref, came_ref, one_ref, cell_ref, lambda part: copy_in(part).wait())
+    spread_drift(plan, came_ref, cell_ref.at[0:LANES], cell_ref.at[LANES : 2 * LANES], drift_ref)
     me = lax.axis_index("space")
     sweep(plan, drift_ref, speed_ref.at[me], one_ref, two_ref)
-    gather(plan, place_ref, out_ref, two_ref, (even_ref, odd_ref), eye_ref, lambda part: copy_out(part).start())
+    gather(plan, place_ref, out_ref, two_ref, cell_ref, lambda part: copy_out(part).start())
     for part in range(PARTS):
         copy_out(part).wait()
 
@@ -743,9 +707,7 @@
             pltpu.VMEM((size, LANES), F32),
             pltpu.VMEM((size, LANES), F32),
             pltpu.VMEM((2 * points, LANES), F32),
-            pltpu.VMEM((LANES, LANES), F32),
-            pltpu.VMEM((LANES, LANES), F32),
-            pltpu.VMEM((LANES, 2 * LANES), BF16),
+            pltpu.VMEM((rows, LANES), F32),
             pltpu.SemaphoreType.DMA((PARTS,)),
             pltpu.SemaphoreType.DMA((PARTS,)),
         ],

time: 201 us -> 192 us (0.955)
  Pallas kernels: 58.3 us -> 49 us
    pallas_call x1, Pallas kernels: 35.3 us -> 26 us  [on_spectrum(): kernel(functools.partial(middle_kernel, plan), flops=24 * size * LANES, t...]
  transfers between devices with their start and end apart: 1 -> 1, of which waited for: 0 -> 0; matrix products, arithmetic and copies ran while one was open for 0% -> 0% of each run, Pallas kernels for 3% -> 4%
where the time goes in v10:
time: 192 us; the launch traced here: 189 us
  blocking collectives  132 us (69%)
  Pallas kernels  49 us (26%)
  starting transfers between devices  6.55 us (3%)
    all_to_all x1, blocking collectives, on_spectrum(): lax.all_to_all(sent.reshape(shares, plan.block, LANES), 'space', 0, 0, ti...  67.5 us
    all_to_all x1, blocking collectives, on_spectrum(): lax.all_to_all(swept.reshape(shares, depth, tiles, LANES), 'space', 0, 0,...  64.8 us
    pallas_call x1, Pallas kernels, on_spectrum(): kernel(functools.partial(middle_kernel, plan), flops=24 * size * LANES, t...  26 us
    pallas_call x1, Pallas kernels, on_spectrum(): kernel(functools.partial(first_kernel, plan), **h_cost, out_shape=[jax.Sh...  8.61 us
    pallas_call x1, Pallas kernels, on_spectrum(): kernel(functools.partial(ready_kernel, plan), flops=0, traffic=12 * rows...  6.88 us
    all_to_all x1, starting transfers between devices, on_spectrum(): parcel = lax.all_to_all(parcel, 'space', 0, 0, tiled=True)  6.55 us
    pallas_call x1, Pallas kernels, on_spectrum(): kernel(functools.partial(last_kernel, plan), vmem=24 * MIB, **h_cost, out...  6.05 us
  transfers between devices with their start and end apart: 1, of which 0 were waited for; matrix products, arithmetic and copies ran while one was open for 0% of the time, Pallas kernels for 4%

profile of v10, /device:TPU:15, one launch (start us, length us, event | category | flops | bytes accessed | tf_op | source)
XLA Modules:
  0.0 188.6 jit_solution(14016649795305962852)
XLA Ops:
  0.0 1.5 pack.1
  1.5 6.6 %all-to-all-start = ((f32[16,2,1152]{2,1,0:T(2,128)}), f32[16,2,1152]{2,1,0:T(2,128)S(1)}, u32[]{:S(2)}, u32[]{:S(2)}) async-start(f32[16,2,1152]{2,1,0:T(2,128)} %pack.1), calls=%async_computation | async-start | bytes 294912 | tf_op jit(solution)/shard_map/all_to_all | solution.py:658
  8.0 6.9 %ready.1 = (f32[144,512]{1,0:T(8,128)}, bf16[1296,1296]{1,0:T(8,128)(2,1)}) custom-call(f32[1296,8]{1,0:T(8,128)} %constant.4.clone.table_ref, bf16[1296,1296]{1,0:T(8,128)(2,1)} %coup_hbm.1, f32[1296,512]{1,0:T(8,128)} %bitcast.12), custom_call_target="tpu_custom_call" | custom-call | bytes 7962624 | tf_op jit(solution)/shard_map/ready/pallas_call | solution.py:667
  14.9 0.0 all-to-all-done.parcel_ref
  14.9 0.0 copy-start.4
  14.9 0.6 copy-done.4
  15.6 8.6 %first_half.1 = (f32[8,512]{1,0:T(8,128)}, f32[5376,128]{1,0:T(8,128)}) custom-call(s32[1,16]{1,0:T(1,128)} %count_ref.1, s32[1,512]{1,0:T(1,128)} %bitcast.15, f32[16,2,1152]{2,1,0:T(2,128)} %copy-done.4, s32[1,16,64]{2,1,0:T(8,128)} %send_ref.1, f32[1296,8]{1,0:T(8,128)} %constant.4.clone.table_ref, f32[144,512]{1,0:T(8,128)} %get-tuple-element.9.unit_ref, ...), custom_call_target="tpu_custom_call" | custom-call | flops 1719926784 | bytes 7962624 | tf_op jit(solution)/shard_map/first_half/pallas_call | solution.py:678
  24.2 0.0 copy-start.2
  24.2 67.5 %all_to_all.15 = f32[16,336,128]{2,1,0:T(8,128)S(1)} all-to-all(f32[16,336,128]{2,1,0:T(8,128)} %bitcast.14), channel_id=1, replica_groups=mesh['members'=2,'space'=16] {'space'}, dimensions={0} | all-to-all | bytes 5505024 | tf_op jit(solution)/shard_map/all_to_all | solution.py:694
  91.7 0.0 copy-done.2
  91.7 26.0 %sweeps.1 = f32[5184,128]{1,0:T(8,128)S(1)} custom-call(s32[8192]{0:T(1024)S(1)} %bitcast.11, f32[16,8,128]{2,1,0:T(8,128)S(1)} %copy-done.2, f32[5376,128]{1,0:T(8,128)S(1)} %bitcast.8), custom_call_target="tpu_custom_call" | custom-call | flops 51118080 | bytes 5308416 | tf_op jit(solution)/shard_map/sweeps/pallas_call | solution.py:698
  117.7 0.0 copy-start
  117.8 0.0 copy-start.1
  117.8 0.0 copy-start.3
  117.8 64.8 %all_to_all.16 = f32[16,81,4,128]{3,2,1,0:T(4,128)S(1)} all-to-all(f32[16,81,4,128]{3,2,1,0:T(4,128)S(1)} %bitcast.10), channel_id=1, replica_groups=mesh['members'=2,'space'=16] {'space'}, dimensions={0} | all-to-all | bytes 5308416 | tf_op jit(solution)/shard_map/all_to_all | solution.py:716
  182.6 0.0 copy-done
  182.6 0.0 copy-done.1
  182.6 0.0 copy-done.3
  182.6 6.0 %last_half.1 = f32[1296,512]{1,0:T(8,128)} custom-call(f32[8,512]{1,0:T(8,128)S(1)} %copy-done.3, f32[1296,8]{1,0:T(8,128)S(1)} %copy-done.1, f32[5184,128]{1,0:T(8,128)S(1)} %bitcast.9, bf16[1296,1296]{1,0:T(8,128)(2,1)S(1)} %copy-done), custom_call_target="tpu_custom_call" | custom-call | flops 1719926784 | bytes 7962624 | tf_op jit(solution)/shard_map/last_half/pallas_call | solution.py:719
  (1 shorter events, 0.0 us)
Async XLA Ops:
  1.5 13.4 %all-to-all-start = ((f32[16,2,1152]{2,1,0:T(2,128)}), f32[16,2,1152]{2,1,0:T(2,128)S(1)}, u32[]{:S(2)}, u32[]{:S(2)}) async-start(f32[16,2,1152]{2,1,0:T(2,128)} %pack.1), calls=%async_computation | async-start | bytes 294912 | tf_op jit(solution)/shard_map/all_to_all | solution.py:658
  14.9 0.7 copy-start.4
  24.2 67.5 %copy-start.2 = (f32[16,8,128]{2,1,0:T(8,128)S(1)}, f32[16,8,128]{2,1,0:T(8,128)}, u32[]{:S(2)}) copy-start(f32[16,8,128]{2,1,0:T(8,128)} %constant.5.clone.speed_ref) | copy-start | bytes 196612
  117.7 64.8 %copy-start = (bf16[1296,1296]{1,0:T(8,128)(2,1)S(1)}, bf16[1296,1296]{1,0:T(8,128)(2,1)}, u32[]{:S(2)}) copy-start(bf16[1296,1296]{1,0:T(8,128)(2,1)} %get-tuple-element.10.coup_hbm) | copy-start | bytes 10077700
  117.8 64.8 %copy-start.1 = (f32[1296,8]{1,0:T(8,128)S(1)}, f32[1296,8]{1,0:T(8,128)}, u32[]{:S(2)}) copy-start(f32[1296,8]{1,0:T(8,128)} %constant.4.clone.table_ref) | copy-start | bytes 124420
  117.8 64.8 %copy-start.3 = (f32[8,512]{1,0:T(8,128)S(1)}, f32[8,512]{1,0:T(8,128)}, u32[]{:S(2)}) copy-start(f32[8,512]{1,0:T(8,128)} %get-tuple-element.11.winds_ref) | copy-start | bytes 49156

commit v11 on v10

--- a/solution.py
+++ b/solution.py
@@ -166,7 +166,7 @@
 MIB = 1024 * 1024
 WHOLE_VMEM = 60 * MIB
 DRY = 1e30
-PARTS = 4
+PARTS = 2
 PERIOD = 4 * FREQS
 
 
@@ -205,7 +205,7 @@
         self.tiles = rows // LANES
         self.data = self.depth * self.tiles
         self.force = 2 * points // (LANES * shares)
-        self.block = ceil_to(self.data + self.tiles + self.force, SUBS)
+        self.block = self.data + self.tiles + self.force
         self.tall = ceil_to(self.depth, SUBS)
         self.strip = strip_rows * cols
         self.grid_rows = strip_rows * shares
@@ -219,6 +219,8 @@
         if self.spec % self.shares or self.depth > LANES or self.rows % (2 * LANES):
             return False
         if 2 * self.points % (LANES * self.shares) or self.points % LANES or self.cap > LANES:
+            return False
+        if self.shares // PARTS * self.block % SUBS or self.shares // PARTS * self.data % SUBS:
             return False
         if 2 * self.points // LANES > LANES or self.cols != LANES or self.shares % PARTS:
             return False
@@ -362,8 +364,6 @@
     current = jnp.sum(parcel_ref[:, :, points : points + width], axis=0)
     spare = own_places(plan, parcel_ref, send_ref, count_ref)
     spare += [current[1:2, f * LANES : (f + 1) * LANES] for f in range(plan.force)]
-    if block > data + len(spare):
-        spare.append(jnp.zeros((block - data - len(spare), LANES), F32))
     for d in range(shares):
         out_ref[d * block + data : (d + 1) * block, :] = jnp.concatenate(spare, axis=0)
     east, north = cell_winds(jnp.sum(parcel_ref[:, :, 0:points], axis=0), cp_ref[...])
@@ -392,7 +392,7 @@
         upto = (first + values.shape[0]) // plan.depth
         for d in range(sent[0], upto):
             out_ref[d * block : d * block + data, :] = buf_ref[d * data : (d + 1) * data, :]
-        at = slice(sent[0] * block, upto * block)
+        at = slice(sent[0] * block // SUBS * SUBS, upto * block // SUBS * SUBS)
         copies.append(
             pltpu.make_async_copy(out_ref.at[at, :], out_hbm.at[at, :], out_sems.at[len(copies)])
         )
@@ -692,7 +692,7 @@
         name="first_half",
     )(send_count, cp, parcel, send_list, table, unit_loss_held, spectra.T, coup)
     came = lax.all_to_all(
-        sent.reshape(shares, plan.block, LANES), "space", 0, 0, tiled=True
+        sent.reshape(shares, plan.block, 1, LANES), "space", 0, 0, tiled=True
     )
     place = came[:, plan.data : plan.data + tiles].astype(jnp.int32).reshape(-1)
     swept = kernel(

time: 192 us -> 190 us (0.990)
  no operation moved by 1% of the time
where the time goes in v11:
time: 190 us; the launch traced here: 186 us
  blocking collectives  131 us (69%)
  Pallas kernels  47.6 us (25%)
  starting transfers between devices  6.55 us (3%)
    all_to_all x1, blocking collectives, on_spectrum(): lax.all_to_all(sent.reshape(shares, plan.block, 1, LANES), 'space', 0, 0,...  66.4 us
    all_to_all x1, blocking collectives, on_spectrum(): lax.all_to_all(swept.reshape(shares, depth, tiles, LANES), 'space', 0, 0,...  64.9 us
    pallas_call x1, Pallas kernels, on_spectrum(): kernel(functools.partial(middle_kernel, plan), flops=24 * size * LANES, t...  24.6 us
    pallas_call x1, Pallas kernels, on_spectrum(): kernel(functools.partial(first_kernel, plan), **h_cost, out_shape=[jax.Sh...  8.64 us
    pallas_call x1, Pallas kernels, on_spectrum(): kernel(functools.partial(ready_kernel, plan), flops=0, traffic=12 * rows...  6.88 us
    all_to_all x1, starting transfers between devices, on_spectrum(): parcel = lax.all_to_all(parcel, 'space', 0, 0, tiled=True)  6.55 us
    pallas_call x1, Pallas kernels, on_spectrum(): kernel(functools.partial(last_kernel, plan), vmem=24 * MIB, **h_cost, out...  6.05 us
  transfers between devices with their start and end apart: 1, of which 0 were waited for; matrix products, arithmetic and copies ran while one was open for 0% of the time, Pallas kernels for 4%

profile of v11, /device:TPU:15, one launch (start us, length us, event | category | flops | bytes accessed | tf_op | source)
XLA Modules:
  0.0 186.2 jit_solution(1221472627788529962)
XLA Ops:
  0.0 1.5 pack.1
  1.5 6.6 %all-to-all-start = ((f32[16,2,1152]{2,1,0:T(2,128)}), f32[16,2,1152]{2,1,0:T(2,128)S(1)}, u32[]{:S(2)}, u32[]{:S(2)}) async-start(f32[16,2,1152]{2,1,0:T(2,128)} %pack.1), calls=%async_computation | async-start | bytes 294912 | tf_op jit(solution)/shard_map/all_to_all | solution.py:658
  8.0 6.9 %ready.1 = (f32[144,512]{1,0:T(8,128)}, bf16[1296,1296]{1,0:T(8,128)(2,1)}) custom-call(f32[1296,8]{1,0:T(8,128)} %constant.4.clone.table_ref, bf16[1296,1296]{1,0:T(8,128)(2,1)} %coup_hbm.1, f32[1296,512]{1,0:T(8,128)} %bitcast.12), custom_call_target="tpu_custom_call" | custom-call | bytes 7962624 | tf_op jit(solution)/shard_map/ready/pallas_call | solution.py:667
  14.9 0.0 all-to-all-done.parcel_ref
  14.9 0.0 copy-start.4
  14.9 0.6 copy-done.4
  15.6 8.6 %first_half.1 = (f32[8,512]{1,0:T(8,128)}, f32[5264,128]{1,0:T(8,128)}) custom-call(s32[1,16]{1,0:T(1,128)} %count_ref.1, s32[1,512]{1,0:T(1,128)} %bitcast.15, f32[16,2,1152]{2,1,0:T(2,128)} %copy-done.4, s32[1,16,64]{2,1,0:T(8,128)} %send_ref.1, f32[1296,8]{1,0:T(8,128)} %constant.4.clone.table_ref, f32[144,512]{1,0:T(8,128)} %get-tuple-element.9.unit_ref, ...), custom_call_target="tpu_custom_call" | custom-call | flops 1719926784 | bytes 7962624 | tf_op jit(solution)/shard_map/first_half/pallas_call | solution.py:678
  24.2 0.0 copy-start.2
  24.2 66.4 %all_to_all.15 = f32[16,329,1,128]{3,2,1,0:T(1,128)S(1)} all-to-all(f32[16,329,1,128]{3,2,1,0:T(1,128)} %bitcast.14), channel_id=1, replica_groups=mesh['members'=2,'space'=16] {'space'}, dimensions={0} | all-to-all | bytes 5390336 | tf_op jit(solution)/shard_map/all_to_all | solution.py:694
  90.6 0.0 copy-done.2
  90.6 24.6 %sweeps.1 = f32[5184,128]{1,0:T(8,128)S(1)} custom-call(s32[8192]{0:T(1024)S(1)} %bitcast.11, f32[16,8,128]{2,1,0:T(8,128)S(1)} %copy-done.2, f32[5264,128]{1,0:T(8,128)S(1)} %bitcast.8), custom_call_target="tpu_custom_call" | custom-call | flops 51118080 | bytes 5308416 | tf_op jit(solution)/shard_map/sweeps/pallas_call | solution.py:698
  115.3 0.0 copy-start
  115.3 0.0 copy-start.1
  115.3 0.0 copy-start.3
  115.3 64.9 %all_to_all.16 = f32[16,81,4,128]{3,2,1,0:T(4,128)S(1)} all-to-all(f32[16,81,4,128]{3,2,1,0:T(4,128)S(1)} %bitcast.10), channel_id=1, replica_groups=mesh['members'=2,'space'=16] {'space'}, dimensions={0} | all-to-all | bytes 5308416 | tf_op jit(solution)/shard_map/all_to_all | solution.py:716
  180.1 0.0 copy-done
  180.1 0.0 copy-done.1
  180.1 0.0 copy-done.3
  180.1 6.0 %last_half.1 = f32[1296,512]{1,0:T(8,128)} custom-call(f32[8,512]{1,0:T(8,128)S(1)} %copy-done.3, f32[1296,8]{1,0:T(8,128)S(1)} %copy-done.1, f32[5184,128]{1,0:T(8,128)S(1)} %bitcast.9, bf16[1296,1296]{1,0:T(8,128)(2,1)S(1)} %copy-done), custom_call_target="tpu_custom_call" | custom-call | flops 1719926784 | bytes 7962624 | tf_op jit(solution)/shard_map/last_half/pallas_call | solution.py:719
  (1 shorter events, 0.0 us)
Async XLA Ops:
  1.5 13.4 %all-to-all-start = ((f32[16,2,1152]{2,1,0:T(2,128)}), f32[16,2,1152]{2,1,0:T(2,128)S(1)}, u32[]{:S(2)}, u32[]{:S(2)}) async-start(f32[16,2,1152]{2,1,0:T(2,128)} %pack.1), calls=%async_computation | async-start | bytes 294912 | tf_op jit(solution)/shard_map/all_to_all | solution.py:658
  14.9 0.7 copy-start.4
  24.2 66.4 %copy-start.2 = (f32[16,8,128]{2,1,0:T(8,128)S(1)}, f32[16,8,128]{2,1,0:T(8,128)}, u32[]{:S(2)}) copy-start(f32[16,8,128]{2,1,0:T(8,128)} %constant.5.clone.speed_ref) | copy-start | bytes 196612
  115.3 64.9 %copy-start = (bf16[1296,1296]{1,0:T(8,128)(2,1)S(1)}, bf16[1296,1296]{1,0:T(8,128)(2,1)}, u32[]{:S(2)}) copy-start(bf16[1296,1296]{1,0:T(8,128)(2,1)} %get-tuple-element.10.coup_hbm) | copy-start | bytes 10077700
  115.3 64.9 %copy-start.1 = (f32[1296,8]{1,0:T(8,128)S(1)}, f32[1296,8]{1,0:T(8,128)}, u32[]{:S(2)}) copy-start(f32[1296,8]{1,0:T(8,128)} %constant.4.clone.table_ref) | copy-start | bytes 124420
  115.3 64.9 %copy-start.3 = (f32[8,512]{1,0:T(8,128)S(1)}, f32[8,512]{1,0:T(8,128)}, u32[]{:S(2)}) copy-start(f32[8,512]{1,0:T(8,128)} %get-tuple-element.11.winds_ref) | copy-start | bytes 49156

commit v12 on v11

--- a/solution.py
+++ b/solution.py
@@ -166,7 +166,6 @@
 MIB = 1024 * 1024
 WHOLE_VMEM = 60 * MIB
 DRY = 1e30
-PARTS = 2
 PERIOD = 4 * FREQS
 
 
@@ -220,9 +219,9 @@
             return False
         if 2 * self.points % (LANES * self.shares) or self.points % LANES or self.cap > LANES:
             return False
-        if self.shares // PARTS * self.block % SUBS or self.shares // PARTS * self.data % SUBS:
+        if self.shares * self.block % SUBS or self.shares * self.data % SUBS:
             return False
-        if 2 * self.points // LANES > LANES or self.cols != LANES or self.shares % PARTS:
+        if 2 * self.points // LANES > LANES or self.cols != LANES:
             return False
         held = 2 * self.size + 2 * self.points + self.shares * (self.block + self.data)
         return 4 * LANES * held + 4 * MIB < 32 * MIB
@@ -446,18 +445,13 @@
         copy.wait()
 
 
-def scatter(plan, place_ref, came_ref, grid_ref, cell_ref, arrived):
+def scatter(plan, place_ref, came_ref, grid_ref, cell_ref):
     depth, tiles, tall = plan.depth, plan.tiles, plan.tall
     sub = lax.broadcasted_iota(jnp.int32, (SUBS, LANES), 0)
     fill = [jnp.zeros((tall - depth, LANES), F32)] if tall > depth else []
-    per = plan.shares // PARTS
 
     @pl.loop(0, plan.shares)
     def _(s):
-        @pl.when(s % per == 0)
-        def _():
-            arrived(s // per)
-
         blocks = [
             came_ref[pl.ds(s * plan.block + j, depth, stride=tiles), :] for j in range(tiles)
         ]
@@ -476,10 +470,9 @@
                     pltpu.store(grid_ref.at[pl.ds(spot, SUBS), :], values, mask=sub == t)
 
 
-def gather(plan, place_ref, out_ref, grid_ref, cell_ref, finished):
+def gather(plan, place_ref, out_ref, grid_ref, cell_ref):
     depth, tiles, tall = plan.depth, plan.tiles, plan.tall
     sub = lax.broadcasted_iota(jnp.int32, (SUBS, LANES), 0)
-    per = plan.shares // PARTS
 
     @pl.loop(0, plan.shares)
     def _(s):
@@ -496,10 +489,6 @@
         turned = [cell_ref[j * LANES : (j + 1) * LANES, 0:tall].T for j in range(tiles)]
         for j in range(tiles):
             out_ref[pl.ds(s * plan.data + j, depth, stride=tiles), :] = turned[j][0:depth, :]
-
-        @pl.when(s % per == per - 1)
-        def _():
-            finished(s // per)
 
 
 def spread_drift(plan, came_ref, held, turned, drift_ref):
@@ -582,35 +571,18 @@
 
 def middle_kernel(
     plan,
-    place_ref, speed_ref, came_hbm, out_hbm,
-    came_ref, out_ref, one_ref, two_ref, drift_ref, cell_ref, in_sems, out_sems,
+    place_ref, speed_ref, came_ref, out_ref, one_ref, two_ref, drift_ref, cell_ref,
 ):
-    shares, block, data = plan.shares, plan.block, plan.data
-    part_in, part_out = shares // PARTS * block, shares // PARTS * data
-
-    def copy_in(part):
-        at = pl.ds(pl.multiple_of(part * part_in, SUBS), part_in)
-        return pltpu.make_async_copy(came_hbm.at[at, :], came_ref.at[at, :], in_sems.at[part])
-
-    def copy_out(part):
-        at = pl.ds(pl.multiple_of(part * part_out, SUBS), part_out)
-        return pltpu.make_async_copy(out_ref.at[at, :], out_hbm.at[at, :], out_sems.at[part])
-
-    for part in range(PARTS):
-        copy_in(part).start()
-
     @pl.loop(0, plan.size // LANES)
     def _(i):
         at = pl.ds(pl.multiple_of(i * LANES, LANES), LANES)
         one_ref[at, :] = jnp.full((LANES, LANES), DRY, F32)
 
-    scatter(plan, place_ref, came_ref, one_ref, cell_ref, lambda part: copy_in(part).wait())
+    scatter(plan, place_ref, came_ref, one_ref, cell_ref)
     spread_drift(plan, came_ref, cell_ref.at[0:LANES], cell_ref.at[LANES : 2 * LANES], drift_ref)
     me = lax.axis_index("space")
     sweep(plan, drift_ref, speed_ref.at[me], one_ref, two_ref)
-    gather(plan, place_ref, out_ref, two_ref, cell_ref, lambda part: copy_out(part).start())
-    for part in range(PARTS):
-        copy_out(part).wait()
+    gather(plan, place_ref, out_ref, two_ref, cell_ref)
 
 
 VMEM = pl.BlockSpec(memory_space=pltpu.VMEM)
@@ -699,17 +671,13 @@
         functools.partial(middle_kernel, plan),
         flops=24 * size * LANES, traffic=8 * rows * spec, vmem=32 * MIB,
         out_shape=jax.ShapeDtypeStruct((data_rows, LANES), F32),
-        in_specs=[SMEM, VMEM, ANY],
-        out_specs=ANY,
+        in_specs=[SMEM, VMEM, VMEM],
+        out_specs=VMEM,
         scratch_shapes=[
-            pltpu.VMEM((shares * plan.block, LANES), F32),
-            pltpu.VMEM((data_rows, LANES), F32),
             pltpu.VMEM((size, LANES), F32),
             pltpu.VMEM((size, LANES), F32),
             pltpu.VMEM((2 * points, LANES), F32),
             pltpu.VMEM((rows, LANES), F32),
-            pltpu.SemaphoreType.DMA((PARTS,)),
-            pltpu.SemaphoreType.DMA((PARTS,)),
         ],
         name="sweeps",
     )(place, jnp.asarray(speed), came.reshape(-1, LANES))

time: 190 us -> 189 us (level)
  no operation moved by 1% of the time
where the time goes in v12:
time: 189 us; the launch traced here: 185 us
  blocking collectives  131 us (69%)
  Pallas kernels  46.9 us (25%)
  starting transfers between devices  6.55 us (3%)
    all_to_all x1, blocking collectives, on_spectrum(): lax.all_to_all(sent.reshape(shares, plan.block, 1, LANES), 'space', 0, 0,...  66.4 us
    all_to_all x1, blocking collectives, on_spectrum(): lax.all_to_all(swept.reshape(shares, depth, tiles, LANES), 'space', 0, 0,...  64.9 us
    pallas_call x1, Pallas kernels, on_spectrum(): kernel(functools.partial(middle_kernel, plan), flops=24 * size * LANES, t...  23.8 us
    pallas_call x1, Pallas kernels, on_spectrum(): kernel(functools.partial(first_kernel, plan), **h_cost, out_shape=[jax.Sh...  8.64 us
    pallas_call x1, Pallas kernels, on_spectrum(): kernel(functools.partial(ready_kernel, plan), flops=0, traffic=12 * rows...  6.88 us
    all_to_all x1, starting transfers between devices, on_spectrum(): parcel = lax.all_to_all(parcel, 'space', 0, 0, tiled=True)  6.55 us
    pallas_call x1, Pallas kernels, on_spectrum(): kernel(functools.partial(last_kernel, plan), vmem=24 * MIB, **h_cost, out...  6.05 us
  transfers between devices with their start and end apart: 1, of which 0 were waited for; matrix products, arithmetic and copies ran while one was open for 0% of the time, Pallas kernels for 4%

profile of v12, /device:TPU:15, one launch (start us, length us, event | category | flops | bytes accessed | tf_op | source)
XLA Modules:
  0.0 185.4 jit_solution(12772763012173187753)
XLA Ops:
  0.0 1.5 pack.1
  1.5 6.6 %all-to-all-start = ((f32[16,2,1152]{2,1,0:T(2,128)}), f32[16,2,1152]{2,1,0:T(2,128)S(1)}, u32[]{:S(2)}, u32[]{:S(2)}) async-start(f32[16,2,1152]{2,1,0:T(2,128)} %pack.1), calls=%async_computation | async-start | bytes 294912 | tf_op jit(solution)/shard_map/all_to_all | solution.py:630
  8.0 6.9 %ready.1 = (f32[144,512]{1,0:T(8,128)}, bf16[1296,1296]{1,0:T(8,128)(2,1)}) custom-call(f32[1296,8]{1,0:T(8,128)} %constant.4.clone.table_ref, bf16[1296,1296]{1,0:T(8,128)(2,1)} %coup_hbm.1, f32[1296,512]{1,0:T(8,128)} %bitcast.12), custom_call_target="tpu_custom_call" | custom-call | bytes 7962624 | tf_op jit(solution)/shard_map/ready/pallas_call | solution.py:639
  14.9 0.0 all-to-all-done.parcel_ref
  14.9 0.0 copy-start.4
  14.9 0.6 copy-done.4
  15.6 8.6 %first_half.1 = (f32[8,512]{1,0:T(8,128)}, f32[5264,128]{1,0:T(8,128)}) custom-call(s32[1,16]{1,0:T(1,128)} %count_ref.1, s32[1,512]{1,0:T(1,128)} %bitcast.15, f32[16,2,1152]{2,1,0:T(2,128)} %copy-done.4, s32[1,16,64]{2,1,0:T(8,128)} %send_ref.1, f32[1296,8]{1,0:T(8,128)} %constant.4.clone.table_ref, f32[144,512]{1,0:T(8,128)} %get-tuple-element.9.unit_ref, ...), custom_call_target="tpu_custom_call" | custom-call | flops 1719926784 | bytes 7962624 | tf_op jit(solution)/shard_map/first_half/pallas_call | solution.py:650
  24.2 0.0 copy-start.2
  24.2 66.4 %all_to_all.15 = f32[16,329,1,128]{3,2,1,0:T(1,128)S(1)} all-to-all(f32[16,329,1,128]{3,2,1,0:T(1,128)} %bitcast.14), channel_id=1, replica_groups=mesh['members'=2,'space'=16] {'space'}, dimensions={0} | all-to-all | bytes 5390336 | tf_op jit(solution)/shard_map/all_to_all | solution.py:666
  90.6 0.0 copy-done.2
  90.6 23.8 %sweeps.1 = f32[5184,128]{1,0:T(8,128)S(1)} custom-call(s32[8192]{0:T(1024)S(1)} %bitcast.11, f32[16,8,128]{2,1,0:T(8,128)S(1)} %copy-done.2, f32[5264,128]{1,0:T(8,128)S(1)} %bitcast.8), custom_call_target="tpu_custom_call" | custom-call | flops 51118080 | bytes 5308416 | tf_op jit(solution)/shard_map/sweeps/pallas_call | solution.py:670
  114.5 0.0 copy-start
  114.5 0.0 copy-start.1
  114.5 0.0 copy-start.3
  114.5 64.9 %all_to_all.16 = f32[16,81,4,128]{3,2,1,0:T(4,128)S(1)} all-to-all(f32[16,81,4,128]{3,2,1,0:T(4,128)S(1)} %bitcast.10), channel_id=1, replica_groups=mesh['members'=2,'space'=16] {'space'}, dimensions={0} | all-to-all | bytes 5308416 | tf_op jit(solution)/shard_map/all_to_all | solution.py:684
  179.4 0.0 copy-done
  179.4 0.0 copy-done.1
  179.4 0.0 copy-done.3
  179.4 6.0 %last_half.1 = f32[1296,512]{1,0:T(8,128)} custom-call(f32[8,512]{1,0:T(8,128)S(1)} %copy-done.3, f32[1296,8]{1,0:T(8,128)S(1)} %copy-done.1, f32[5184,128]{1,0:T(8,128)S(1)} %bitcast.9, bf16[1296,1296]{1,0:T(8,128)(2,1)S(1)} %copy-done), custom_call_target="tpu_custom_call" | custom-call | flops 1719926784 | bytes 7962624 | tf_op jit(solution)/shard_map/last_half/pallas_call | solution.py:687
  (1 shorter events, 0.0 us)
Async XLA Ops:
  1.5 13.4 %all-to-all-start = ((f32[16,2,1152]{2,1,0:T(2,128)}), f32[16,2,1152]{2,1,0:T(2,128)S(1)}, u32[]{:S(2)}, u32[]{:S(2)}) async-start(f32[16,2,1152]{2,1,0:T(2,128)} %pack.1), calls=%async_computation | async-start | bytes 294912 | tf_op jit(solution)/shard_map/all_to_all | solution.py:630
  14.9 0.7 copy-start.4
  24.2 66.4 %copy-start.2 = (f32[16,8,128]{2,1,0:T(8,128)S(1)}, f32[16,8,128]{2,1,0:T(8,128)}, u32[]{:S(2)}) copy-start(f32[16,8,128]{2,1,0:T(8,128)} %constant.5.clone.speed_ref) | copy-start | bytes 196612
  114.5 64.9 %copy-start = (bf16[1296,1296]{1,0:T(8,128)(2,1)S(1)}, bf16[1296,1296]{1,0:T(8,128)(2,1)}, u32[]{:S(2)}) copy-start(bf16[1296,1296]{1,0:T(8,128)(2,1)} %get-tuple-element.10.coup_hbm) | copy-start | bytes 10077700
  114.5 64.9 %copy-start.1 = (f32[1296,8]{1,0:T(8,128)S(1)}, f32[1296,8]{1,0:T(8,128)}, u32[]{:S(2)}) copy-start(f32[1296,8]{1,0:T(8,128)} %constant.4.clone.table_ref) | copy-start | bytes 124420
  114.5 64.9 %copy-start.3 = (f32[8,512]{1,0:T(8,128)S(1)}, f32[8,512]{1,0:T(8,128)}, u32[]{:S(2)}) copy-start(f32[8,512]{1,0:T(8,128)} %get-tuple-element.11.winds_ref) | copy-start | bytes 49156

commit v13 on v12

--- a/solution.py
+++ b/solution.py
@@ -270,15 +270,17 @@
 
 
 def unit_loss(plan, load, arrive, table_ref, unit_ref):
-    tall = plan.spec // len(arrive)
+    parts = max(len(arrive), 1)
+    tall = plan.spec // parts
 
     def squares(i, total):
         piece = load(pl.multiple_of(i * 48, 48), 48)
         return total + jnp.sum((piece * piece).reshape(48 // SUBS, SUBS, plan.rows), axis=0)
 
     total = jnp.zeros((SUBS, plan.rows), F32)
-    for q, copy in enumerate(arrive):
-        copy.wait()
+    for q in range(parts):
+        if arrive:
+            arrive[q].wait()
         total = lax.fori_loop(q * tall // 48, (q + 1) * tall // 48, squares, total)
     mean_square = jnp.sum(total, axis=0, keepdims=True) * (1.0 / plan.spec)
     unit_ref[...] = 1.0 / (1.0 + table_ref[0:PERIOD, 3:4] * mean_square)
@@ -405,14 +407,10 @@
 
 def last_kernel(
     plan,
-    winds_ref, table_ref, came_hbm, coup_hbm, out_hbm,
-    came_ref, coup_ref, loc_ref, locb_ref, unit_ref, sems, coup_sem, out_sems,
+    winds_ref, table_ref, came_ref, coup_ref, out_hbm, loc_ref, locb_ref, unit_ref, out_sems,
 ):
     tiles = plan.tiles
     copies = []
-    arrive = fetch(came_hbm, came_ref, sems, plan.thirds)
-    get = pltpu.make_async_copy(coup_hbm, coup_ref, coup_sem)
-    get.start()
 
     def load(first, count):
         start = pl.multiple_of(first * tiles, SUBS)
@@ -420,7 +418,7 @@
             [came_ref[pl.ds(start + j, count, stride=tiles), :] for j in range(tiles)], axis=1
         )
 
-    unit_loss(plan, load, arrive, table_ref, unit_ref)
+    unit_loss(plan, load, [], table_ref, unit_ref)
     east, north = winds_ref[0:1, :], winds_ref[1:2, :]
 
     @pl.loop(0, plan.spec // PERIOD)
@@ -439,7 +437,6 @@
         )
         copies[-1].start()
 
-    get.wait()
     coupled(plan, coup_ref, loc_ref, locb_ref, store)
     for copy in copies:
         copy.wait()
@@ -688,12 +685,9 @@
         functools.partial(last_kernel, plan),
         vmem=24 * MIB, **h_cost,
         out_shape=jax.ShapeDtypeStruct((spec, rows), F32),
-        in_specs=[VMEM] * 2 + [ANY] * 2,
+        in_specs=[VMEM] * 4,
         out_specs=ANY,
-        scratch_shapes=[
-            pltpu.VMEM((data_rows, LANES), F32),
-            square, whole, rounded, unit, dma((plan.thirds,)), dma, dma((plan.thirds,)),
-        ],
+        scratch_shapes=[whole, rounded, unit, dma((plan.thirds,))],
         name="last_half",
     )(winds, table, back.reshape(data_rows, LANES), coup)
     return result.T

time: 189 us -> 188 us (level)
  no operation moved by 1% of the time
where the time goes in v13:
time: 188 us; the launch traced here: 184 us
  blocking collectives  131 us (70%)
  Pallas kernels  45.7 us (24%)
  starting transfers between devices  6.55 us (3%)
    all_to_all x1, blocking collectives, on_spectrum(): lax.all_to_all(sent.reshape(shares, plan.block, 1, LANES), 'space', 0, 0,...  66.4 us
    all_to_all x1, blocking collectives, on_spectrum(): lax.all_to_all(swept.reshape(shares, depth, tiles, LANES), 'space', 0, 0,...  64.9 us
    pallas_call x1, Pallas kernels, on_spectrum(): kernel(functools.partial(middle_kernel, plan), flops=24 * size * LANES, t...  23.8 us
    pallas_call x1, Pallas kernels, on_spectrum(): kernel(functools.partial(first_kernel, plan), **h_cost, out_shape=[jax.Sh...  8.64 us
    pallas_call x1, Pallas kernels, on_spectrum(): kernel(functools.partial(ready_kernel, plan), flops=0, traffic=12 * rows...  6.88 us
    all_to_all x1, starting transfers between devices, on_spectrum(): parcel = lax.all_to_all(parcel, 'space', 0, 0, tiled=True)  6.55 us
    pallas_call x1, Pallas kernels, on_spectrum(): kernel(functools.partial(last_kernel, plan), vmem=24 * MIB, **h_cost, out...  4.92 us
  transfers between devices with their start and end apart: 1, of which 0 were waited for; matrix products, arithmetic and copies ran while one was open for 0% of the time, Pallas kernels for 4%

profile of v13, /device:TPU:15, one launch (start us, length us, event | category | flops | bytes accessed | tf_op | source)
XLA Modules:
  0.0 184.3 jit_solution(2149904875280486859)
XLA Ops:
  0.0 1.5 pack.1
  1.5 6.6 %all-to-all-start = ((f32[16,2,1152]{2,1,0:T(2,128)}), f32[16,2,1152]{2,1,0:T(2,128)S(1)}, u32[]{:S(2)}, u32[]{:S(2)}) async-start(f32[16,2,1152]{2,1,0:T(2,128)} %pack.1), calls=%async_computation | async-start | bytes 294912 | tf_op jit(solution)/shard_map/all_to_all | solution.py:627
  8.0 6.9 %ready.1 = (f32[144,512]{1,0:T(8,128)}, bf16[1296,1296]{1,0:T(8,128)(2,1)}) custom-call(f32[1296,8]{1,0:T(8,128)} %constant.4.clone.table_ref, bf16[1296,1296]{1,0:T(8,128)(2,1)} %coup_hbm.1, f32[1296,512]{1,0:T(8,128)} %bitcast.12), custom_call_target="tpu_custom_call" | custom-call | bytes 7962624 | tf_op jit(solution)/shard_map/ready/pallas_call | solution.py:636
  14.9 0.0 all-to-all-done.parcel_ref
  14.9 0.0 copy-start.4
  14.9 0.6 copy-done.4
  15.6 8.6 %first_half.1 = (f32[8,512]{1,0:T(8,128)}, f32[5264,128]{1,0:T(8,128)}) custom-call(s32[1,16]{1,0:T(1,128)} %count_ref.1, s32[1,512]{1,0:T(1,128)} %bitcast.15, f32[16,2,1152]{2,1,0:T(2,128)} %copy-done.4, s32[1,16,64]{2,1,0:T(8,128)} %send_ref.1, f32[1296,8]{1,0:T(8,128)} %constant.4.clone.table_ref, f32[144,512]{1,0:T(8,128)} %get-tuple-element.9.unit_ref, ...), custom_call_target="tpu_custom_call" | custom-call | flops 1719926784 | bytes 7962624 | tf_op jit(solution)/shard_map/first_half/pallas_call | solution.py:647
  24.2 0.0 copy-start.2
  24.2 66.4 %all_to_all.15 = f32[16,329,1,128]{3,2,1,0:T(1,128)S(1)} all-to-all(f32[16,329,1,128]{3,2,1,0:T(1,128)} %bitcast.14), channel_id=1, replica_groups=mesh['members'=2,'space'=16] {'space'}, dimensions={0} | all-to-all | bytes 5390336 | tf_op jit(solution)/shard_map/all_to_all | solution.py:663
  90.6 0.0 copy-done.2
  90.6 23.8 %sweeps.1 = f32[5184,128]{1,0:T(8,128)S(1)} custom-call(s32[8192]{0:T(1024)S(1)} %bitcast.11, f32[16,8,128]{2,1,0:T(8,128)S(1)} %copy-done.2, f32[5264,128]{1,0:T(8,128)S(1)} %bitcast.8), custom_call_target="tpu_custom_call" | custom-call | flops 51118080 | bytes 5308416 | tf_op jit(solution)/shard_map/sweeps/pallas_call | solution.py:667
  114.5 0.0 copy-start
  114.5 0.0 copy-start.1
  114.5 0.0 copy-start.3
  114.5 64.9 %all_to_all.16 = f32[16,81,4,128]{3,2,1,0:T(4,128)S(1)} all-to-all(f32[16,81,4,128]{3,2,1,0:T(4,128)S(1)} %bitcast.10), channel_id=1, replica_groups=mesh['members'=2,'space'=16] {'space'}, dimensions={0} | all-to-all | bytes 5308416 | tf_op jit(solution)/shard_map/all_to_all | solution.py:681
  179.4 0.0 copy-done
  179.4 0.0 copy-done.1
  179.4 0.0 copy-done.3
  179.4 4.9 %last_half.1 = f32[1296,512]{1,0:T(8,128)} custom-call(f32[8,512]{1,0:T(8,128)S(1)} %copy-done.3, f32[1296,8]{1,0:T(8,128)S(1)} %copy-done.1, f32[5184,128]{1,0:T(8,128)S(1)} %bitcast.9, bf16[1296,1296]{1,0:T(8,128)(2,1)S(1)} %copy-done), custom_call_target="tpu_custom_call" | custom-call | flops 1719926784 | bytes 7962624 | tf_op jit(solution)/shard_map/last_half/pallas_call | solution.py:684
  (1 shorter events, 0.0 us)
Async XLA Ops:
  1.5 13.4 %all-to-all-start = ((f32[16,2,1152]{2,1,0:T(2,128)}), f32[16,2,1152]{2,1,0:T(2,128)S(1)}, u32[]{:S(2)}, u32[]{:S(2)}) async-start(f32[16,2,1152]{2,1,0:T(2,128)} %pack.1), calls=%async_computation | async-start | bytes 294912 | tf_op jit(solution)/shard_map/all_to_all | solution.py:627
  14.9 0.7 copy-start.4
  24.2 66.4 %copy-start.2 = (f32[16,8,128]{2,1,0:T(8,128)S(1)}, f32[16,8,128]{2,1,0:T(8,128)}, u32[]{:S(2)}) copy-start(f32[16,8,128]{2,1,0:T(8,128)} %constant.5.clone.speed_ref) | copy-start | bytes 196612
  114.5 64.9 %copy-start = (bf16[1296,1296]{1,0:T(8,128)(2,1)S(1)}, bf16[1296,1296]{1,0:T(8,128)(2,1)}, u32[]{:S(2)}) copy-start(bf16[1296,1296]{1,0:T(8,128)(2,1)} %get-tuple-element.10.coup_hbm.coup_ref) | copy-start | bytes 10077700
  114.5 64.9 %copy-start.1 = (f32[1296,8]{1,0:T(8,128)S(1)}, f32[1296,8]{1,0:T(8,128)}, u32[]{:S(2)}) copy-start(f32[1296,8]{1,0:T(8,128)} %constant.4.clone.table_ref) | copy-start | bytes 124420
  114.5 64.9 %copy-start.3 = (f32[8,512]{1,0:T(8,128)S(1)}, f32[8,512]{1,0:T(8,128)}, u32[]{:S(2)}) copy-start(f32[8,512]{1,0:T(8,128)} %get-tuple-element.11.winds_ref) | copy-start | bytes 49156

commit v14 on v13

--- a/solution.py
+++ b/solution.py
@@ -456,7 +456,7 @@
         for j in range(tiles):
             cell_ref[j * LANES : (j + 1) * LANES, 0:tall] = turned[j]
 
-        @pl.loop(0, tiles)
+        @pl.loop(0, tiles, unroll=2)
         def _(j):
             first = s * plan.rows + j * LANES
             for g in range(LANES // SUBS):
@@ -473,7 +473,7 @@
 
     @pl.loop(0, plan.shares)
     def _(s):
-        @pl.loop(0, tiles)
+        @pl.loop(0, tiles, unroll=2)
         def _(j):
             first = s * plan.rows + j * LANES
             for g in range(LANES // SUBS):

time: 188 us -> 187 us (level)
  no operation moved by 1% of the time
where the time goes in v14:
time: 187 us; the launch traced here: 184 us
  blocking collectives  131 us (70%)
  Pallas kernels  45.4 us (24%)
  starting transfers between devices  6.55 us (4%)
    all_to_all x1, blocking collectives, on_spectrum(): lax.all_to_all(sent.reshape(shares, plan.block, 1, LANES), 'space', 0, 0,...  66.4 us
    all_to_all x1, blocking collectives, on_spectrum(): lax.all_to_all(swept.reshape(shares, depth, tiles, LANES), 'space', 0, 0,...  64.9 us
    pallas_call x1, Pallas kernels, on_spectrum(): kernel(functools.partial(middle_kernel, plan), flops=24 * size * LANES, t...  23.5 us
    pallas_call x1, Pallas kernels, on_spectrum(): kernel(functools.partial(first_kernel, plan), **h_cost, out_shape=[jax.Sh...  8.64 us
    pallas_call x1, Pallas kernels, on_spectrum(): kernel(functools.partial(ready_kernel, plan), flops=0, traffic=12 * rows...  6.88 us
    all_to_all x1, starting transfers between devices, on_spectrum(): parcel = lax.all_to_all(parcel, 'space', 0, 0, tiled=True)  6.55 us
    pallas_call x1, Pallas kernels, on_spectrum(): kernel(functools.partial(last_kernel, plan), vmem=24 * MIB, **h_cost, out...  4.92 us
  transfers between devices with their start and end apart: 1, of which 0 were waited for; matrix products, arithmetic and copies ran while one was open for 0% of the time, Pallas kernels for 4%

profile of v14, /device:TPU:15, one launch (start us, length us, event | category | flops | bytes accessed | tf_op | source)
XLA Modules:
  0.0 184.0 jit_solution(15127346320562339182)
XLA Ops:
  0.0 1.5 pack.1
  1.5 6.6 %all-to-all-start = ((f32[16,2,1152]{2,1,0:T(2,128)}), f32[16,2,1152]{2,1,0:T(2,128)S(1)}, u32[]{:S(2)}, u32[]{:S(2)}) async-start(f32[16,2,1152]{2,1,0:T(2,128)} %pack.1), calls=%async_computation | async-start | bytes 294912 | tf_op jit(solution)/shard_map/all_to_all | solution.py:627
  8.0 6.9 %ready.1 = (f32[144,512]{1,0:T(8,128)}, bf16[1296,1296]{1,0:T(8,128)(2,1)}) custom-call(f32[1296,8]{1,0:T(8,128)} %constant.4.clone.table_ref, bf16[1296,1296]{1,0:T(8,128)(2,1)} %coup_hbm.1, f32[1296,512]{1,0:T(8,128)} %bitcast.12), custom_call_target="tpu_custom_call" | custom-call | bytes 7962624 | tf_op jit(solution)/shard_map/ready/pallas_call | solution.py:636
  14.9 0.0 all-to-all-done.parcel_ref
  14.9 0.0 copy-start.4
  14.9 0.6 copy-done.4
  15.6 8.6 %first_half.1 = (f32[8,512]{1,0:T(8,128)}, f32[5264,128]{1,0:T(8,128)}) custom-call(s32[1,16]{1,0:T(1,128)} %count_ref.1, s32[1,512]{1,0:T(1,128)} %bitcast.15, f32[16,2,1152]{2,1,0:T(2,128)} %copy-done.4, s32[1,16,64]{2,1,0:T(8,128)} %send_ref.1, f32[1296,8]{1,0:T(8,128)} %constant.4.clone.table_ref, f32[144,512]{1,0:T(8,128)} %get-tuple-element.9.unit_ref, ...), custom_call_target="tpu_custom_call" | custom-call | flops 1719926784 | bytes 7962624 | tf_op jit(solution)/shard_map/first_half/pallas_call | solution.py:647
  24.2 0.0 copy-start.2
  24.2 66.4 %all_to_all.15 = f32[16,329,1,128]{3,2,1,0:T(1,128)S(1)} all-to-all(f32[16,329,1,128]{3,2,1,0:T(1,128)} %bitcast.14), channel_id=1, replica_groups=mesh['members'=2,'space'=16] {'space'}, dimensions={0} | all-to-all | bytes 5390336 | tf_op jit(solution)/shard_map/all_to_all | solution.py:663
  90.6 0.0 copy-done.2
  90.6 23.5 %sweeps.1 = f32[5184,128]{1,0:T(8,128)S(1)} custom-call(s32[8192]{0:T(1024)S(1)} %bitcast.11, f32[16,8,128]{2,1,0:T(8,128)S(1)} %copy-done.2, f32[5264,128]{1,0:T(8,128)S(1)} %bitcast.8), custom_call_target="tpu_custom_call" | custom-call | flops 51118080 | bytes 5308416 | tf_op jit(solution)/shard_map/sweeps/pallas_call | solution.py:667
  114.2 0.0 copy-start
  114.2 0.0 copy-start.1
  114.2 0.0 copy-start.3
  114.2 64.9 %all_to_all.16 = f32[16,81,4,128]{3,2,1,0:T(4,128)S(1)} all-to-all(f32[16,81,4,128]{3,2,1,0:T(4,128)S(1)} %bitcast.10), channel_id=1, replica_groups=mesh['members'=2,'space'=16] {'space'}, dimensions={0} | all-to-all | bytes 5308416 | tf_op jit(solution)/shard_map/all_to_all | solution.py:681
  179.1 0.0 copy-done
  179.1 0.0 copy-done.1
  179.1 0.0 copy-done.3
  179.1 4.9 %last_half.1 = f32[1296,512]{1,0:T(8,128)} custom-call(f32[8,512]{1,0:T(8,128)S(1)} %copy-done.3, f32[1296,8]{1,0:T(8,128)S(1)} %copy-done.1, f32[5184,128]{1,0:T(8,128)S(1)} %bitcast.9, bf16[1296,1296]{1,0:T(8,128)(2,1)S(1)} %copy-done), custom_call_target="tpu_custom_call" | custom-call | flops 1719926784 | bytes 7962624 | tf_op jit(solution)/shard_map/last_half/pallas_call | solution.py:684
  (1 shorter events, 0.0 us)
Async XLA Ops:
  1.5 13.4 %all-to-all-start = ((f32[16,2,1152]{2,1,0:T(2,128)}), f32[16,2,1152]{2,1,0:T(2,128)S(1)}, u32[]{:S(2)}, u32[]{:S(2)}) async-start(f32[16,2,1152]{2,1,0:T(2,128)} %pack.1), calls=%async_computation | async-start | bytes 294912 | tf_op jit(solution)/shard_map/all_to_all | solution.py:627
  14.9 0.7 copy-start.4
  24.2 66.4 %copy-start.2 = (f32[16,8,128]{2,1,0:T(8,128)S(1)}, f32[16,8,128]{2,1,0:T(8,128)}, u32[]{:S(2)}) copy-start(f32[16,8,128]{2,1,0:T(8,128)} %constant.5.clone.speed_ref) | copy-start | bytes 196612
  114.2 64.9 %copy-start = (bf16[1296,1296]{1,0:T(8,128)(2,1)S(1)}, bf16[1296,1296]{1,0:T(8,128)(2,1)}, u32[]{:S(2)}) copy-start(bf16[1296,1296]{1,0:T(8,128)(2,1)} %get-tuple-element.10.coup_hbm.coup_ref) | copy-start | bytes 10077700
  114.2 64.9 %copy-start.1 = (f32[1296,8]{1,0:T(8,128)S(1)}, f32[1296,8]{1,0:T(8,128)}, u32[]{:S(2)}) copy-start(f32[1296,8]{1,0:T(8,128)} %constant.4.clone.table_ref) | copy-start | bytes 124420
  114.2 64.9 %copy-start.3 = (f32[8,512]{1,0:T(8,128)S(1)}, f32[8,512]{1,0:T(8,128)}, u32[]{:S(2)}) copy-start(f32[8,512]{1,0:T(8,128)} %get-tuple-element.11.winds_ref) | copy-start | bytes 49156
